TPU v7x, 512 devices: a whole 4x8x8 slice. The times are simulated.
512 devices in a mesh: rep: 4 (over x_hi, core), exp: 128 (over z, x_lo, y).
Axes of the slice: x: 4 (x_hi: 2, x_lo: 2; x = x_hi * 2 + x_lo), y: 8, z: 8, core: 2. Of those that a mesh axis runs over, the one named last changes fastest.
Arguments:
- tokens: bfloat16 [16384, 1440], P('exp', 'rep'), may hold values from -6 to 6
- expert_ids: int32 [16384, 4], P('exp'), may hold values from 0 to 63, all different within a row; in each aligned block of 64 rows (0 to 63, 64 to 127, ...) at most 5 rows name the same one
- gate_values: float32 [16384, 4], P('exp'), may hold values from 0.05 to 0.45
- out_grad: bfloat16 [16384, 1440], P('exp', 'rep'), may hold values from -6 to 6
- gate_weight: bfloat16 [128, 720, 1440], P('exp', 'rep'), may hold values from -0.15625 to 0.15625
- up_weight: bfloat16 [128, 720, 1440], P('exp', 'rep'), may hold values from -0.15625 to 0.15625
- down_weight: bfloat16 [128, 720, 1440], P('exp', 'rep'), may hold values from -0.15625 to 0.15625
Outputs:
- layer_out: bfloat16 [16384, 1440], P('exp', 'rep')
- input_grad: bfloat16 [16384, 1440], P('exp', 'rep')
- gate_grad: bfloat16 [128, 720, 1440], P('exp', 'rep')
- up_grad: bfloat16 [128, 720, 1440], P('exp', 'rep')
- down_grad: bfloat16 [128, 720, 1440], P('exp', 'rep')
Inputs may be any that keep to these rules, and one draw needn't show every extreme that they name: `expert_ids`: each row names 4 different experts. In each aligned block of half of 128 rows no expert is named by more than 5 rows, a bound that some block reaches.
All inputs are finite; a program needn't handle non-finite values.
Results may differ from a plain program's by a relative error of at most 0.015.
Values may be sent and summed in bfloat16 or wider, within the bound.
No kernel may reach another device: no remote copies, remote signals or barrier semaphores. Data moves between devices by JAX's collectives and lax.ppermute only.
A program may use at most 64 MiB of HBM per device.

v0:
```python
import jax
import jax.numpy as jnp
from jax import lax
from jax.sharding import PartitionSpec as P

swish_alpha = 1.702


def swapped(block, axis, distance):
    count = lax.axis_size(axis)
    route = []
    for low in range(count):
        high = low | 1 << distance
        if high != low and high < count:
            route += [(low, high), (high, low)]
    return lax.ppermute(block, axis, route)


def matmul(left, right):
    return jnp.dot(left, right, preferred_element_type=jnp.float32)


def contract(left, right, left_dim, right_dim):
    return lax.dot_general(
        left, right, (((left_dim,), (right_dim,)), ((), ())), preferred_element_type=jnp.float32
    )


def arrange(leading, own, partner, axis):
    return jnp.where(
        leading, jnp.concatenate([own, partner], axis), jnp.concatenate([partner, own], axis)
    )


def own_peer(leading, whole, axis):
    width = whole.shape[axis] // 2
    lower = lax.slice_in_dim(whole, 0, width, axis=axis)
    upper = lax.slice_in_dim(whole, width, 2 * width, axis=axis)
    return (jnp.where(leading, lower, upper), jnp.where(leading, upper, lower))


def local(tokens, expert_ids, gate_values, out_grad, gate_weight, up_weight, down_weight):
    exp_count = lax.axis_size("exp")
    leading = lax.axis_index("exp") % 2 == 0
    tok_rows, top_count = expert_ids.shape
    half_rows = tok_rows // 2
    experts = exp_count // 2
    capacity = min(half_rows, max(2, tok_rows * top_count // exp_count + 1))
    slot_count = exp_count * capacity
    assigns = tok_rows * top_count
    flat_ids = expert_ids.reshape(-1)
    onehot = (flat_ids[:, None] == jnp.arange(experts, dtype=jnp.int32)[None, :]).astype(jnp.int32)
    counted = jnp.cumsum(onehot.reshape(2, half_rows * top_count, experts), axis=1).reshape(
        assigns, experts
    )
    position = jnp.sum((counted - 1) * onehot, axis=1)
    block_ids = jnp.arange(assigns, dtype=jnp.int32) // (half_rows * top_count)
    target = (2 * flat_ids + block_ids) * capacity + position
    placer = (jnp.arange(slot_count, dtype=jnp.int32)[:, None] == target[None, :]).astype(
        jnp.bfloat16
    )
    token_placer = jnp.sum(placer.reshape(slot_count, tok_rows, top_count), axis=2)
    partner = swapped((gate_weight, up_weight, down_weight), "exp", 0)
    gate_rows = arrange(leading, gate_weight[0], partner[0][0], 0)
    up_rows = arrange(leading, up_weight[0], partner[1][0], 0)
    down_rows = arrange(leading, down_weight[0], partner[2][0], 0)
    full_tokens = lax.all_gather(tokens, "rep", axis=1, tiled=True)
    packed = matmul(token_placer, full_tokens).astype(jnp.bfloat16).reshape(exp_count, capacity, -1)
    received = lax.all_to_all(packed, "exp", split_axis=0, concat_axis=0, tiled=True)
    token_rows = received.reshape(slot_count, -1)
    pre_gate = contract(token_rows, gate_rows, 1, 1)
    pre_up = contract(token_rows, up_rows, 1, 1)
    sig_gate = jax.nn.sigmoid(swish_alpha * pre_gate)
    swish = pre_gate * sig_gate
    hidden = ((pre_up + 1.0) * swish).astype(jnp.bfloat16)
    partial_term = matmul(hidden, down_rows).astype(jnp.bfloat16)
    expert_out = (
        lax.psum_scatter(partial_term, "rep", scatter_dimension=1, tiled=True)
        .astype(jnp.float32)
        .astype(jnp.bfloat16)
    )
    returned = lax.all_to_all(
        expert_out.reshape(exp_count, capacity, -1), "exp", split_axis=0, concat_axis=0, tiled=True
    )
    per_assign = contract(placer, returned.reshape(slot_count, -1), 0, 0).reshape(
        tok_rows, top_count, -1
    )
    layer_out = jnp.sum(gate_values[:, :, None] * per_assign, axis=1).astype(jnp.bfloat16)
    full_grad = lax.all_gather(out_grad, "rep", axis=1, tiled=True)
    scaled = (gate_values[:, :, None] * full_grad[:, None, :].astype(jnp.float32)).astype(
        jnp.bfloat16
    )
    packed_grad = (
        matmul(placer, scaled.reshape(assigns, -1))
        .astype(jnp.bfloat16)
        .reshape(exp_count, capacity, -1)
    )
    grad_arrived = lax.all_to_all(packed_grad, "exp", split_axis=0, concat_axis=0, tiled=True)
    row_grads = grad_arrived.reshape(slot_count, -1)
    grad_hidden = contract(row_grads, down_rows, 1, 1)
    down_part = contract(hidden, row_grads, 0, 0)
    own_down, peer_down = own_peer(leading, down_part, 0)
    grad_up = (grad_hidden * swish).astype(jnp.bfloat16)
    slope = sig_gate + swish_alpha * pre_gate * sig_gate * (1.0 - sig_gate)
    grad_gate = (grad_hidden * (pre_up + 1.0) * slope).astype(jnp.bfloat16)
    input_partial = (matmul(grad_gate, gate_rows) + matmul(grad_up, up_rows)).astype(jnp.bfloat16)
    input_rows = (
        lax.psum_scatter(input_partial, "rep", scatter_dimension=1, tiled=True)
        .astype(jnp.float32)
        .astype(jnp.bfloat16)
    )
    input_back = lax.all_to_all(
        input_rows.reshape(exp_count, capacity, -1), "exp", split_axis=0, concat_axis=0, tiled=True
    )
    input_assign = contract(placer, input_back.reshape(slot_count, -1), 0, 0).reshape(
        tok_rows, top_count, -1
    )
    input_grad = jnp.sum(input_assign, axis=1).astype(jnp.bfloat16)
    gate_part = contract(grad_gate, token_rows, 0, 0)
    up_part = contract(grad_up, token_rows, 0, 0)
    own_gate, peer_gate = own_peer(leading, gate_part, 0)
    own_up, peer_up = own_peer(leading, up_part, 0)
    got_gate, got_up, got_down = swapped((peer_gate, peer_up, peer_down), "exp", 0)
    down_total = own_down + got_down
    gate_grad = (own_gate + got_gate).astype(jnp.bfloat16)[None]
    up_grad = (own_up + got_up).astype(jnp.bfloat16)[None]
    down_grad = down_total.astype(jnp.bfloat16)[None]
    return (layer_out, input_grad, gate_grad, up_grad, down_grad)


def solution(mesh):
    in_specs = (
        P("exp", "rep"),
        P("exp", None),
        P("exp", None),
        P("exp", "rep"),
        P("exp", "rep", None),
        P("exp", "rep", None),
        P("exp", "rep", None),
    )
    out_specs = (
        P("exp", "rep"),
        P("exp", "rep"),
        P("exp", "rep", None),
        P("exp", "rep", None),
        P("exp", "rep", None),
    )
    return jax.shard_map(local, mesh=mesh, in_specs=in_specs, out_specs=out_specs, check_vma=False)
```

profile of v0, /device:TPU:1, one launch (start us, length us, event | category | flops | bytes accessed | tf_op | source)
XLA Modules:
  0.0 390.3 jit_solution(5381352074659027077)
XLA Ops:
  7.2 0.8 copy.58
  8.2 1.2 reduce-window.6
  9.4 0.2 slice_reduce_fusion
  9.7 0.1 fusion.18
  10.0 0.7 fusion.25
  10.7 0.1 fusion.7
  10.8 14.5 %all_gather.6 = bf16[128,1440]{0,1:T(8,128)(2,1)S(1)} all-gather(bf16[128,360]{0,1:T(8,128)(2,1)} %param.7), channel_id=1, replica_groups=mesh['rep'=4,'exp'=128] {'rep'}, dimensions={1}, use_global_device_ids=true | all-gather | bytes 460800 | tf_op jit(solution)/shard_map/all_gather | solution.py:67
  25.4 1.9 convolution_convert_fusion.1
  27.3 2.6 copy.62
  29.9 2.5 reshape.156
  32.4 13.1 %all-to-all-start = ((bf16[128,5,1440]{2,1,0:T(8,128)(2,1)}), bf16[128,5,1440]{2,1,0:T(8,128)(2,1)S(1)}, u32[]{:S(2)}, u32[]{:S(2)}) async-start(bf16[128,5,1440]{2,1,0:T(8,128)(2,1)} %reshape.156), calls=%async_computation | async-start | bytes 6291456 | tf_op jit(solution)/shard_map/all_to_all | solution.py:69
  45.5 0.1 copy.57
  45.8 10.5 %all_gather.7 = bf16[128,1440]{0,1:T(8,128)(2,1)S(1)} all-gather(bf16[128,360]{0,1:T(8,128)(2,1)} %param.10), channel_id=1, replica_groups=mesh['rep'=4,'exp'=128] {'rep'}, dimensions={1}, use_global_device_ids=true | all-gather | bytes 460800 | tf_op jit(solution)/shard_map/all_gather | solution.py:89
  56.3 1.1 copy.67
  57.4 3.4 mul.98
  60.7 5.0 %mul.99 = f32[512,1440]{1,0:T(8,128)} reshape(f32[128,4,1440]{2,1,0:T(4,128)} %mul.98) | data formatting | bytes 5898240 | tf_op jit(solution)/shard_map/mul | solution.py:90
  65.9 4.6 %convolution_convert_fusion.2 = bf16[640,1440]{0,1:T(8,128)(2,1)} fusion(f32[512,1440]{1,0:T(8,128)} %mul.99, f32[512]{0:T(512)S(1)} %mul.96, s32[512]{0:T(512)S(1)} %fusion.22), kind=kOutput, calls=%fused_computation.4 | convolution fusion | flops 946442240 | bytes 4796416 | tf_op jit(solution)/shard_map/dot_general | solution.py:20
  70.5 3.9 %copy.68 = bf16[640,1440]{1,0:T(8,128)(2,1)} copy(bf16[640,1440]{0,1:T(8,128)(2,1)} %convolution_convert_fusion.2) | data formatting | bytes 3686400 | tf_op jit(solution)/shard_map/convert_element_type | solution.py:95
  74.5 4.4 %reshape.160 = bf16[128,5,1440]{2,1,0:T(8,128)(2,1)} reshape(bf16[640,1440]{1,0:T(8,128)(2,1)} %copy.68) | data formatting | bytes 3686400 | tf_op jit(solution)/shard_map/reshape | solution.py:96
  78.8 40.5 %all-to-all-done = bf16[128,5,1440]{2,1,0:T(8,128)(2,1)S(1)} async-done(((bf16[128,5,1440]{2,1,0:T(8,128)(2,1)}), bf16[128,5,1440]{2,1,0:T(8,128)(2,1)S(1)}, u32[]{:S(2)}, u32[]{:S(2)}) %all-to-all-start) | async-done | bytes 1843232 | tf_op jit(solution)/shard_map/all_to_all | solution.py:69
  119.3 9.2 %all-to-all-start.2 = ((bf16[128,5,1440]{2,1,0:T(8,128)(2,1)}), bf16[128,5,1440]{2,1,0:T(8,128)(2,1)}, u32[]{:S(2)}, u32[]{:S(2)}) async-start(bf16[128,5,1440]{2,1,0:T(8,128)(2,1)} %reshape.160), calls=%async_computation.2 | async-start | bytes 6291456 | tf_op jit(solution)/shard_map/all_to_all | solution.py:98
  128.5 2.4 collective-permute-start.1
  131.0 2.9 collective-permute-start
  133.8 2.6 collective-permute-start.2
  136.5 2.7 reshape.157
  139.1 68.5 %collective-permute-done.1 = bf16[1,180,1440]{2,1,0:T(8,128)(2,1)} collective-permute-done((bf16[1,180,1440]{2,1,0:T(8,128)(2,1)}, bf16[1,180,1440]{2,1,0:T(8,128)(2,1)}, u32[]{:S(2)}, u32[]{:S(2)}) %collective-permute-start.1) | collective-permute-done | bytes 518432 | tf_op jit(solution)/shard_map/ppermute | solution.py:16
  207.6 4.3 %fusion.15 = f32[640,360]{0,1:T(8,128)} fusion(bf16[640,1440]{1,0:T(8,128)(2,1)} %reshape.157, bf16[180,1440]{1,0:T(8,128)(2,1)} %bitcast.4, bf16[180,1440]{1,0:T(8,128)(2,1)} %bitcast.50, pred[]{:T(512)S(6)} %eq.85), kind=kOutput, calls=%fused_computation.39 | convolution fusion | flops 668217600 | bytes 3801601 | tf_op jit(solution)/shard_map/dot_general | solution.py:24
  211.9 4.7 %reshape.161 = bf16[640,1440]{1,0:T(8,128)(2,1)} reshape(bf16[128,5,1440]{2,1,0:T(8,128)(2,1)} %all-to-all-done.2) | data formatting | bytes 3686400 | tf_op jit(solution)/shard_map/reshape | solution.py:99
  216.7 3.0 collective-permute-done
  219.7 2.5 convolution_add_fusion.1
  222.2 9.6 %collective-permute-done.2 = bf16[1,180,1440]{2,1,0:T(8,128)(2,1)} collective-permute-done((bf16[1,180,1440]{2,1,0:T(8,128)(2,1)}, bf16[1,180,1440]{2,1,0:T(8,128)(2,1)}, u32[]{:S(2)}, u32[]{:S(2)}) %collective-permute-start.2) | collective-permute-done | bytes 518432 | tf_op jit(solution)/shard_map/ppermute | solution.py:16
  231.8 3.6 multiply_convert_fusion.3
  235.4 2.7 fusion.16
  238.2 3.9 %fusion = bf16[640,1440]{0,1:T(8,128)(2,1)} fusion(f32[640,1440]{0,1:T(8,128)S(1)} %fusion.16, bf16[640,360]{0,1:T(8,128)(2,1)S(1)} %get-tuple-element.5, bf16[180,1440]{1,0:T(8,128)(2,1)} %bitcast.4, bf16[180,1440]{1,0:T(8,128)(2,1)S(1)} %bitcast.51, pred[]{:T(512)S(6)} %eq.85), kind=kOutput, calls=%fused_computation.1 | convolution fusion | flops 670060800 | bytes 7027201 | tf_op jit(solution)/shard_map/dot_general | solution.py:20
  242.2 4.3 %convolution_convert_fusion = bf16[640,1440]{0,1:T(8,128)(2,1)} fusion(bf16[640,360]{0,1:T(8,128)(2,1)} %get-tuple-element.6, bf16[180,1440]{1,0:T(8,128)(2,1)} %bitcast.6, bf16[180,1440]{1,0:T(8,128)(2,1)} %bitcast.56, pred[]{:T(512)S(6)} %eq.85), kind=kOutput, calls=%fused_computation.2 | convolution fusion | flops 669139200 | bytes 3340801 | tf_op jit(solution)/shard_map/dot_general | solution.py:20
  246.5 0.2 iota_compare_fusion.2
  246.8 0.9 eq.81
  247.7 2.7 fusion.38
  250.4 1.2 slice_select_fusion
  251.6 0.6 copy-done.1
  252.3 2.8 collective-permute-start.5
  255.1 1.0 fusion.37
  256.1 1.2 slice_select_fusion.1
  257.3 0.6 copy-done
  257.9 2.6 collective-permute-start.4
  260.5 1.0 fusion.36
  261.5 29.1 %reduce-scatter.9.cloned.1.call-done = bf16[640,360]{0,1:T(8,128)(2,1)} async-done(((bf16[640,1440]{0,1:T(8,128)(2,1)}), bf16[640,360]{0,1:T(8,128)(2,1)}) %reduce-scatter.9.cloned.1.call-update) | async-done | bytes 460816
  290.6 1.3 copy.69
  291.9 1.1 reshape.162
  293.0 14.5 %all-to-all-start.3 = ((bf16[128,5,360]{2,1,0:T(8,128)(2,1)}), bf16[128,5,360]{2,1,0:T(8,128)(2,1)S(1)}, u32[]{:S(2)}, u32[]{:S(2)}) async-start(bf16[128,5,360]{2,1,0:T(8,128)(2,1)} %reshape.162), calls=%async_computation.3 | async-start | bytes 1572864 | tf_op jit(solution)/shard_map/all_to_all | solution.py:112
  307.5 1.2 slice_select_fusion.2
  308.7 2.5 collective-permute-start.3
  311.2 2.5 fusion.11
  313.7 27.8 %reduce-scatter.7.cloned.1.call-done = bf16[640,360]{0,1:T(8,128)(2,1)} async-done(((bf16[640,1440]{0,1:T(8,128)(2,1)}), bf16[640,360]{0,1:T(8,128)(2,1)}) %reduce-scatter.7.cloned.1.call-update) | async-done | bytes 460816
  341.5 1.3 copy.63
  342.8 1.1 reshape.158
  343.9 14.1 %all-to-all-start.1 = ((bf16[128,5,360]{2,1,0:T(8,128)(2,1)}), bf16[128,5,360]{2,1,0:T(8,128)(2,1)}, u32[]{:S(2)}, u32[]{:S(2)}) async-start(bf16[128,5,360]{2,1,0:T(8,128)(2,1)} %reshape.158), calls=%async_computation.1 | async-start | bytes 1572864 | tf_op jit(solution)/shard_map/all_to_all | solution.py:82
  358.0 3.1 fusion.10
  361.1 2.4 fusion.9
  363.5 0.3 reshape.163
  363.8 1.1 convolution_reduce_fusion
  365.0 15.8 %all-to-all-done.1 = bf16[128,5,360]{2,1,0:T(8,128)(2,1)} async-done(((bf16[128,5,360]{2,1,0:T(8,128)(2,1)}), bf16[128,5,360]{2,1,0:T(8,128)(2,1)}, u32[]{:S(2)}, u32[]{:S(2)}) %all-to-all-start.1) | async-done | bytes 460832 | tf_op jit(solution)/shard_map/all_to_all | solution.py:82
  380.8 1.5 reshape.159
  382.3 1.1 fusion.3
  (49 shorter events, 1.0 us)
Async XLA Ops:
  32.4 86.9 %all-to-all-start = ((bf16[128,5,1440]{2,1,0:T(8,128)(2,1)}), bf16[128,5,1440]{2,1,0:T(8,128)(2,1)S(1)}, u32[]{:S(2)}, u32[]{:S(2)}) async-start(bf16[128,5,1440]{2,1,0:T(8,128)(2,1)} %reshape.156), calls=%async_computation | async-start | bytes 6291456 | tf_op jit(solution)/shard_map/all_to_all | solution.py:69
  60.7 5.0 %copy-start.8 = (f32[128,4]{0,1:T(4,128)S(1)}, f32[128,4]{0,1:T(4,128)}, u32[]{:S(2)}) copy-start(f32[128,4]{0,1:T(4,128)} %param.9) | copy-start | bytes 6148
  119.3 92.6 %all-to-all-start.2 = ((bf16[128,5,1440]{2,1,0:T(8,128)(2,1)}), bf16[128,5,1440]{2,1,0:T(8,128)(2,1)}, u32[]{:S(2)}, u32[]{:S(2)}) async-start(bf16[128,5,1440]{2,1,0:T(8,128)(2,1)} %reshape.160), calls=%async_computation.2 | async-start | bytes 6291456 | tf_op jit(solution)/shard_map/all_to_all | solution.py:98
  128.5 162.1 %reduce-scatter.9.cloned.1.call-start = ((), (), s32[]{:S(2)}) async-start(), calls=%async_computation.7 | async-start | bytes 2304000
  128.5 79.0 %collective-permute-start.1 = (bf16[1,180,1440]{2,1,0:T(8,128)(2,1)}, bf16[1,180,1440]{2,1,0:T(8,128)(2,1)}, u32[]{:S(2)}, u32[]{:S(2)}) collective-permute-start(bf16[1,180,1440]{2,1,0:T(8,128)(2,1)} %param.11), channel_id=1, source_target_pairs={{0,1},{1,0},{2,3},{3,2},{4,5},{5,4},{6,7},{7,6},{8,9},{9,8},{10,11... | collective-permute-start | bytes 1555208 | tf_op jit(solution)/shard_map/ppermute | solution.py:16
  131.0 88.7 %collective-permute-start = (bf16[1,180,1440]{2,1,0:T(8,128)(2,1)}, bf16[1,180,1440]{2,1,0:T(8,128)(2,1)}, u32[]{:S(2)}, u32[]{:S(2)}) collective-permute-start(bf16[1,180,1440]{2,1,0:T(8,128)(2,1)} %param.12), channel_id=1, source_target_pairs={{0,1},{1,0},{2,3},{3,2},{4,5},{5,4},{6,7},{7,6},{8,9},{9,8},{10,11... | collective-permute-start | bytes 1555208 | tf_op jit(solution)/shard_map/ppermute | solution.py:16
  133.8 98.0 %collective-permute-start.2 = (bf16[1,180,1440]{2,1,0:T(8,128)(2,1)}, bf16[1,180,1440]{2,1,0:T(8,128)(2,1)}, u32[]{:S(2)}, u32[]{:S(2)}) collective-permute-start(bf16[1,180,1440]{2,1,0:T(8,128)(2,1)} %param.13), channel_id=1, source_target_pairs={{0,1},{1,0},{2,3},{3,2},{4,5},{5,4},{6,7},{7,6},{8,9},{9,8},{10,11... | collective-permute-start | bytes 1555208 | tf_op jit(solution)/shard_map/ppermute | solution.py:16
  211.9 7.8 %copy-start.3 = (bf16[640,1440]{1,0:T(8,128)(2,1)S(1)}, bf16[640,1440]{1,0:T(8,128)(2,1)}, u32[]{:S(2)}) copy-start(bf16[640,1440]{1,0:T(8,128)(2,1)} %reshape.157) | copy-start | bytes 5529604
  211.9 7.8 %copy-start.9 = (bf16[1,180,1440]{2,1,0:T(8,128)(2,1)S(1)}, bf16[1,180,1440]{2,1,0:T(8,128)(2,1)}, u32[]{:S(2)}) copy-start(bf16[1,180,1440]{2,1,0:T(8,128)(2,1)} %param.12) | copy-start | bytes 1555204
  219.7 12.1 %copy-start.5 = (bf16[640,1440]{1,0:T(8,128)(2,1)S(1)}, bf16[640,1440]{1,0:T(8,128)(2,1)}, u32[]{:S(2)}) copy-start(bf16[640,1440]{1,0:T(8,128)(2,1)} %reshape.161) | copy-start | bytes 5529604
  219.7 12.1 %copy-start.11 = (bf16[1,180,1440]{2,1,0:T(8,128)(2,1)S(1)}, bf16[1,180,1440]{2,1,0:T(8,128)(2,1)}, u32[]{:S(2)}) copy-start(bf16[1,180,1440]{2,1,0:T(8,128)(2,1)} %param.13) | copy-start | bytes 1555204
  219.7 12.1 %copy-start.14 = (f32[640,360]{0,1:T(8,128)S(1)}, f32[640,360]{0,1:T(8,128)}, u32[]{:S(2)}) copy-start(f32[640,360]{0,1:T(8,128)} %fusion.15) | copy-start | bytes 2764804
  231.8 3.6 copy-start.10
  235.4 2.8 copy-start.12
  235.4 2.8 copy-start.6
  242.2 99.3 %reduce-scatter.7.cloned.1.call-start = ((), (), s32[]{:S(2)}) async-start(), calls=%async_computation.6 | async-start | bytes 2304000
  250.4 1.8 copy-start.1
  250.4 4.6 %copy-start.13 = (bf16[640,360]{0,1:T(8,128)(2,1)S(1)}, bf16[640,360]{0,1:T(8,128)(2,1)}, u32[]{:S(2)}) copy-start(bf16[640,360]{0,1:T(8,128)(2,1)} %copy-done.12) | copy-start | bytes 1382404
  252.3 58.9 %collective-permute-start.5 = (f32[180,1440]{1,0:T(8,128)}, f32[180,1440]{1,0:T(8,128)}, u32[]{:S(2)}, u32[]{:S(2)}) collective-permute-start(f32[180,1440]{1,0:T(8,128)} %slice_select_fusion), channel_id=1, source_target_pairs={{0,1},{1,0},{2,3},{3,2},{4,5},{5,4},{6,7},{7,6},{8,9},{9,8},{10,11... | collective-permute-start | bytes 3110408 | tf_op jit(solution)/shard_map/ppermute | solution.py:16
  256.1 1.8 copy-start
  256.1 4.4 %copy-start.4 = (bf16[640,1440]{1,0:T(8,128)(2,1)S(1)}, bf16[640,1440]{1,0:T(8,128)(2,1)}, u32[]{:S(2)}) copy-start(bf16[640,1440]{1,0:T(8,128)(2,1)} %reshape.157) | copy-start | bytes 5529604
  257.9 100.1 %collective-permute-start.4 = (f32[180,1440]{1,0:T(8,128)}, f32[180,1440]{1,0:T(8,128)}, u32[]{:S(2)}, u32[]{:S(2)}) collective-permute-start(f32[180,1440]{1,0:T(8,128)} %slice_select_fusion.1), channel_id=1, source_target_pairs={{0,1},{1,0},{2,3},{3,2},{4,5},{5,4},{6,7},{7,6},{8,9},{9,8},{10,11... | collective-permute-start | bytes 3110408 | tf_op jit(solution)/shard_map/ppermute | solution.py:16
  293.0 50.9 %all-to-all-start.3 = ((bf16[128,5,360]{2,1,0:T(8,128)(2,1)}), bf16[128,5,360]{2,1,0:T(8,128)(2,1)S(1)}, u32[]{:S(2)}, u32[]{:S(2)}) async-start(bf16[128,5,360]{2,1,0:T(8,128)(2,1)} %reshape.162), calls=%async_computation.3 | async-start | bytes 1572864 | tf_op jit(solution)/shard_map/all_to_all | solution.py:112
  307.5 3.7 copy-start.2
  308.7 52.4 %collective-permute-start.3 = (f32[180,1440]{1,0:T(8,128)}, f32[180,1440]{1,0:T(8,128)}, u32[]{:S(2)}, u32[]{:S(2)}) collective-permute-start(f32[180,1440]{1,0:T(8,128)} %slice_select_fusion.2), channel_id=1, source_target_pairs={{0,1},{1,0},{2,3},{3,2},{4,5},{5,4},{6,7},{7,6},{8,9},{9,8},{10,11... | collective-permute-start | bytes 3110408 | tf_op jit(solution)/shard_map/ppermute | solution.py:16
  343.9 36.9 %all-to-all-start.1 = ((bf16[128,5,360]{2,1,0:T(8,128)(2,1)}), bf16[128,5,360]{2,1,0:T(8,128)(2,1)}, u32[]{:S(2)}, u32[]{:S(2)}) async-start(bf16[128,5,360]{2,1,0:T(8,128)(2,1)} %reshape.158), calls=%async_computation.1 | async-start | bytes 1572864 | tf_op jit(solution)/shard_map/all_to_all | solution.py:82
  361.1 2.8 copy-start.7
Sparse Core Ops, SparseCore 0:
  242.3 48.3 reduce-scatter.8
  293.7 47.7 reduce-scatter.6
where the time goes:
time: 393 us; the launch traced here: 390 us
  waiting for transfers between devices  194 us (49%)
  starting transfers between devices  66.6 us (17%)
  local copies, waits for them, and re-layouts  41 us (10%)
  matrix products  34.9 us (9%)
  blocking collectives  25 us (6%)
  between operations  14.4 us (4%)
  other arithmetic  14 us (4%)
    ppermute x6, waiting for transfers between devices, swapped(): return lax.ppermute(block, axis, route)  81.1 us
    unnamed x4, waiting for transfers between devices  57 us
    all_to_all x1, waiting for transfers between devices, local(): lax.all_to_all(packed, 'exp', split_axis=0, concat_axis=0, tiled=True)  40.5 us
    dot_general x5, matrix products, matmul(): return jnp.dot(left, right, preferred_element_type=jnp.float32)  17.4 us
    dot_general x8, matrix products, contract(): lax.dot_general(left, right, (((left_dim,), (right_dim,)), ((), ())), pre...  17.4 us
    all_to_all x1, waiting for transfers between devices, local(): lax.all_to_all(expert_out.reshape(exp_count, capacity, -1), 'exp', split_...  15.8 us
    ppermute x6, starting transfers between devices, swapped(): return lax.ppermute(block, axis, route)  15.8 us
    all_gather x1, blocking collectives, local(): full_tokens = lax.all_gather(tokens, 'rep', axis=1, tiled=True)  14.5 us
  transfers between devices with their start and end apart: 12, of which 7 were waited for; matrix products, arithmetic and copies ran while one was open for 17% of the time, Pallas kernels for 0%

commit v1 on v0

v1 whole, which is shorter than its diff:
```python
import jax
import jax.numpy as jnp
from jax import lax
from jax.experimental import pallas as pl
from jax.experimental.pallas import tpu as pltpu
from jax.sharding import PartitionSpec as P

swish_alpha = 1.702
low = jnp.bfloat16
full = jnp.float32


def exchanged(block, axis, distance):
    count = lax.axis_size(axis)
    return lax.ppermute(block, axis, [(i, i ^ distance) for i in range(count)])


def contract(left, right, left_dim, right_dim):
    return lax.dot_general(
        left, right, (((left_dim,), (right_dim,)), ((), ())), preferred_element_type=full
    )


def expert_kernel(
    rep_ref,
    row0, row1, row2, row3,
    gate_own, gate_peer, up_own, up_peer, down_own, down_peer,
    term0, term1, term2, term3,
    tok_ref, grad_ref,
    hid_own, hid_peer, gg_own, gg_peer, gu_own, gu_peer,
    out_sum, in_sum,
):
    rep = rep_ref[0]
    rows = (row0, row1, row2, row3)
    terms = (term0, term1, term2, term3)
    width = row0.shape[1] // 2
    for mine in range(4):

        @pl.when(rep == mine)
        def _():
            for place in range(4):
                start = (mine ^ place) * width
                block = rows[place][...]
                tok_ref[:, start : start + width] = block[:, :width]
                grad_ref[:, start : start + width] = block[:, width:]

    tok = tok_ref[...]
    grad = grad_ref[...]
    halves = (
        (gate_own, up_own, down_own, hid_own, gg_own, gu_own),
        (gate_peer, up_peer, down_peer, hid_peer, gg_peer, gu_peer),
    )
    for number, (gate_w, up_w, down_w, hid_out, gg_out, gu_out) in enumerate(halves):
        gate_m, up_m, down_m = gate_w[0], up_w[0], down_w[0]
        pre_gate = contract(tok, gate_m, 1, 1)
        pre_up = contract(tok, up_m, 1, 1)
        grad_hidden = contract(grad, down_m, 1, 1)
        sig = jax.nn.sigmoid(swish_alpha * pre_gate)
        swish = pre_gate * sig
        hidden = ((pre_up + 1.0) * swish).astype(low)
        grad_up = (grad_hidden * swish).astype(low)
        slope = sig + swish_alpha * swish * (1.0 - sig)
        grad_gate = (grad_hidden * (pre_up + 1.0) * slope).astype(low)
        hid_out[...] = hidden
        gg_out[...] = grad_gate
        gu_out[...] = grad_up
        out_part = contract(hidden, down_m, 1, 0)
        in_part = contract(grad_gate, gate_m, 1, 0) + contract(grad_up, up_m, 1, 0)
        if number == 0:
            out_sum[...] = out_part
            in_sum[...] = in_part
        else:
            out_sum[...] += out_part
            in_sum[...] += in_part
    for mine in range(4):

        @pl.when(rep == mine)
        def _():
            for place in range(4):
                start = (mine ^ place) * width
                terms[place][:, :width] = out_sum[:, start : start + width].astype(low)
                terms[place][:, width:] = in_sum[:, start : start + width].astype(low)


def expert(rep, rows, weights, step):
    count, double = rows[0].shape
    width = 2 * double
    hidden = weights[0].shape[1]
    by_row = lambda cols: pl.BlockSpec((step, cols), lambda i, rep: (i, 0))
    whole = pl.BlockSpec((1, hidden, width), lambda i, rep: (0, 0, 0))
    shape = lambda cols: jax.ShapeDtypeStruct((count, cols), low)
    return pl.pallas_call(
        expert_kernel,
        grid_spec=pltpu.PrefetchScalarGridSpec(
            num_scalar_prefetch=1,
            grid=(count // step,),
            in_specs=[by_row(double)] * 4 + [whole] * 6,
            out_specs=[by_row(double)] * 4 + [by_row(width)] * 2 + [by_row(hidden)] * 6,
            scratch_shapes=[pltpu.VMEM((step, width), full)] * 2,
        ),
        out_shape=[shape(double)] * 4 + [shape(width)] * 2 + [shape(hidden)] * 6,
        compiler_params=pltpu.CompilerParams(vmem_limit_bytes=48 << 20),
        cost_estimate=pl.CostEstimate(
            flops=24 * count * width * hidden,
            bytes_accessed=24 * count * width,
            transcendentals=2 * count * hidden,
        ),
    )(rep, *rows, *weights)


def local(tokens, expert_ids, gate_values, out_grad, gate_weight, up_weight, down_weight):
    exp_count = lax.axis_size("exp")
    rep = lax.axis_index("rep")
    tok_rows, top_count = expert_ids.shape
    width = tokens.shape[1]
    half_rows = tok_rows // 2
    experts = exp_count // 2
    capacity = min(half_rows, max(2, tok_rows * top_count // exp_count + 1))
    slot_count = exp_count * capacity
    assigns = tok_rows * top_count
    chunk = (exp_count, 8, capacity * width // 4)

    peer_weights = [exchanged(w, "exp", 1) for w in (gate_weight, up_weight, down_weight)]

    flat_ids = expert_ids.reshape(-1)
    onehot = (flat_ids[:, None] == jnp.arange(experts, dtype=jnp.int32)[None, :]).astype(jnp.int32)
    counted = jnp.cumsum(onehot.reshape(2, half_rows * top_count, experts), axis=1).reshape(
        assigns, experts
    )
    position = jnp.sum((counted - 1) * onehot, axis=1)
    block_ids = jnp.arange(assigns, dtype=jnp.int32) // (half_rows * top_count)
    target = (2 * flat_ids + block_ids) * capacity + position
    match = jnp.arange(slot_count, dtype=jnp.int32)[:, None] == target[None, :]
    placer = match.astype(low)
    token_placer = jnp.sum(placer.reshape(slot_count, tok_rows, top_count), axis=2)
    slot_gate = jnp.sum(jnp.where(match, gate_values.reshape(1, -1), 0.0), axis=1)

    both = jnp.concatenate([tokens, out_grad], axis=1)
    column = jnp.arange(2 * width)[None, :]
    scale = jnp.where(column < width, 1.0, slot_gate[:, None])
    packed = (contract(token_placer, both, 1, 0) * scale).astype(low)
    arrived = lax.all_to_all(
        packed.reshape(chunk), "exp", split_axis=0, concat_axis=0, tiled=True
    ).reshape(slot_count, 2 * width)
    across = exchanged(arrived, "rep", 2)
    beside = exchanged(arrived, "rep", 1)
    far = exchanged(across, "rep", 1)

    weights = [w for pair in zip((gate_weight, up_weight, down_weight), peer_weights) for w in pair]
    (
        term0, term1, term2, term3,
        tok_all, grad_all,
        hid_own, hid_peer, gg_own, gg_peer, gu_own, gu_peer,
    ) = expert(rep.astype(jnp.int32).reshape(1), (arrived, beside, across, far), weights, tok_rows)

    got3 = exchanged(term3, "rep", 1)
    got1 = exchanged(term1, "rep", 1)
    sent = (term2.astype(full) + got3.astype(full)).astype(low)
    got2 = exchanged(sent, "rep", 2)
    kept = term0.astype(full) + got1.astype(full)
    rows = (kept + got2.astype(full)).astype(low)
    returned = lax.all_to_all(
        rows.reshape(chunk), "exp", split_axis=0, concat_axis=0, tiled=True
    ).reshape(slot_count, 2 * width)

    peers = [
        contract(gg_peer, tok_all, 0, 0).astype(low),
        contract(gu_peer, tok_all, 0, 0).astype(low),
        contract(hid_peer, grad_all, 0, 0).astype(low),
    ]
    got = [exchanged(part, "exp", 1) for part in peers]
    owns = [
        contract(gg_own, tok_all, 0, 0),
        contract(gu_own, tok_all, 0, 0),
        contract(hid_own, grad_all, 0, 0),
    ]
    gate_grad, up_grad, down_grad = [
        (own + other.astype(full)).astype(low)[None] for own, other in zip(owns, got)
    ]

    picked = contract(placer, returned, 0, 0).reshape(tok_rows, top_count, 2 * width)
    layer_out = jnp.sum(gate_values[:, :, None] * picked[:, :, :width], axis=1).astype(low)
    input_grad = jnp.sum(picked[:, :, width:], axis=1).astype(low)
    return (layer_out, input_grad, gate_grad, up_grad, down_grad)


def solution(mesh):
    in_specs = (
        P("exp", "rep"),
        P("exp", None),
        P("exp", None),
        P("exp", "rep"),
        P("exp", "rep", None),
        P("exp", "rep", None),
        P("exp", "rep", None),
    )
    out_specs = (
        P("exp", "rep"),
        P("exp", "rep"),
        P("exp", "rep", None),
        P("exp", "rep", None),
        P("exp", "rep", None),
    )
    return jax.shard_map(local, mesh=mesh, in_specs=in_specs, out_specs=out_specs, check_vma=False)
```

time: 393 us -> 278 us (0.71)
  waiting for transfers between devices: 194 us -> 94.9 us
  blocking collectives: 25 us -> 48.5 us
  starting transfers between devices: 66.6 us -> 47.2 us
  matrix products: 34.9 us -> 15.6 us
  Pallas kernels: 0 us -> 17.5 us
  between operations: 14.4 us -> 1 us
  other arithmetic: 14 us -> 8 us
    unnamed x4 -> x0, waiting for transfers between devices: 57 us -> none
    all_to_all x4 -> x1, waiting for transfers between devices: 56.3 us -> 0.01 us  [local(): lax.all_to_all(rows.reshape(chunk), 'exp', split_axis=0, concat_axis=0, t...]
    all_to_all x0 -> x1, blocking collectives: none -> 48.5 us  [local(): lax.all_to_all(packed.reshape(chunk), 'exp', split_axis=0, concat_axis=0,...]
    all_to_all x4 -> x1, starting transfers between devices: 50.8 us -> 8.38 us  [local(): lax.all_to_all(rows.reshape(chunk), 'exp', split_axis=0, concat_axis=0, t...]
    all_gather x2 -> x0, blocking collectives: 25 us -> none  [the longest x1 14.5 us: local(): full_tokens = lax.all_gather(tokens, 'rep', axis=1, tiled=True)]
    ppermute x6 -> x12, starting transfers between devices: 15.8 us -> 38.8 us  [exchanged(): return lax.ppermute(block, axis, [(i, i ^ distance) for i in range(count)])]
    pallas_call x0 -> x1, Pallas kernels: none -> 17.5 us  [expert(): pl.pallas_call(expert_kernel, grid_spec=pltpu.PrefetchScalarGridSpec(num_...]
    dot_general x5 -> x0, matrix products: 17.4 us -> none  [matmul(): return jnp.dot(left, right, preferred_element_type=jnp.float32)]
  transfers between devices with their start and end apart: 12 -> 13, of which waited for: 7 -> 8; matrix products, arithmetic and copies ran while one was open for 17% -> 11% of each run, Pallas kernels for 0% -> 0%
where the time goes in v1:
time: 278 us; the launch traced here: 276 us
  waiting for transfers between devices  94.9 us (34%)
  blocking collectives  48.5 us (17%)
  starting transfers between devices  47.2 us (17%)
  local copies, waits for them, and re-layouts  43.2 us (16%)
  Pallas kernels  17.5 us (6%)
  matrix products  15.6 us (6%)
  other arithmetic  8 us (3%)
    ppermute x12, waiting for transfers between devices, exchanged(): return lax.ppermute(block, axis, [(i, i ^ distance) for i in range(count)])  94.9 us
    all_to_all x1, blocking collectives, local(): lax.all_to_all(packed.reshape(chunk), 'exp', split_axis=0, concat_axis=0,...  48.5 us
    ppermute x12, starting transfers between devices, exchanged(): return lax.ppermute(block, axis, [(i, i ^ distance) for i in range(count)])  38.8 us
    pallas_call x1, Pallas kernels, expert(): pl.pallas_call(expert_kernel, grid_spec=pltpu.PrefetchScalarGridSpec(num_...  17.5 us
    dot_general x8, matrix products, contract(): lax.dot_general(left, right, (((left_dim,), (right_dim,)), ((), ())), pre...  15.6 us
    ppermute x6, local copies, waits for them, and re-layouts, exchanged(): return lax.ppermute(block, axis, [(i, i ^ distance) for i in range(count)])  13.1 us
    all_to_all x1, starting transfers between devices, local(): lax.all_to_all(rows.reshape(chunk), 'exp', split_axis=0, concat_axis=0, t...  8.38 us
    unnamed x33, local copies, waits for them, and re-layouts  6.4 us
  transfers between devices with their start and end apart: 13, of which 8 were waited for; matrix products, arithmetic and copies ran while one was open for 11% of the time, Pallas kernels for 0%

profile of v1, /device:TPU:1, one launch (start us, length us, event | category | flops | bytes accessed | tf_op | source)
XLA Modules:
  0.0 276.0 jit_solution(6568143130794560068)
XLA Ops:
  0.6 0.8 copy.61
  1.7 1.2 reduce-window.6
  2.9 0.2 slice_reduce_fusion.1
  3.2 0.1 fusion.16
  3.5 0.7 fusion.23
  4.4 0.8 copy.65
  5.3 0.1 fusion.11
  5.5 0.2 select_reduce_fusion
  5.7 1.4 multiply_convert_fusion
  7.1 1.0 copy.66
  8.1 3.0 %reshape.137 = bf16[128,8,450]{2,1,0:T(8,128)(2,1)S(1)} reshape(bf16[640,720]{1,0:T(8,128)(2,1)S(1)} %copy.66) | data formatting | bytes 1843200 | tf_op jit(solution)/shard_map/reshape | solution.py:143
  11.1 48.5 %all_to_all.10 = bf16[128,8,450]{2,1,0:T(8,128)(2,1)} all-to-all(bf16[128,8,450]{2,1,0:T(8,128)(2,1)S(1)} %reshape.137), channel_id=1, replica_groups=mesh['rep'=4,'exp'=128] {'exp'}, dimensions={0} | all-to-all | bytes 1843200 | tf_op jit(solution)/shard_map/all_to_all | solution.py:142
  59.6 3.5 %reshape.138.row0 = bf16[640,720]{1,0:T(8,128)(2,1)S(1)} reshape(bf16[128,8,450]{2,1,0:T(8,128)(2,1)} %all_to_all.10) | data formatting | bytes 1843200 | tf_op jit(solution)/shard_map/reshape | solution.py:144
  63.1 1.4 copy.67
  64.5 4.3 %collective-permute-start.1 = (bf16[640,720]{0,1:T(8,128)(2,1)}, bf16[640,720]{0,1:T(8,128)(2,1)}, u32[]{:S(2)}, u32[]{:S(2)}) collective-permute-start(bf16[640,720]{0,1:T(8,128)(2,1)} %copy.67), channel_id=1, source_target_pairs={{0,256},{128,384},{256,0},{384,128},{1,257},{129,385},{257,1},{385... | collective-permute-start | bytes 2764808 | tf_op jit(solution)/shard_map/ppermute | solution.py:15
  68.8 4.5 %collective-permute-start = (bf16[640,720]{0,1:T(8,128)(2,1)}, bf16[640,720]{0,1:T(8,128)(2,1)}, u32[]{:S(2)}, u32[]{:S(2)}) collective-permute-start(bf16[640,720]{0,1:T(8,128)(2,1)} %copy.67), channel_id=1, source_target_pairs={{0,128},{128,0},{256,384},{384,256},{1,129},{129,1},{257,385},{385... | collective-permute-start | bytes 2764808 | tf_op jit(solution)/shard_map/ppermute | solution.py:15
  73.4 14.4 %collective-permute-done.1 = bf16[640,720]{0,1:T(8,128)(2,1)} collective-permute-done((bf16[640,720]{0,1:T(8,128)(2,1)}, bf16[640,720]{0,1:T(8,128)(2,1)}, u32[]{:S(2)}, u32[]{:S(2)}) %collective-permute-start.1) | collective-permute-done | bytes 921632 | tf_op jit(solution)/shard_map/ppermute | solution.py:15
  87.8 5.2 %collective-permute-start.2 = (bf16[640,720]{0,1:T(8,128)(2,1)}, bf16[640,720]{0,1:T(8,128)(2,1)}, u32[]{:S(2)}, u32[]{:S(2)}) collective-permute-start(bf16[640,720]{0,1:T(8,128)(2,1)} %collective-permute-done.1), channel_id=1, source_target_pairs={{0,128},{128,0},{256,384},{384,256},{1,129},{129,1},{257,385},{385... | collective-permute-start | bytes 2764808 | tf_op jit(solution)/shard_map/ppermute | solution.py:15
  92.9 2.5 collective-permute-start.3
  95.5 2.8 %collective-permute-start.4 = (bf16[1,180,1440]{2,1,0:T(8,128)(2,1)S(1)}, bf16[1,180,1440]{2,1,0:T(8,128)(2,1)S(1)}, u32[]{:S(2)}, u32[]{:S(2)}) collective-permute-start(bf16[1,180,1440]{2,1,0:T(8,128)(2,1)S(1)} %copy-done.1), channel_id=1, source_target_pairs={{0,1},{1,0},{2,3},{3,2},{4,5},{5,4},{6,7},{7,6},{8,9},{9,8},{10,11... | collective-permute-start | bytes 1555208 | tf_op jit(solution)/shard_map/ppermute | solution.py:15
  98.3 2.7 collective-permute-start.5
  101.0 2.3 copy.70.row2
  103.2 2.3 copy.69.row1
  105.6 2.3 copy.71.row3
  107.8 1.4 collective-permute-done.3.gate_peer
  109.3 0.8 copy-done.4
  110.1 11.3 %collective-permute-done.4.up_peer = bf16[1,180,1440]{2,1,0:T(8,128)(2,1)S(1)} collective-permute-done((bf16[1,180,1440]{2,1,0:T(8,128)(2,1)S(1)}, bf16[1,180,1440]{2,1,0:T(8,128)(2,1)S(1)}, u32[]{:S(2)}, u32[]{:S(2)}) %collective-permute-start.4) | collective-permute-done | bytes 518432 | tf_op jit(solution)/shard_map/ppermute | solution.py:15
  121.4 0.8 copy-done.6
  122.2 11.4 %collective-permute-done.5.down_peer = bf16[1,180,1440]{2,1,0:T(8,128)(2,1)} collective-permute-done((bf16[1,180,1440]{2,1,0:T(8,128)(2,1)S(1)}, bf16[1,180,1440]{2,1,0:T(8,128)(2,1)}, u32[]{:S(2)}, u32[]{:S(2)}) %collective-permute-start.5) | collective-permute-done | bytes 518432 | tf_op jit(solution)/shard_map/ppermute | solution.py:15
  133.6 1.1 copy-done.3
  134.6 1.1 copy-done.5
  135.7 1.1 copy-done.7
  136.8 17.5 %shard_map.110 = (bf16[640,720]{1,0:T(8,128)(2,1)}, bf16[640,720]{1,0:T(8,128)(2,1)}, bf16[640,720]{1,0:T(8,128)(2,1)}, bf16[640,720]{1,0:T(8,128)(2,1)}, bf16[6...) custom-call(s32[1]{0:T(128)} %bitcast.1.rep_ref, ...), custom_call_target="tpu_custom_call" | custom-call | flops 3981312000 | bytes 22118400 | tf_op jit(solution)/shard_map/pallas_call | solution.py:92
  154.3 2.4 copy.74
  156.7 2.6 collective-permute-start.7
  159.3 1.4 copy.72
  160.7 1.9 collective-permute-start.6
  162.6 1.6 copy.75
  164.2 2.4 add_convert_fusion.1
  166.6 1.9 copy.76
  168.5 4.4 %collective-permute-start.8 = (bf16[640,720]{0,1:T(8,128)(2,1)S(1)}, bf16[640,720]{0,1:T(8,128)(2,1)}, u32[]{:S(2)}, u32[]{:S(2)}) collective-permute-start(bf16[640,720]{0,1:T(8,128)(2,1)S(1)} %copy.76), channel_id=1, source_target_pairs={{0,256},{128,384},{256,0},{384,128},{1,257},{129,385},{257,1},{385... | collective-permute-start | bytes 2764808 | tf_op jit(solution)/shard_map/ppermute | solution.py:15
  173.0 2.4 copy.73
  175.3 18.2 %collective-permute-done.8 = bf16[640,720]{0,1:T(8,128)(2,1)} collective-permute-done((bf16[640,720]{0,1:T(8,128)(2,1)S(1)}, bf16[640,720]{0,1:T(8,128)(2,1)}, u32[]{:S(2)}, u32[]{:S(2)}) %collective-permute-start.8) | collective-permute-done | bytes 921632 | tf_op jit(solution)/shard_map/ppermute | solution.py:15
  193.5 2.3 copy.77
  195.8 2.1 add_convert_fusion
  197.9 4.0 %reshape.139 = bf16[128,8,450]{2,1,0:T(8,128)(2,1)} reshape(bf16[640,720]{1,0:T(8,128)(2,1)S(1)} %add_convert_fusion) | data formatting | bytes 1843200 | tf_op jit(solution)/shard_map/reshape | solution.py:163
  201.9 8.4 %all-to-all-start.1 = ((bf16[128,8,450]{2,1,0:T(8,128)(2,1)}), bf16[128,8,450]{2,1,0:T(8,128)(2,1)}, u32[]{:S(2)}, u32[]{:S(2)}) async-start(bf16[128,8,450]{2,1,0:T(8,128)(2,1)} %reshape.139), calls=%async_computation.1 | async-start | bytes 2097152 | tf_op jit(solution)/shard_map/all_to_all | solution.py:162
  210.3 3.1 %convolution_convert_fusion = bf16[180,1440]{1,0:T(8,128)(2,1)} fusion(bf16[640,180]{1,0:T(8,128)(2,1)S(1)} %get-tuple-element.28, bf16[640,1440]{1,0:T(8,128)(2,1)} %get-tuple-element.27), kind=kOutput, calls=%fused_computation.6 | convolution fusion | flops 332035200 | bytes 2592000 | tf_op jit(solution)/shard_map/dot_general | solution.py:19
  213.4 2.4 collective-permute-start.11
  215.9 1.4 convolution_convert_fusion.1
  217.3 3.1 %collective-permute-start.10 = (bf16[180,1440]{1,0:T(8,128)(2,1)}, bf16[180,1440]{1,0:T(8,128)(2,1)}, u32[]{:S(2)}, u32[]{:S(2)}) collective-permute-start(bf16[180,1440]{1,0:T(8,128)(2,1)} %convolution_convert_fusion.1), channel_id=1, source_target_pairs={{0,1},{1,0},{2,3},{3,2},{4,5},{5,4},{6,7},{7,6},{8,9},{9,8},{10,11... | collective-permute-start | bytes 1555208 | tf_op jit(solution)/shard_map/ppermute | solution.py:15
  220.4 1.4 convolution_convert_fusion.2
  221.8 2.4 collective-permute-start.9
  224.2 0.2 iota_compare_fusion.2
  224.5 0.9 eq.73
  225.4 18.9 %collective-permute-done.11 = bf16[180,1440]{1,0:T(8,128)(2,1)} collective-permute-done((bf16[180,1440]{1,0:T(8,128)(2,1)}, bf16[180,1440]{1,0:T(8,128)(2,1)}, u32[]{:S(2)}, u32[]{:S(2)}) %collective-permute-start.11) | collective-permute-done | bytes 518432 | tf_op jit(solution)/shard_map/ppermute | solution.py:15
  244.3 2.5 fusion.3
  246.8 9.6 %collective-permute-done.10 = bf16[180,1440]{1,0:T(8,128)(2,1)} collective-permute-done((bf16[180,1440]{1,0:T(8,128)(2,1)}, bf16[180,1440]{1,0:T(8,128)(2,1)}, u32[]{:S(2)}, u32[]{:S(2)}) %collective-permute-start.10) | collective-permute-done | bytes 518432 | tf_op jit(solution)/shard_map/ppermute | solution.py:15
  256.4 2.5 fusion.4
  258.9 9.6 %collective-permute-done.9 = bf16[180,1440]{1,0:T(8,128)(2,1)} collective-permute-done((bf16[180,1440]{1,0:T(8,128)(2,1)}, bf16[180,1440]{1,0:T(8,128)(2,1)}, u32[]{:S(2)}, u32[]{:S(2)}) %collective-permute-start.9) | collective-permute-done | bytes 518432 | tf_op jit(solution)/shard_map/ppermute | solution.py:15
  268.5 2.5 fusion.5
  271.0 3.4 %reshape.140 = bf16[640,720]{1,0:T(8,128)(2,1)S(1)} reshape(bf16[128,8,450]{2,1,0:T(8,128)(2,1)} %all-to-all-done.1) | data formatting | bytes 1843200 | tf_op jit(solution)/shard_map/reshape | solution.py:164
  274.4 0.8 fusion.7
  275.2 0.7 slice_reduce_fusion
  (43 shorter events, 0.8 us)
Async XLA Ops:
  59.6 33.3 %copy-start = (bf16[1,180,1440]{2,1,0:T(8,128)(2,1)S(1)}, bf16[1,180,1440]{2,1,0:T(8,128)(2,1)}, u32[]{:S(2)}) copy-start(bf16[1,180,1440]{2,1,0:T(8,128)(2,1)} %gate_own.1) | copy-start | bytes 1555204
  59.6 35.8 %copy-start.1 = (bf16[1,180,1440]{2,1,0:T(8,128)(2,1)S(1)}, bf16[1,180,1440]{2,1,0:T(8,128)(2,1)}, u32[]{:S(2)}) copy-start(bf16[1,180,1440]{2,1,0:T(8,128)(2,1)} %up_own.1) | copy-start | bytes 1555204
  59.6 38.6 %copy-start.2 = (bf16[1,180,1440]{2,1,0:T(8,128)(2,1)S(1)}, bf16[1,180,1440]{2,1,0:T(8,128)(2,1)}, u32[]{:S(2)}) copy-start(bf16[1,180,1440]{2,1,0:T(8,128)(2,1)} %down_own.1) | copy-start | bytes 1555204
  63.1 24.7 %copy-start.11 = (bf16[640,720]{1,0:T(8,128)(2,1)}, bf16[640,720]{1,0:T(8,128)(2,1)S(1)}, u32[]{:S(2)}) copy-start(bf16[640,720]{1,0:T(8,128)(2,1)S(1)} %reshape.138.row0) | copy-start | bytes 2764804
  64.5 23.3 %collective-permute-start.1 = (bf16[640,720]{0,1:T(8,128)(2,1)}, bf16[640,720]{0,1:T(8,128)(2,1)}, u32[]{:S(2)}, u32[]{:S(2)}) collective-permute-start(bf16[640,720]{0,1:T(8,128)(2,1)} %copy.67), channel_id=1, source_target_pairs={{0,256},{128,384},{256,0},{384,128},{1,257},{129,385},{257,1},{385... | collective-permute-start | bytes 2764808 | tf_op jit(solution)/shard_map/ppermute | solution.py:15
  68.8 34.4 %collective-permute-start = (bf16[640,720]{0,1:T(8,128)(2,1)}, bf16[640,720]{0,1:T(8,128)(2,1)}, u32[]{:S(2)}, u32[]{:S(2)}) collective-permute-start(bf16[640,720]{0,1:T(8,128)(2,1)} %copy.67), channel_id=1, source_target_pairs={{0,128},{128,0},{256,384},{384,256},{1,129},{129,1},{257,385},{385... | collective-permute-start | bytes 2764808 | tf_op jit(solution)/shard_map/ppermute | solution.py:15
  87.8 17.8 %collective-permute-start.2 = (bf16[640,720]{0,1:T(8,128)(2,1)}, bf16[640,720]{0,1:T(8,128)(2,1)}, u32[]{:S(2)}, u32[]{:S(2)}) collective-permute-start(bf16[640,720]{0,1:T(8,128)(2,1)} %collective-permute-done.1), channel_id=1, source_target_pairs={{0,128},{128,0},{256,384},{384,256},{1,129},{129,1},{257,385},{385... | collective-permute-start | bytes 2764808 | tf_op jit(solution)/shard_map/ppermute | solution.py:15
  92.9 16.3 %collective-permute-start.3 = (bf16[1,180,1440]{2,1,0:T(8,128)(2,1)S(1)}, bf16[1,180,1440]{2,1,0:T(8,128)(2,1)S(1)}, u32[]{:S(2)}, u32[]{:S(2)}) collective-permute-start(bf16[1,180,1440]{2,1,0:T(8,128)(2,1)S(1)} %copy-done), channel_id=1, source_target_pairs={{0,1},{1,0},{2,3},{3,2},{4,5},{5,4},{6,7},{7,6},{8,9},{9,8},{10,11... | collective-permute-start | bytes 1555208 | tf_op jit(solution)/shard_map/ppermute | solution.py:15
  95.5 25.9 %collective-permute-start.4 = (bf16[1,180,1440]{2,1,0:T(8,128)(2,1)S(1)}, bf16[1,180,1440]{2,1,0:T(8,128)(2,1)S(1)}, u32[]{:S(2)}, u32[]{:S(2)}) collective-permute-start(bf16[1,180,1440]{2,1,0:T(8,128)(2,1)S(1)} %copy-done.1), channel_id=1, source_target_pairs={{0,1},{1,0},{2,3},{3,2},{4,5},{5,4},{6,7},{7,6},{8,9},{9,8},{10,11... | collective-permute-start | bytes 1555208 | tf_op jit(solution)/shard_map/ppermute | solution.py:15
  98.3 35.3 %collective-permute-start.5 = (bf16[1,180,1440]{2,1,0:T(8,128)(2,1)S(1)}, bf16[1,180,1440]{2,1,0:T(8,128)(2,1)}, u32[]{:S(2)}, u32[]{:S(2)}) collective-permute-start(bf16[1,180,1440]{2,1,0:T(8,128)(2,1)S(1)} %copy-done.2), channel_id=1, source_target_pairs={{0,1},{1,0},{2,3},{3,2},{4,5},{5,4},{6,7},{7,6},{8,9},{9,8},{10,11... | collective-permute-start | bytes 1555208 | tf_op jit(solution)/shard_map/ppermute | solution.py:15
  109.3 0.8 copy-start.4
  121.4 0.8 copy-start.6
  133.6 1.1 copy-start.3
  134.6 1.1 copy-start.5
  135.7 1.1 copy-start.7
  154.3 5.0 %copy-start.12 = (bf16[640,720]{1,0:T(8,128)(2,1)S(1)}, bf16[640,720]{1,0:T(8,128)(2,1)}, u32[]{:S(2)}) copy-start(bf16[640,720]{1,0:T(8,128)(2,1)} %get-tuple-element.18) | copy-start | bytes 2764804
  156.7 5.9 %collective-permute-start.7 = (bf16[640,720]{0,1:T(8,128)(2,1)}, bf16[640,720]{0,1:T(8,128)(2,1)}, u32[]{:S(2)}, u32[]{:S(2)}) collective-permute-start(bf16[640,720]{0,1:T(8,128)(2,1)} %copy.74), channel_id=1, source_target_pairs={{0,128},{128,0},{256,384},{384,256},{1,129},{129,1},{257,385},{385... | collective-permute-start | bytes 2764808 | tf_op jit(solution)/shard_map/ppermute | solution.py:15
  160.7 12.3 %collective-permute-start.6 = (bf16[640,720]{0,1:T(8,128)(2,1)}, bf16[640,720]{0,1:T(8,128)(2,1)}, u32[]{:S(2)}, u32[]{:S(2)}) collective-permute-start(bf16[640,720]{0,1:T(8,128)(2,1)} %copy.72), channel_id=1, source_target_pairs={{0,128},{128,0},{256,384},{384,256},{1,129},{129,1},{257,385},{385... | collective-permute-start | bytes 2764808 | tf_op jit(solution)/shard_map/ppermute | solution.py:15
  168.5 25.0 %collective-permute-start.8 = (bf16[640,720]{0,1:T(8,128)(2,1)S(1)}, bf16[640,720]{0,1:T(8,128)(2,1)}, u32[]{:S(2)}, u32[]{:S(2)}) collective-permute-start(bf16[640,720]{0,1:T(8,128)(2,1)S(1)} %copy.76), channel_id=1, source_target_pairs={{0,256},{128,384},{256,0},{384,128},{1,257},{129,385},{257,1},{385... | collective-permute-start | bytes 2764808 | tf_op jit(solution)/shard_map/ppermute | solution.py:15
  201.9 69.1 %all-to-all-start.1 = ((bf16[128,8,450]{2,1,0:T(8,128)(2,1)}), bf16[128,8,450]{2,1,0:T(8,128)(2,1)}, u32[]{:S(2)}, u32[]{:S(2)}) async-start(bf16[128,8,450]{2,1,0:T(8,128)(2,1)} %reshape.139), calls=%async_computation.1 | async-start | bytes 2097152 | tf_op jit(solution)/shard_map/all_to_all | solution.py:162
  210.3 5.5 %copy-start.8 = (bf16[640,1440]{1,0:T(8,128)(2,1)S(1)}, bf16[640,1440]{1,0:T(8,128)(2,1)}, u32[]{:S(2)}) copy-start(bf16[640,1440]{1,0:T(8,128)(2,1)} %get-tuple-element.22) | copy-start | bytes 5529604
  213.4 30.8 %collective-permute-start.11 = (bf16[180,1440]{1,0:T(8,128)(2,1)}, bf16[180,1440]{1,0:T(8,128)(2,1)}, u32[]{:S(2)}, u32[]{:S(2)}) collective-permute-start(bf16[180,1440]{1,0:T(8,128)(2,1)} %convolution_convert_fusion), channel_id=1, source_target_pairs={{0,1},{1,0},{2,3},{3,2},{4,5},{5,4},{6,7},{7,6},{8,9},{9,8},{10,11... | collective-permute-start | bytes 1555208 | tf_op jit(solution)/shard_map/ppermute | solution.py:15
  217.3 39.1 %collective-permute-start.10 = (bf16[180,1440]{1,0:T(8,128)(2,1)}, bf16[180,1440]{1,0:T(8,128)(2,1)}, u32[]{:S(2)}, u32[]{:S(2)}) collective-permute-start(bf16[180,1440]{1,0:T(8,128)(2,1)} %convolution_convert_fusion.1), channel_id=1, source_target_pairs={{0,1},{1,0},{2,3},{3,2},{4,5},{5,4},{6,7},{7,6},{8,9},{9,8},{10,11... | collective-permute-start | bytes 1555208 | tf_op jit(solution)/shard_map/ppermute | solution.py:15
  220.4 23.9 %copy-start.10 = (bf16[640,1440]{1,0:T(8,128)(2,1)S(1)}, bf16[640,1440]{1,0:T(8,128)(2,1)}, u32[]{:S(2)}) copy-start(bf16[640,1440]{1,0:T(8,128)(2,1)} %get-tuple-element.27) | copy-start | bytes 5529604
  221.8 46.7 %collective-permute-start.9 = (bf16[180,1440]{1,0:T(8,128)(2,1)}, bf16[180,1440]{1,0:T(8,128)(2,1)}, u32[]{:S(2)}, u32[]{:S(2)}) collective-permute-start(bf16[180,1440]{1,0:T(8,128)(2,1)} %convolution_convert_fusion.2), channel_id=1, source_target_pairs={{0,1},{1,0},{2,3},{3,2},{4,5},{5,4},{6,7},{7,6},{8,9},{9,8},{10,11... | collective-permute-start | bytes 1555208 | tf_op jit(solution)/shard_map/ppermute | solution.py:15
  225.4 31.0 %copy-start.9 = (bf16[640,1440]{1,0:T(8,128)(2,1)S(1)}, bf16[640,1440]{1,0:T(8,128)(2,1)}, u32[]{:S(2)}) copy-start(bf16[640,1440]{1,0:T(8,128)(2,1)} %get-tuple-element.22) | copy-start | bytes 5529604
  271.0 3.4 %copy-start.13 = (pred[128,4,640]{2,1,0:T(4,128)(4,1)S(1)}, pred[128,4,640]{2,1,0:T(4,128)(4,1)}, u32[]{:S(2)}) copy-start(pred[128,4,640]{2,1,0:T(4,128)(4,1)} %eq.73) | copy-start | bytes 983044
  274.4 0.8 copy-start.14

commit v2 on v1

v2 whole, which is shorter than its diff:
```python
import jax
import jax.numpy as jnp
from jax import lax
from jax.experimental import pallas as pl
from jax.experimental.pallas import tpu as pltpu
from jax.sharding import PartitionSpec as P

swish_alpha = 1.702
low = jnp.bfloat16
full = jnp.float32
HALF = 64
SLOTS = 5
QUARTER = 360
SECOND = 384
LANES = 768
GROUP = 32


def exchanged(block, axis, distance):
    count = lax.axis_size(axis)
    return lax.ppermute(block, axis, [(i, i ^ distance) for i in range(count)])


def contract(left, right, left_dim, right_dim):
    return lax.dot_general(
        left, right, (((left_dim,), (right_dim,)), ((), ())), preferred_element_type=full
    )


def iota(shape, dim):
    return lax.broadcasted_iota(jnp.int32, shape, dim)


def placed(ids, gates, experts):
    tokens = ids.shape[1]
    named = jnp.zeros((experts, tokens), full)
    gate = jnp.zeros((experts, tokens), full)
    for k in range(ids.shape[0]):
        hit = ids[k : k + 1, :] == iota((experts, tokens), 0)
        named = named + jnp.where(hit, 1.0, 0.0)
        gate = gate + jnp.where(hit, gates[k : k + 1, :], 0.0)
    first, later = iota((tokens, tokens), 0), iota((tokens, tokens), 1)
    before = jnp.where((first < later) & (first // HALF == later // HALF), 1.0, 0.0).astype(low)
    number = jnp.where(named > 0.0, contract(named.astype(low), before, 1, 0) + 1.0, 0.0)

    def spread(block):
        return jnp.broadcast_to(block[:, None, :], (experts, 16, tokens)).reshape(
            experts * 16, tokens
        )

    number, gate = spread(number), spread(gate)
    shape = (experts * 16, tokens)
    row = iota(shape, 0) % 8
    same = (iota(shape, 0) // 8) % 2 == iota(shape, 1) // HALF
    number = jnp.where(same, number, 0.0)
    slot = row.astype(full) + 1.0
    rest = 2.0 * (row - SLOTS).astype(full) + 1.0
    main = (row < SLOTS) & (number == slot)
    even = (row >= SLOTS) & (number == rest)
    odd = (row >= SLOTS) & (number == rest + 1.0)
    return main, even, odd, gate


def ones_at(mask):
    return jnp.where(mask, 1.0, 0.0)


def pack_kernel(ids_ref, gates_ref, tok_ref, grad_ref, raw_ref, x_ref):
    experts = raw_ref.shape[0] // 16
    x_ref[...] = jnp.zeros_like(x_ref)
    x_ref[:QUARTER, :] = tok_ref[...]
    x_ref[SECOND : SECOND + QUARTER, :] = grad_ref[...]
    main, even, odd, gate = placed(ids_ref[...], gates_ref[...], experts)
    main1, even1, odd1 = ones_at(main), ones_at(even), ones_at(odd)
    total = lambda block: jnp.sum(block, axis=1, keepdims=True)
    main_gate, even_gate, odd_gate = total(main1 * gate), total(even1 * gate), total(odd1 * gate)
    head = iota(main_gate.shape, 0) % 8 < SLOTS
    main1, even1, odd1 = main1.astype(low), even1.astype(low), odd1.astype(low)
    tail = x_ref[512:768, :]
    left = contract(main1, x_ref[0:256, :], 1, 1) + contract(even1, tail, 1, 1)
    right = contract(main1, x_ref[256:512, :], 1, 1) + contract(odd1, tail, 1, 1)
    raw_ref[:, 0:256] = (left * jnp.where(head, 1.0, even_gate)).astype(low)
    raw_ref[:, 256:384] = (right[:, :128] * jnp.where(head, 1.0, odd_gate)).astype(low)
    raw_ref[:, 384:512] = (right[:, 128:] * jnp.where(head, main_gate, odd_gate)).astype(low)


def pack(ids, gates, tok, grad, rows):
    return pl.pallas_call(
        pack_kernel,
        out_shape=jax.ShapeDtypeStruct((rows, 512), low),
        scratch_shapes=[pltpu.VMEM((LANES, tok.shape[1]), low)],
        compiler_params=pltpu.CompilerParams(vmem_limit_bytes=32 << 20),
        cost_estimate=pl.CostEstimate(
            flops=8 * rows * 128 * 512, bytes_accessed=2 * rows * 512, transcendentals=0
        ),
    )(ids, gates, tok, grad)


def combine_kernel(ids_ref, gates_ref, raw_ref, out_ref, in_ref):
    experts = raw_ref.shape[0] // 16
    main, even, odd, gate = placed(ids_ref[...], gates_ref[...], experts)
    weight = jnp.where(main, gate, 0.0)
    high = weight.astype(low)
    rest = (weight - high.astype(full)).astype(low)
    main1, even1, odd1 = [ones_at(mask).astype(low) for mask in (main, even, odd)]
    out = contract(raw_ref[:, :384], high, 0, 0) + contract(raw_ref[:, :384], rest, 0, 0)
    out_ref[...] = out[:QUARTER].astype(low)
    first = contract(raw_ref[:, 384:512], main1, 0, 0)
    second = contract(raw_ref[:, 0:256], even1, 0, 0) + contract(raw_ref[:, 256:512], odd1, 0, 0)
    in_ref[0:128, :] = first.astype(low)
    in_ref[128:QUARTER, :] = second[: QUARTER - 128].astype(low)


def combine(ids, gates, raw):
    rows = raw.shape[0]
    return pl.pallas_call(
        combine_kernel,
        out_shape=[jax.ShapeDtypeStruct((QUARTER, ids.shape[1]), low)] * 2,
        compiler_params=pltpu.CompilerParams(vmem_limit_bytes=32 << 20),
        cost_estimate=pl.CostEstimate(
            flops=8 * rows * 128 * 512, bytes_accessed=2 * rows * 512, transcendentals=0
        ),
    )(ids, gates, raw)


def selections():
    shape = (GROUP * SLOTS, GROUP * 8)
    dense, raw = iota(shape, 0), iota(shape, 1)
    slot, row = dense % SLOTS, raw % 8
    same = dense // SLOTS == raw // 8
    main = same & (row == slot)
    rest = same & (row == SLOTS + slot // 2)
    even, odd = rest & (slot % 2 == 0), rest & (slot % 2 == 1)
    return [ones_at(mask).astype(low) for mask in (main, even, odd)]


def expert_kernel(
    rep_ref,
    row0, row1, row2, row3,
    gate_own, gate_peer, up_own, up_peer, down_own, down_peer,
    term0, term1, term2, term3,
    tok_ref, grad_ref,
    hid_own, hid_peer, gg_own, gg_peer, gu_own, gu_peer,
    out_sum, in_sum, dense,
):
    rep = rep_ref[0]
    rows = (row0, row1, row2, row3)
    terms = (term0, term1, term2, term3)
    main, even, odd = selections()
    many, wide = main.shape
    groups = row0.shape[0] // wide
    for place in range(4):
        for g in range(groups):
            raw = rows[place][g * wide : (g + 1) * wide, :]
            at = slice(g * many, (g + 1) * many)
            dense[place, at, 0:512] = contract(main, raw, 1, 0).astype(low)
            dense[place, at, 512:768] = (
                contract(even, raw[:, 0:256], 1, 0) + contract(odd, raw[:, 256:512], 1, 0)
            ).astype(low)
    for mine in range(4):

        @pl.when(rep == mine)
        def _():
            for place in range(4):
                start = (mine ^ place) * QUARTER
                tok_ref[:, start : start + QUARTER] = dense[place, :, 0:QUARTER]
                grad_ref[:, start : start + QUARTER] = dense[place, :, SECOND : SECOND + QUARTER]

    tok = tok_ref[...]
    grad = grad_ref[...]
    halves = (
        (gate_own, up_own, down_own, hid_own, gg_own, gu_own),
        (gate_peer, up_peer, down_peer, hid_peer, gg_peer, gu_peer),
    )
    for number, (gate_w, up_w, down_w, hid_out, gg_out, gu_out) in enumerate(halves):
        gate_m, up_m, down_m = gate_w[0], up_w[0], down_w[0]
        pre_gate = contract(tok, gate_m, 1, 1)
        pre_up = contract(tok, up_m, 1, 1)
        grad_hidden = contract(grad, down_m, 1, 1)
        sig = jax.nn.sigmoid(swish_alpha * pre_gate)
        swish = pre_gate * sig
        hidden = ((pre_up + 1.0) * swish).astype(low)
        grad_up = (grad_hidden * swish).astype(low)
        slope = sig + swish_alpha * swish * (1.0 - sig)
        grad_gate = (grad_hidden * (pre_up + 1.0) * slope).astype(low)
        hid_out[...] = hidden
        gg_out[...] = grad_gate
        gu_out[...] = grad_up
        out_part = contract(hidden, down_m, 1, 0)
        in_part = contract(grad_gate, gate_m, 1, 0) + contract(grad_up, up_m, 1, 0)
        if number == 0:
            out_sum[...] = out_part
            in_sum[...] = in_part
        else:
            out_sum[...] += out_part
            in_sum[...] += in_part
    for mine in range(4):

        @pl.when(rep == mine)
        def _():
            for place in range(4):
                start = (mine ^ place) * QUARTER
                dense[place, :, 0:QUARTER] = out_sum[:, start : start + QUARTER].astype(low)
                dense[place, :, SECOND : SECOND + QUARTER] = in_sum[
                    :, start : start + QUARTER
                ].astype(low)

    for place in range(4):
        for g in range(groups):
            block = dense[place, g * many : (g + 1) * many, :]
            tail = block[:, 512:768]
            head = contract(main, block[:, 0:512], 0, 0)
            at = slice(g * wide, (g + 1) * wide)
            terms[place][at, 0:256] = (head[:, 0:256] + contract(even, tail, 0, 0)).astype(low)
            terms[place][at, 256:512] = (head[:, 256:512] + contract(odd, tail, 0, 0)).astype(low)


def expert(rep, rows, weights, steps):
    raw_rows = rows[0].shape[0]
    count = raw_rows // 8 * SLOTS
    hidden, width = weights[0].shape[1:]
    raw = pl.BlockSpec((raw_rows // steps, 512), lambda i, rep: (i, 0))
    by_row = lambda cols: pl.BlockSpec((count // steps, cols), lambda i, rep: (i, 0))
    whole = pl.BlockSpec((1, hidden, width), lambda i, rep: (0, 0, 0))
    shape = lambda cols: jax.ShapeDtypeStruct((count, cols), low)
    return pl.pallas_call(
        expert_kernel,
        grid_spec=pltpu.PrefetchScalarGridSpec(
            num_scalar_prefetch=1,
            grid=(steps,),
            in_specs=[raw] * 4 + [whole] * 6,
            out_specs=[raw] * 4 + [by_row(width)] * 2 + [by_row(hidden)] * 6,
            scratch_shapes=[pltpu.VMEM((count // steps, width), full)] * 2
            + [pltpu.VMEM((4, count // steps, LANES), low)],
        ),
        out_shape=[jax.ShapeDtypeStruct((raw_rows, 512), low)] * 4
        + [shape(width)] * 2
        + [shape(hidden)] * 6,
        compiler_params=pltpu.CompilerParams(vmem_limit_bytes=56 << 20),
        cost_estimate=pl.CostEstimate(
            flops=24 * count * width * hidden,
            bytes_accessed=24 * count * width,
            transcendentals=2 * count * hidden,
        ),
    )(rep, *rows, *weights)


def peer_kernel(gg, gu, hid, tok, grad, gate_out, up_out, down_out):
    gate_out[...] = contract(gg[...], tok[...], 0, 0).astype(low)
    up_out[...] = contract(gu[...], tok[...], 0, 0).astype(low)
    down_out[...] = contract(hid[...], grad[...], 0, 0).astype(low)


def own_kernel(gg, gu, hid, tok, grad, got_gate, got_up, got_down, gate_out, up_out, down_out):
    gate_out[...] = (contract(gg[...], tok[...], 0, 0) + got_gate[...].astype(full)).astype(low)
    up_out[...] = (contract(gu[...], tok[...], 0, 0) + got_up[...].astype(full)).astype(low)
    down_out[...] = (contract(hid[...], grad[...], 0, 0) + got_down[...].astype(full)).astype(low)


def weight_grads(kernel, gg, gu, hid, tok, grad, *got):
    hidden, width = gg.shape[1], tok.shape[1]
    return pl.pallas_call(
        kernel,
        out_shape=[jax.ShapeDtypeStruct((hidden, width), low)] * 3,
        compiler_params=pltpu.CompilerParams(vmem_limit_bytes=48 << 20),
        cost_estimate=pl.CostEstimate(
            flops=6 * tok.shape[0] * width * hidden,
            bytes_accessed=8 * tok.shape[0] * width,
            transcendentals=0,
        ),
    )(gg, gu, hid, tok, grad, *got)


def local(tokens, expert_ids, gate_values, out_grad, gate_weight, up_weight, down_weight):
    exp_count = lax.axis_size("exp")
    rep = lax.axis_index("rep").astype(jnp.int32).reshape(1)
    chunk = (exp_count, 8, 512)
    raw_shape = (exp_count * 8, 512)
    ids, gates = expert_ids.T, gate_values.T

    gate_peer, up_peer, down_peer = [
        exchanged(w, "exp", 1) for w in (gate_weight, up_weight, down_weight)
    ]
    packed = pack(ids, gates, tokens.T, out_grad.T, raw_shape[0])
    arrived = lax.all_to_all(
        packed.reshape(chunk), "exp", split_axis=0, concat_axis=0, tiled=True
    ).reshape(raw_shape)
    arrived, gate_peer, up_peer = lax.optimization_barrier((arrived, gate_peer, up_peer))
    across = exchanged(arrived, "rep", 2)
    beside = exchanged(arrived, "rep", 1)
    far = exchanged(across, "rep", 1)

    weights = (gate_weight, gate_peer, up_weight, up_peer, down_weight, down_peer)
    (
        term0, term1, term2, term3,
        tok_all, grad_all,
        hid_own, hid_peer, gg_own, gg_peer, gu_own, gu_peer,
    ) = expert(rep, (arrived, beside, across, far), weights, 2)

    got3 = exchanged(term3, "rep", 1)
    got1 = exchanged(term1, "rep", 1)
    peers = weight_grads(peer_kernel, gg_peer, gu_peer, hid_peer, tok_all, grad_all)
    got3, *peers = lax.optimization_barrier((got3, *peers))
    got = [exchanged(part, "exp", 1) for part in peers]
    sent = (term2.astype(full) + got3.astype(full)).astype(low)
    got2 = exchanged(sent, "rep", 2)
    rows = (term0.astype(full) + got1.astype(full) + got2.astype(full)).astype(low)
    rows, got[0], got[1] = lax.optimization_barrier((rows, got[0], got[1]))
    returned = lax.all_to_all(
        rows.reshape(chunk), "exp", split_axis=0, concat_axis=0, tiled=True
    ).reshape(raw_shape)
    gate_grad, up_grad, down_grad = weight_grads(
        own_kernel, gg_own, gu_own, hid_own, tok_all, grad_all, *got
    )
    layer_out, input_grad = combine(ids, gates, returned)
    return (layer_out.T, input_grad.T, gate_grad[None], up_grad[None], down_grad[None])


def solution(mesh):
    in_specs = (
        P("exp", "rep"),
        P("exp", None),
        P("exp", None),
        P("exp", "rep"),
        P("exp", "rep", None),
        P("exp", "rep", None),
        P("exp", "rep", None),
    )
    out_specs = (
        P("exp", "rep"),
        P("exp", "rep"),
        P("exp", "rep", None),
        P("exp", "rep", None),
        P("exp", "rep", None),
    )
    return jax.shard_map(local, mesh=mesh, in_specs=in_specs, out_specs=out_specs, check_vma=False)
```

time: 278 us -> 244 us (0.88)
  blocking collectives: 48.5 us -> 0 us
  waiting for transfers between devices: 94.9 us -> 124 us
  local copies, waits for them, and re-layouts: 43.2 us -> 15.1 us
  starting transfers between devices: 47.2 us -> 70.4 us
  matrix products: 15.6 us -> 0 us
  Pallas kernels: 17.5 us -> 30.1 us
  other arithmetic: 8 us -> 1.71 us
    all_to_all x1 -> x0, blocking collectives: 48.5 us -> none  [local(): lax.all_to_all(packed.reshape(chunk), 'exp', split_axis=0, concat_axis=0,...]
    ppermute x12, waiting for transfers between devices: 94.9 us -> 124 us  [exchanged(): return lax.ppermute(block, axis, [(i, i ^ distance) for i in range(count)])]
    all_to_all x0 -> x1, starting transfers between devices: none -> 19.3 us  [local(): lax.all_to_all(packed.reshape(chunk), 'exp', split_axis=0, concat_axis=0,...]
    dot_general x8 -> x0, matrix products: 15.6 us -> none  [contract(): lax.dot_general(left, right, (((left_dim,), (right_dim,)), ((), ())), pre...]
    reshape x5 -> x0, local copies, waits for them, and re-layouts: 15.2 us -> none  [the longest x2 4.83 us: local(): arrived = lax.all_to_all(packed.reshape(chunk), 'exp', split_axis=0, conc...]
    ppermute x6 -> x0, local copies, waits for them, and re-layouts: 13.1 us -> none  [exchanged(): return lax.ppermute(block, axis, [(i, i ^ distance) for i in range(count)])]
    pallas_call x0 -> x4, Pallas kernels: none -> 11.1 us  [the longest x2 7.15 us: weight_grads(): pl.pallas_call(kernel, out_shape=[jax.ShapeDtypeStruct((hidden, width), l...]
    unnamed x33 -> x54, local copies, waits for them, and re-layouts: 6.4 us -> 15.1 us
  transfers between devices with their start and end apart: 13 -> 14, of which waited for: 8 -> 7; matrix products, arithmetic and copies ran while one was open for 11% -> 1% of each run, Pallas kernels for 0% -> 3%
where the time goes in v2:
time: 244 us; the launch traced here: 243 us
  waiting for transfers between devices  124 us (51%)
  starting transfers between devices  70.4 us (29%)
  Pallas kernels  30.1 us (12%)
  local copies, waits for them, and re-layouts  15.1 us (6%)
    ppermute x12, waiting for transfers between devices, exchanged(): return lax.ppermute(block, axis, [(i, i ^ distance) for i in range(count)])  124 us
    ppermute x12, starting transfers between devices, exchanged(): return lax.ppermute(block, axis, [(i, i ^ distance) for i in range(count)])  37.6 us
    all_to_all x1, starting transfers between devices, local(): lax.all_to_all(packed.reshape(chunk), 'exp', split_axis=0, concat_axis=0,...  19.3 us
    pallas_call x1, Pallas kernels, expert(): pl.pallas_call(expert_kernel, grid_spec=pltpu.PrefetchScalarGridSpec(num_...  19.1 us
    unnamed x54, local copies, waits for them, and re-layouts  15.1 us
    all_to_all x1, starting transfers between devices, local(): lax.all_to_all(rows.reshape(chunk), 'exp', split_axis=0, concat_axis=0, t...  13.5 us
    pallas_call x2, Pallas kernels, weight_grads(): pl.pallas_call(kernel, out_shape=[jax.ShapeDtypeStruct((hidden, width), l...  7.15 us
  transfers between devices with their start and end apart: 14, of which 7 were waited for; matrix products, arithmetic and copies ran while one was open for 1% of the time, Pallas kernels for 3%

profile of v2, /device:TPU:1, one launch (start us, length us, event | category | flops | bytes accessed | tf_op | source)
XLA Modules:
  0.0 242.7 jit_solution(13109987767184079849)
XLA Ops:
  0.6 0.0 copy-start.13
  0.6 0.9 copy-done.13
  1.5 0.9 copy-done.14
  2.4 0.7 copy-done.15
  3.1 0.7 copy-done.17
  3.8 2.1 shard_map.110
  5.9 19.3 %all-to-all-start = ((bf16[128,8,512]{2,1,0:T(8,128)(2,1)}), bf16[128,8,512]{2,1,0:T(8,128)(2,1)S(1)}, u32[]{:S(2)}, u32[]{:S(2)}) async-start(bf16[128,8,512]{2,1,0:T(8,128)(2,1)} %bitcast.5), calls=%async_computation | async-start | bytes 2097152 | tf_op jit(solution)/shard_map/all_to_all | solution.py:285
  25.2 0.0 copy-done.24
  25.2 2.5 %collective-permute-start = (bf16[1,180,1440]{2,1,0:T(8,128)(2,1)S(1)}, bf16[1,180,1440]{2,1,0:T(8,128)(2,1)S(1)}, u32[]{:S(2)}, u32[]{:S(2)}) collective-permute-start(bf16[1,180,1440]{2,1,0:T(8,128)(2,1)S(1)} %copy-done.24), channel_id=1, source_target_pairs={{0,1},{1,0},{2,3},{3,2},{4,5},{5,4},{6,7},{7,6},{8,9},{9,8},{10,11... | collective-permute-start | bytes 1555208 | tf_op jit(solution)/shard_map/ppermute | solution.py:21
  27.7 0.0 copy-done.25
  27.7 2.8 %collective-permute-start.1 = (bf16[1,180,1440]{2,1,0:T(8,128)(2,1)S(1)}, bf16[1,180,1440]{2,1,0:T(8,128)(2,1)}, u32[]{:S(2)}, u32[]{:S(2)}) collective-permute-start(bf16[1,180,1440]{2,1,0:T(8,128)(2,1)S(1)} %copy-done.25), channel_id=1, source_target_pairs={{0,1},{1,0},{2,3},{3,2},{4,5},{5,4},{6,7},{7,6},{8,9},{9,8},{10,11... | collective-permute-start | bytes 1555208 | tf_op jit(solution)/shard_map/ppermute | solution.py:21
  30.5 29.3 %collective-permute-done.gate_peer = bf16[1,180,1440]{2,1,0:T(8,128)(2,1)S(1)} collective-permute-done((bf16[1,180,1440]{2,1,0:T(8,128)(2,1)S(1)}, bf16[1,180,1440]{2,1,0:T(8,128)(2,1)S(1)}, u32[]{:S(2)}, u32[]{:S(2)}) %collective-permute-start) | collective-permute-done | bytes 518432 | tf_op jit(solution)/shard_map/ppermute | solution.py:21
  59.8 0.8 copy-done.26
  60.6 11.4 %collective-permute-done.1.up_peer = bf16[1,180,1440]{2,1,0:T(8,128)(2,1)} collective-permute-done((bf16[1,180,1440]{2,1,0:T(8,128)(2,1)S(1)}, bf16[1,180,1440]{2,1,0:T(8,128)(2,1)}, u32[]{:S(2)}, u32[]{:S(2)}) %collective-permute-start.1) | collective-permute-done | bytes 518432 | tf_op jit(solution)/shard_map/ppermute | solution.py:21
  72.0 0.0 all-to-all-done
  72.0 4.3 %collective-permute-start.3 = (bf16[1024,512]{1,0:T(8,128)(2,1)S(1)}, bf16[1024,512]{1,0:T(8,128)(2,1)S(1)}, u32[]{:S(2)}, u32[]{:S(2)}) collective-permute-start(bf16[1024,512]{1,0:T(8,128)(2,1)S(1)} %bitcast.22), channel_id=1, source_target_pairs={{0,256},{128,384},{256,0},{384,128},{1,257},{129,385},{257,1},{385... | collective-permute-start | bytes 3145736 | tf_op jit(solution)/shard_map/ppermute | solution.py:21
  76.3 3.7 %collective-permute-start.2 = (bf16[1024,512]{1,0:T(8,128)(2,1)S(1)}, bf16[1024,512]{1,0:T(8,128)(2,1)S(1)}, u32[]{:S(2)}, u32[]{:S(2)}) collective-permute-start(bf16[1024,512]{1,0:T(8,128)(2,1)S(1)} %bitcast.23), channel_id=1, source_target_pairs={{0,128},{128,0},{256,384},{384,256},{1,129},{129,1},{257,385},{385... | collective-permute-start | bytes 3145736 | tf_op jit(solution)/shard_map/ppermute | solution.py:21
  80.1 18.4 %collective-permute-done.3.row2 = bf16[1024,512]{1,0:T(8,128)(2,1)S(1)} collective-permute-done((bf16[1024,512]{1,0:T(8,128)(2,1)S(1)}, bf16[1024,512]{1,0:T(8,128)(2,1)S(1)}, u32[]{:S(2)}, u32[]{:S(2)}) %collective-permute-start.3) | collective-permute-done | bytes 1048608 | tf_op jit(solution)/shard_map/ppermute | solution.py:21
  98.5 4.3 %collective-permute-start.4 = (bf16[1024,512]{1,0:T(8,128)(2,1)S(1)}, bf16[1024,512]{1,0:T(8,128)(2,1)}, u32[]{:S(2)}, u32[]{:S(2)}) collective-permute-start(bf16[1024,512]{1,0:T(8,128)(2,1)S(1)} %collective-permute-done.3.row2), channel_id=1, source_target_pairs={{0,128},{128,0},{256,384},{384,256},{1,129},{129,1},{257,385},{385... | collective-permute-start | bytes 3145736 | tf_op jit(solution)/shard_map/ppermute | solution.py:21
  102.9 2.8 %collective-permute-start.5 = (bf16[1,180,1440]{2,1,0:T(8,128)(2,1)}, bf16[1,180,1440]{2,1,0:T(8,128)(2,1)}, u32[]{:S(2)}, u32[]{:S(2)}) collective-permute-start(bf16[1,180,1440]{2,1,0:T(8,128)(2,1)} %down_own.1), channel_id=1, source_target_pairs={{0,1},{1,0},{2,3},{3,2},{4,5},{5,4},{6,7},{7,6},{8,9},{9,8},{10,11... | collective-permute-start | bytes 1555208 | tf_op jit(solution)/shard_map/ppermute | solution.py:21
  105.7 13.8 %collective-permute-done.5.down_peer = bf16[1,180,1440]{2,1,0:T(8,128)(2,1)} collective-permute-done((bf16[1,180,1440]{2,1,0:T(8,128)(2,1)}, bf16[1,180,1440]{2,1,0:T(8,128)(2,1)}, u32[]{:S(2)}, u32[]{:S(2)}) %collective-permute-start.5) | collective-permute-done | bytes 518432 | tf_op jit(solution)/shard_map/ppermute | solution.py:21
  119.5 0.0 collective-permute-done.2.row1
  119.5 0.0 collective-permute-done.4.row3
  119.5 0.0 copy-done.20
  119.5 0.0 copy-done.22
  119.5 1.0 copy-done.23
  120.5 19.1 %shard_map.111 = (bf16[1024,512]{1,0:T(8,128)(2,1)}, bf16[1024,512]{1,0:T(8,128)(2,1)}, bf16[1024,512]{1,0:T(8,128)(2,1)}, bf16[1024,512]{1,0:T(8,128)(2,1)}, bf...) custom-call(s32[1]{0:T(128)} %bitcast.2.rep_ref, ...), custom_call_target="tpu_custom_call" | custom-call | flops 3981312000 | bytes 22118400 | tf_op jit(solution)/shard_map/pallas_call | solution.py:226
  139.5 2.6 %collective-permute-start.7 = (bf16[1024,512]{1,0:T(8,128)(2,1)}, bf16[1024,512]{1,0:T(8,128)(2,1)S(1)}, u32[]{:S(2)}, u32[]{:S(2)}) collective-permute-start(bf16[1024,512]{1,0:T(8,128)(2,1)} %get-tuple-element.41), channel_id=1, source_target_pairs={{0,128},{128,0},{256,384},{384,256},{1,129},{129,1},{257,385},{385... | collective-permute-start | bytes 3145736 | tf_op jit(solution)/shard_map/ppermute | solution.py:21
  142.2 1.9 collective-permute-start.6
  144.1 0.0 copy-start
  144.1 1.5 copy-done
  145.7 1.0 copy-done.9
  146.6 1.0 copy-done.10
  147.6 1.0 copy-done.11
  148.6 3.2 %shard_map.112 = (bf16[180,1440]{1,0:T(8,128)(2,1)S(1)}, bf16[180,1440]{1,0:T(8,128)(2,1)S(1)}, bf16[180,1440]{1,0:T(8,128)(2,1)S(1)}) custom-call(bf16[640,180]{1,0:T(8,128)(2,1)S(1)} %copy-done.10, bf16[640,180]{1,0:T(8,128)(2,1)S(1)} %copy-done.11, bf16[640,180]{1,0:T(8,128)(2,1)S(1)} %copy-done.9, bf16[640,1440]{1,0:T(8,128)(2,1)S(1)} %copy-done, ...), custom_call_target="tpu_custom_call" | custom-call | flops 995328000 | bytes 7372800 | tf_op jit(solution)/shard_map/pallas_call | solution.py:262
  151.8 0.0 copy-start.12
  151.8 0.0 copy-start.21
  151.8 0.0 collective-permute-done.7
  151.8 0.0 copy-done.19
  151.8 0.3 add_convert_fusion.1
  152.1 4.6 %collective-permute-start.8 = (bf16[1024,512]{1,0:T(8,128)(2,1)S(1)}, bf16[1024,512]{1,0:T(8,128)(2,1)S(1)}, u32[]{:S(2)}, u32[]{:S(2)}) collective-permute-start(bf16[1024,512]{1,0:T(8,128)(2,1)S(1)} %add_convert_fusion.1), channel_id=1, source_target_pairs={{0,256},{128,384},{256,0},{384,128},{1,257},{129,385},{257,1},{385... | collective-permute-start | bytes 3145736 | tf_op jit(solution)/shard_map/ppermute | solution.py:21
  156.7 2.7 %collective-permute-start.9 = (bf16[180,1440]{1,0:T(8,128)(2,1)S(1)}, bf16[180,1440]{1,0:T(8,128)(2,1)S(1)}, u32[]{:S(2)}, u32[]{:S(2)}) collective-permute-start(bf16[180,1440]{1,0:T(8,128)(2,1)S(1)} %get-tuple-element.51), channel_id=1, source_target_pairs={{0,1},{1,0},{2,3},{3,2},{4,5},{5,4},{6,7},{7,6},{8,9},{9,8},{10,11... | collective-permute-start | bytes 1555208 | tf_op jit(solution)/shard_map/ppermute | solution.py:21
  159.3 2.8 %collective-permute-start.10 = (bf16[180,1440]{1,0:T(8,128)(2,1)S(1)}, bf16[180,1440]{1,0:T(8,128)(2,1)S(1)}, u32[]{:S(2)}, u32[]{:S(2)}) collective-permute-start(bf16[180,1440]{1,0:T(8,128)(2,1)S(1)} %get-tuple-element.52), channel_id=1, source_target_pairs={{0,1},{1,0},{2,3},{3,2},{4,5},{5,4},{6,7},{7,6},{8,9},{9,8},{10,11... | collective-permute-start | bytes 1555208 | tf_op jit(solution)/shard_map/ppermute | solution.py:21
  162.2 0.0 collective-permute-done.6
  162.2 17.7 %collective-permute-done.8 = bf16[1024,512]{1,0:T(8,128)(2,1)S(1)} collective-permute-done((bf16[1024,512]{1,0:T(8,128)(2,1)S(1)}, bf16[1024,512]{1,0:T(8,128)(2,1)S(1)}, u32[]{:S(2)}, u32[]{:S(2)}) %collective-permute-start.8) | collective-permute-done | bytes 1048608 | tf_op jit(solution)/shard_map/ppermute | solution.py:21
  179.9 0.0 copy-done.21
  179.9 1.4 add_convert_fusion
  181.3 0.0 copy-done.12
  181.3 0.0 collective-permute-done.9.got_gate
  181.3 0.8 copy-done.2
  182.1 2.1 collective-permute-done.10.got_up
  184.2 0.8 copy-done.4
  185.0 13.5 %all-to-all-start.1 = ((bf16[128,8,512]{2,1,0:T(8,128)(2,1)}), bf16[128,8,512]{2,1,0:T(8,128)(2,1)S(1)}, u32[]{:S(2)}, u32[]{:S(2)}) async-start(bf16[128,8,512]{2,1,0:T(8,128)(2,1)} %bitcast.21), calls=%async_computation.1 | async-start | bytes 2097152 | tf_op jit(solution)/shard_map/all_to_all | solution.py:309
  198.6 2.5 %collective-permute-start.11 = (bf16[180,1440]{1,0:T(8,128)(2,1)}, bf16[180,1440]{1,0:T(8,128)(2,1)S(1)}, u32[]{:S(2)}, u32[]{:S(2)}) collective-permute-start(bf16[180,1440]{1,0:T(8,128)(2,1)} %copy-done.12), channel_id=1, source_target_pairs={{0,1},{1,0},{2,3},{3,2},{4,5},{5,4},{6,7},{7,6},{8,9},{9,8},{10,11... | collective-permute-start | bytes 1555208 | tf_op jit(solution)/shard_map/ppermute | solution.py:21
  201.1 31.7 %collective-permute-done.11.got_down = bf16[180,1440]{1,0:T(8,128)(2,1)S(1)} collective-permute-done((bf16[180,1440]{1,0:T(8,128)(2,1)}, bf16[180,1440]{1,0:T(8,128)(2,1)S(1)}, u32[]{:S(2)}, u32[]{:S(2)}) %collective-permute-start.11) | collective-permute-done | bytes 518432 | tf_op jit(solution)/shard_map/ppermute | solution.py:21
  232.8 0.0 copy-done.6
  232.8 0.0 copy-done.1
  232.8 1.1 copy-done.3
  233.9 1.1 copy-done.5
  234.9 1.0 copy-done.7
  235.9 1.0 copy-done.8
  236.9 4.0 %shard_map.114 = (bf16[180,1440]{1,0:T(8,128)(2,1)}, bf16[180,1440]{1,0:T(8,128)(2,1)}, bf16[180,1440]{1,0:T(8,128)(2,1)}) custom-call(bf16[640,180]{1,0:T(8,128)(2,1)S(1)} %copy-done.7, bf16[640,180]{1,0:T(8,128)(2,1)S(1)} %copy-done.8, bf16[640,180]{1,0:T(8,128)(2,1)S(1)} %copy-done.6, bf16[640,1440]{1,0:T(8,128)(2,1)S(1)} %copy-done.1, ...), custom_call_target="tpu_custom_call" | custom-call | flops 995328000 | bytes 7372800 | tf_op jit(solution)/shard_map/pallas_call | solution.py:262
  240.8 0.0 all-to-all-done.1
  240.8 1.9 shard_map.113
  (25 shorter events, 0.0 us)
Async XLA Ops:
  0.6 0.9 copy-start.13
  1.5 0.9 copy-start.14
  2.4 0.7 copy-start.15
  3.1 0.7 copy-start.17
  3.8 21.4 %copy-start.24 = (bf16[1,180,1440]{2,1,0:T(8,128)(2,1)S(1)}, bf16[1,180,1440]{2,1,0:T(8,128)(2,1)}, u32[]{:S(2)}) copy-start(bf16[1,180,1440]{2,1,0:T(8,128)(2,1)} %gate_own.1) | copy-start | bytes 1555204
  3.8 23.9 %copy-start.25 = (bf16[1,180,1440]{2,1,0:T(8,128)(2,1)S(1)}, bf16[1,180,1440]{2,1,0:T(8,128)(2,1)}, u32[]{:S(2)}) copy-start(bf16[1,180,1440]{2,1,0:T(8,128)(2,1)} %up_own.1) | copy-start | bytes 1555204
  5.9 66.1 %all-to-all-start = ((bf16[128,8,512]{2,1,0:T(8,128)(2,1)}), bf16[128,8,512]{2,1,0:T(8,128)(2,1)S(1)}, u32[]{:S(2)}, u32[]{:S(2)}) async-start(bf16[128,8,512]{2,1,0:T(8,128)(2,1)} %bitcast.5), calls=%async_computation | async-start | bytes 2097152 | tf_op jit(solution)/shard_map/all_to_all | solution.py:285
  25.2 34.6 %collective-permute-start = (bf16[1,180,1440]{2,1,0:T(8,128)(2,1)S(1)}, bf16[1,180,1440]{2,1,0:T(8,128)(2,1)S(1)}, u32[]{:S(2)}, u32[]{:S(2)}) collective-permute-start(bf16[1,180,1440]{2,1,0:T(8,128)(2,1)S(1)} %copy-done.24), channel_id=1, source_target_pairs={{0,1},{1,0},{2,3},{3,2},{4,5},{5,4},{6,7},{7,6},{8,9},{9,8},{10,11... | collective-permute-start | bytes 1555208 | tf_op jit(solution)/shard_map/ppermute | solution.py:21
  27.7 44.3 %collective-permute-start.1 = (bf16[1,180,1440]{2,1,0:T(8,128)(2,1)S(1)}, bf16[1,180,1440]{2,1,0:T(8,128)(2,1)}, u32[]{:S(2)}, u32[]{:S(2)}) collective-permute-start(bf16[1,180,1440]{2,1,0:T(8,128)(2,1)S(1)} %copy-done.25), channel_id=1, source_target_pairs={{0,1},{1,0},{2,3},{3,2},{4,5},{5,4},{6,7},{7,6},{8,9},{9,8},{10,11... | collective-permute-start | bytes 1555208 | tf_op jit(solution)/shard_map/ppermute | solution.py:21
  59.8 0.8 copy-start.26
  72.0 47.5 %copy-start.20 = (bf16[128,8,512]{2,1,0:T(8,128)(2,1)}, bf16[128,8,512]{2,1,0:T(8,128)(2,1)S(1)}, u32[]{:S(2)}) copy-start(bf16[128,8,512]{2,1,0:T(8,128)(2,1)S(1)} %all-to-all-done) | copy-start | bytes 3145732
  72.0 26.5 %collective-permute-start.3 = (bf16[1024,512]{1,0:T(8,128)(2,1)S(1)}, bf16[1024,512]{1,0:T(8,128)(2,1)S(1)}, u32[]{:S(2)}, u32[]{:S(2)}) collective-permute-start(bf16[1024,512]{1,0:T(8,128)(2,1)S(1)} %bitcast.22), channel_id=1, source_target_pairs={{0,256},{128,384},{256,0},{384,128},{1,257},{129,385},{257,1},{385... | collective-permute-start | bytes 3145736 | tf_op jit(solution)/shard_map/ppermute | solution.py:21
  76.3 43.2 %collective-permute-start.2 = (bf16[1024,512]{1,0:T(8,128)(2,1)S(1)}, bf16[1024,512]{1,0:T(8,128)(2,1)S(1)}, u32[]{:S(2)}, u32[]{:S(2)}) collective-permute-start(bf16[1024,512]{1,0:T(8,128)(2,1)S(1)} %bitcast.23), channel_id=1, source_target_pairs={{0,128},{128,0},{256,384},{384,256},{1,129},{129,1},{257,385},{385... | collective-permute-start | bytes 3145736 | tf_op jit(solution)/shard_map/ppermute | solution.py:21
  98.5 21.0 %copy-start.22 = (bf16[1024,512]{1,0:T(8,128)(2,1)}, bf16[1024,512]{1,0:T(8,128)(2,1)S(1)}, u32[]{:S(2)}) copy-start(bf16[1024,512]{1,0:T(8,128)(2,1)S(1)} %collective-permute-done.3.row2) | copy-start | bytes 3145732
  98.5 21.0 %collective-permute-start.4 = (bf16[1024,512]{1,0:T(8,128)(2,1)S(1)}, bf16[1024,512]{1,0:T(8,128)(2,1)}, u32[]{:S(2)}, u32[]{:S(2)}) collective-permute-start(bf16[1024,512]{1,0:T(8,128)(2,1)S(1)} %collective-permute-done.3.row2), channel_id=1, source_target_pairs={{0,128},{128,0},{256,384},{384,256},{1,129},{129,1},{257,385},{385... | collective-permute-start | bytes 3145736 | tf_op jit(solution)/shard_map/ppermute | solution.py:21
  102.9 16.6 %collective-permute-start.5 = (bf16[1,180,1440]{2,1,0:T(8,128)(2,1)}, bf16[1,180,1440]{2,1,0:T(8,128)(2,1)}, u32[]{:S(2)}, u32[]{:S(2)}) collective-permute-start(bf16[1,180,1440]{2,1,0:T(8,128)(2,1)} %down_own.1), channel_id=1, source_target_pairs={{0,1},{1,0},{2,3},{3,2},{4,5},{5,4},{6,7},{7,6},{8,9},{9,8},{10,11... | collective-permute-start | bytes 1555208 | tf_op jit(solution)/shard_map/ppermute | solution.py:21
  119.5 1.0 copy-start.23
  139.5 12.3 %collective-permute-start.7 = (bf16[1024,512]{1,0:T(8,128)(2,1)}, bf16[1024,512]{1,0:T(8,128)(2,1)S(1)}, u32[]{:S(2)}, u32[]{:S(2)}) collective-permute-start(bf16[1024,512]{1,0:T(8,128)(2,1)} %get-tuple-element.41), channel_id=1, source_target_pairs={{0,128},{128,0},{256,384},{384,256},{1,129},{129,1},{257,385},{385... | collective-permute-start | bytes 3145736 | tf_op jit(solution)/shard_map/ppermute | solution.py:21
  142.2 20.0 %collective-permute-start.6 = (bf16[1024,512]{1,0:T(8,128)(2,1)}, bf16[1024,512]{1,0:T(8,128)(2,1)S(1)}, u32[]{:S(2)}, u32[]{:S(2)}) collective-permute-start(bf16[1024,512]{1,0:T(8,128)(2,1)} %get-tuple-element.39), channel_id=1, source_target_pairs={{0,128},{128,0},{256,384},{384,256},{1,129},{129,1},{257,385},{385... | collective-permute-start | bytes 3145736 | tf_op jit(solution)/shard_map/ppermute | solution.py:21
  144.1 1.5 copy-start
  145.7 1.0 copy-start.9
  146.6 1.0 copy-start.10
  147.6 1.0 copy-start.11
  148.6 3.2 %copy-start.19 = (bf16[1024,512]{1,0:T(8,128)(2,1)S(1)}, bf16[1024,512]{1,0:T(8,128)(2,1)}, u32[]{:S(2)}) copy-start(bf16[1024,512]{1,0:T(8,128)(2,1)} %get-tuple-element.40) | copy-start | bytes 3145732
  151.8 29.5 %copy-start.12 = (bf16[180,1440]{1,0:T(8,128)(2,1)}, bf16[180,1440]{1,0:T(8,128)(2,1)S(1)}, u32[]{:S(2)}) copy-start(bf16[180,1440]{1,0:T(8,128)(2,1)S(1)} %get-tuple-element.61) | copy-start | bytes 1555204
  151.8 28.1 %copy-start.21 = (bf16[1024,512]{1,0:T(8,128)(2,1)S(1)}, bf16[1024,512]{1,0:T(8,128)(2,1)}, u32[]{:S(2)}) copy-start(bf16[1024,512]{1,0:T(8,128)(2,1)} %get-tuple-element.38) | copy-start | bytes 3145732
  152.1 27.8 %collective-permute-start.8 = (bf16[1024,512]{1,0:T(8,128)(2,1)S(1)}, bf16[1024,512]{1,0:T(8,128)(2,1)S(1)}, u32[]{:S(2)}, u32[]{:S(2)}) collective-permute-start(bf16[1024,512]{1,0:T(8,128)(2,1)S(1)} %add_convert_fusion.1), channel_id=1, source_target_pairs={{0,256},{128,384},{256,0},{384,128},{1,257},{129,385},{257,1},{385... | collective-permute-start | bytes 3145736 | tf_op jit(solution)/shard_map/ppermute | solution.py:21
  156.7 24.6 %collective-permute-start.9 = (bf16[180,1440]{1,0:T(8,128)(2,1)S(1)}, bf16[180,1440]{1,0:T(8,128)(2,1)S(1)}, u32[]{:S(2)}, u32[]{:S(2)}) collective-permute-start(bf16[180,1440]{1,0:T(8,128)(2,1)S(1)} %get-tuple-element.51), channel_id=1, source_target_pairs={{0,1},{1,0},{2,3},{3,2},{4,5},{5,4},{6,7},{7,6},{8,9},{9,8},{10,11... | collective-permute-start | bytes 1555208 | tf_op jit(solution)/shard_map/ppermute | solution.py:21
  159.3 24.9 %collective-permute-start.10 = (bf16[180,1440]{1,0:T(8,128)(2,1)S(1)}, bf16[180,1440]{1,0:T(8,128)(2,1)S(1)}, u32[]{:S(2)}, u32[]{:S(2)}) collective-permute-start(bf16[180,1440]{1,0:T(8,128)(2,1)S(1)} %get-tuple-element.52), channel_id=1, source_target_pairs={{0,1},{1,0},{2,3},{3,2},{4,5},{5,4},{6,7},{7,6},{8,9},{9,8},{10,11... | collective-permute-start | bytes 1555208 | tf_op jit(solution)/shard_map/ppermute | solution.py:21
  179.9 52.9 %copy-start.6 = (bf16[640,180]{1,0:T(8,128)(2,1)S(1)}, bf16[640,180]{1,0:T(8,128)(2,1)}, u32[]{:S(2)}) copy-start(bf16[640,180]{1,0:T(8,128)(2,1)} %get-tuple-element.58.hid) | copy-start | bytes 691204
  181.3 51.5 %copy-start.1 = (bf16[640,1440]{1,0:T(8,128)(2,1)S(1)}, bf16[640,1440]{1,0:T(8,128)(2,1)}, u32[]{:S(2)}) copy-start(bf16[640,1440]{1,0:T(8,128)(2,1)} %get-tuple-element.45.tok) | copy-start | bytes 5529604
  181.3 0.8 copy-start.2
  184.2 0.8 copy-start.4
  185.0 55.8 %all-to-all-start.1 = ((bf16[128,8,512]{2,1,0:T(8,128)(2,1)}), bf16[128,8,512]{2,1,0:T(8,128)(2,1)S(1)}, u32[]{:S(2)}, u32[]{:S(2)}) async-start(bf16[128,8,512]{2,1,0:T(8,128)(2,1)} %bitcast.21), calls=%async_computation.1 | async-start | bytes 2097152 | tf_op jit(solution)/shard_map/all_to_all | solution.py:309
  198.6 34.2 %collective-permute-start.11 = (bf16[180,1440]{1,0:T(8,128)(2,1)}, bf16[180,1440]{1,0:T(8,128)(2,1)S(1)}, u32[]{:S(2)}, u32[]{:S(2)}) collective-permute-start(bf16[180,1440]{1,0:T(8,128)(2,1)} %copy-done.12), channel_id=1, source_target_pairs={{0,1},{1,0},{2,3},{3,2},{4,5},{5,4},{6,7},{7,6},{8,9},{9,8},{10,11... | collective-permute-start | bytes 1555208 | tf_op jit(solution)/shard_map/ppermute | solution.py:21
  232.8 1.1 copy-start.3
  233.9 1.1 copy-start.5
  234.9 1.0 copy-start.7
  235.9 1.0 copy-start.8
  236.9 4.0 %copy-start.16 = (s32[128,4]{0,1:T(4,128)S(1)}, s32[128,4]{0,1:T(4,128)}, u32[]{:S(2)}) copy-start(s32[128,4]{0,1:T(4,128)} %param.8) | copy-start | bytes 6148
  236.9 4.0 %copy-start.18 = (f32[128,4]{0,1:T(4,128)S(1)}, f32[128,4]{0,1:T(4,128)}, u32[]{:S(2)}) copy-start(f32[128,4]{0,1:T(4,128)} %param.9) | copy-start | bytes 6148

commit v3 on v0

v3 whole, which is shorter than its diff:
```python
import jax
import jax.numpy as jnp
from jax import lax
from jax.experimental import pallas as pl
from jax.experimental.pallas import tpu as pltpu
from jax.sharding import PartitionSpec as P

swish_alpha = 1.702
low = jnp.bfloat16
full = jnp.float32
HALF = 64
SLOTS = 5
QUARTER = 360
STRIDE = 384
PIECE = 512
PIECES = 3
CHUNK = 16
GROUP = 16
PEER = 256


def exchanged(block, axis, distance):
    count = lax.axis_size(axis)
    return lax.ppermute(block, axis, [(i, i ^ distance) for i in range(count)])


def contract(left, right, left_dim, right_dim):
    return lax.dot_general(
        left, right, (((left_dim,), (right_dim,)), ((), ())), preferred_element_type=full
    )


def iota(shape, dim):
    return lax.broadcasted_iota(jnp.int32, shape, dim)


def ones_at(mask):
    return jnp.where(mask, 1.0, 0.0)


def placed(block, ids, gates, experts):
    ids = jnp.where(block == 0, ids[:, :HALF], ids[:, HALF:])
    gates = jnp.where(block == 0, gates[:, :HALF], gates[:, HALF:])
    named = jnp.zeros((experts, HALF), full)
    gate = jnp.zeros((experts, HALF), full)
    for k in range(ids.shape[0]):
        hit = ids[k : k + 1, :] == iota((experts, HALF), 0)
        named = named + jnp.where(hit, 1.0, 0.0)
        gate = gate + jnp.where(hit, gates[k : k + 1, :], 0.0)
    before = ones_at(iota((HALF, HALF), 0) < iota((HALF, HALF), 1)).astype(low)
    number = jnp.where(named > 0.0, contract(named.astype(low), before, 1, 0) + 1.0, 0.0)

    def spread(part):
        return jnp.broadcast_to(part[:, None, :], (experts, CHUNK, HALF)).reshape(
            experts * CHUNK, HALF
        )

    number, gate = spread(number), spread(gate)
    row = iota(number.shape, 0) % CHUNK
    slot = (row // PIECES).astype(full) + 1.0
    here = number == slot
    masks = [here & (row % PIECES == m) & (row < SLOTS * PIECES) for m in range(PIECES)]
    return masks, gate


def pack_kernel(block_ref, ids_ref, gates_ref, own_ref, got_ref, raw_ref, x_ref):
    block = block_ref[0]
    x_ref[...] = jnp.zeros_like(x_ref)
    for mine in range(2):

        @pl.when(block == mine)
        def _():
            for quarter, rows in ((mine, own_ref), (1 - mine, got_ref)):
                tok = STRIDE * quarter
                grad = STRIDE * (2 + quarter)
                x_ref[:, tok : tok + QUARTER] = rows[:, :QUARTER]
                x_ref[:, grad : grad + QUARTER] = rows[:, QUARTER:]

    masks, gate = placed(block, ids_ref[...], gates_ref[...], raw_ref.shape[0] // CHUNK)
    parts = [ones_at(mask) for mask in masks]
    slot_gate = jnp.sum((parts[0] + parts[1] + parts[2]) * gate, axis=1, keepdims=True)
    piece = (iota(slot_gate.shape, 0) % CHUNK) % PIECES
    result = sum(
        contract(parts[m].astype(low), x_ref[:, m * PIECE : (m + 1) * PIECE], 1, 0)
        for m in range(PIECES)
    )
    early = jnp.where(piece == 2, slot_gate, 1.0)
    late = jnp.where(piece >= 1, slot_gate, 1.0)
    raw_ref[:, :256] = (result[:, :256] * early).astype(low)
    raw_ref[:, 256:] = (result[:, 256:] * late).astype(low)


def small_params(size=32):
    return pltpu.CompilerParams(vmem_limit_bytes=size << 20)


def in_vmem(count):
    return [pl.BlockSpec(memory_space=pltpu.VMEM)] * count


def scalar():
    return pl.BlockSpec(memory_space=pltpu.SMEM)


def pack(block, ids, gates, own, got, rows):
    return pl.pallas_call(
        pack_kernel,
        in_specs=[scalar()] + in_vmem(4),
        out_specs=in_vmem(1)[0],
        out_shape=jax.ShapeDtypeStruct((rows, PIECE), low),
        scratch_shapes=[pltpu.VMEM((HALF, PIECE * PIECES), low)],
        compiler_params=small_params(),
        cost_estimate=pl.CostEstimate(
            flops=6 * rows * 128 * 512, bytes_accessed=2 * rows * 512, transcendentals=0
        ),
    )(block, ids, gates, own, got)


def combine_kernel(block_ref, ids_ref, gates_ref, raw_ref, keep_ref, send_ref, dense):
    block = block_ref[0]
    masks, gate = placed(block, ids_ref[...], gates_ref[...], raw_ref.shape[0] // CHUNK)
    plain = [ones_at(mask).astype(low) for mask in masks]
    high, rest = [], []
    for m in range(2):
        weight = jnp.where(masks[m], gate, 0.0)
        high.append(weight.astype(low))
        rest.append((weight - high[m].astype(full)).astype(low))
    dense[:, 0:512] = contract(high[0], raw_ref[...], 0, 0) + contract(rest[0], raw_ref[...], 0, 0)
    dense[:, 512:768] = contract(high[1], raw_ref[:, :256], 0, 0) + contract(
        rest[1], raw_ref[:, :256], 0, 0
    )
    dense[:, 768:1024] = contract(plain[1], raw_ref[:, 256:], 0, 0)
    dense[:, 1024:1536] = contract(plain[2], raw_ref[...], 0, 0)
    for mine in range(2):

        @pl.when(block == mine)
        def _():
            for quarter, rows in ((mine, keep_ref), (1 - mine, send_ref)):
                out = STRIDE * quarter
                inner = STRIDE * (2 + quarter)
                rows[:, :QUARTER] = dense[:, out : out + QUARTER].astype(low)
                rows[:, QUARTER:] = dense[:, inner : inner + QUARTER].astype(low)


def combine(block, ids, gates, raw):
    return pl.pallas_call(
        combine_kernel,
        in_specs=[scalar()] + in_vmem(3),
        out_specs=in_vmem(2),
        out_shape=[jax.ShapeDtypeStruct((HALF, 2 * QUARTER), low)] * 2,
        scratch_shapes=[pltpu.VMEM((HALF, PIECE * PIECES), full)],
        compiler_params=small_params(),
        cost_estimate=pl.CostEstimate(
            flops=8 * raw.shape[0] * 128 * 512,
            bytes_accessed=2 * raw.shape[0] * 512,
            transcendentals=0,
        ),
    )(block, ids, gates, raw)


def selection():
    shape = (PIECES * GROUP * SLOTS, GROUP * CHUNK)
    dense, raw = iota(shape, 0), iota(shape, 1)
    piece, row = dense // (GROUP * SLOTS), dense % (GROUP * SLOTS)
    hit = (row // SLOTS == raw // CHUNK) & (raw % CHUNK == PIECES * (row % SLOTS) + piece)
    return ones_at(hit).astype(low)


def expert_kernel(
    core_ref, mine_ref, other_ref, w_ref,
    keep_ref, send_ref, tok_ref, grad_ref, hid_ref, both_ref,
    dense, out_rows, in_rows,
):
    core = core_ref[0]
    chosen = selection()
    many, wide = GROUP * SLOTS, GROUP * CHUNK
    groups = mine_ref.shape[0] // wide
    for source, raw_ref in enumerate((mine_ref, other_ref)):
        for g in range(groups):
            found = contract(chosen, raw_ref[g * wide : (g + 1) * wide, :], 1, 0).astype(low)
            for m in range(PIECES):
                dense[
                    source, g * many : (g + 1) * many, m * PIECE : (m + 1) * PIECE
                ] = found[m * many : (m + 1) * many]
    for mine in range(2):

        @pl.when(core == mine)
        def _():
            for source in range(2):
                for pair in range(2):
                    start = QUARTER * (2 * pair + (mine ^ source))
                    tok, grad = STRIDE * pair, STRIDE * (2 + pair)
                    tok_ref[:, start : start + QUARTER] = dense[source, :, tok : tok + QUARTER]
                    grad_ref[:, start : start + QUARTER] = dense[source, :, grad : grad + QUARTER]

    tok = tok_ref[...]
    pre_gate = contract(tok, w_ref[0], 1, 1)
    pre_up = contract(tok, w_ref[1], 1, 1)
    grad_hidden = contract(grad_ref[...], w_ref[2], 1, 1)
    hidden_wide = pre_gate.shape[1]
    sig = jax.nn.sigmoid(swish_alpha * pre_gate)
    swish = pre_gate * sig
    hid_ref[...] = ((pre_up + 1.0) * swish).astype(low)
    both_ref[:, hidden_wide:] = (grad_hidden * swish).astype(low)
    slope = sig + swish_alpha * swish * (1.0 - sig)
    both_ref[:, :hidden_wide] = (grad_hidden * (pre_up + 1.0) * slope).astype(low)
    out_rows[...] = contract(hid_ref[...], w_ref[2], 1, 0).astype(low)
    in_rows[...] = contract(
        both_ref[...], w_ref[0:2].reshape(2 * hidden_wide, w_ref.shape[2]), 1, 0
    ).astype(low)
    for mine in range(2):

        @pl.when(core == mine)
        def _():
            for source in range(2):
                for pair in range(2):
                    start = QUARTER * (2 * pair + (mine ^ source))
                    out, inner = STRIDE * pair, STRIDE * (2 + pair)
                    dense[source, :, out : out + QUARTER] = out_rows[:, start : start + QUARTER]
                    dense[source, :, inner : inner + QUARTER] = in_rows[:, start : start + QUARTER]

    for source, raw_ref in enumerate((keep_ref, send_ref)):
        for g in range(groups):
            at = slice(g * many, (g + 1) * many)
            block = jnp.concatenate(
                [dense[source, at, m * PIECE : (m + 1) * PIECE] for m in range(PIECES)], axis=0
            )
            raw_ref[g * wide : (g + 1) * wide, :] = contract(chosen, block, 0, 0).astype(low)


def expert(core, mine, other, weights):
    raw_rows = mine.shape[0]
    count = raw_rows // CHUNK * SLOTS
    hidden, width = weights.shape[1:]
    shape = lambda cols: jax.ShapeDtypeStruct((count, cols), low)
    return pl.pallas_call(
        expert_kernel,
        in_specs=[scalar()] + in_vmem(3),
        out_specs=in_vmem(6),
        out_shape=[jax.ShapeDtypeStruct((raw_rows, PIECE), low)] * 2
        + [shape(width)] * 2
        + [shape(hidden), shape(2 * hidden)],
        scratch_shapes=[pltpu.VMEM((2, count, PIECE * PIECES), low)]
        + [pltpu.VMEM((count, width), low)] * 2,
        compiler_params=small_params(56),
        cost_estimate=pl.CostEstimate(
            flops=12 * count * width * hidden,
            bytes_accessed=16 * count * width,
            transcendentals=count * hidden,
        ),
    )(core, mine, other, weights)


def weight_products(refs, lanes):
    (hid_a, both_a, tok_a, grad_a), (hid_b, both_b, tok_b, grad_b) = refs
    hidden_wide = hid_a.shape[1]
    for pair, rows, at in (
        ((both_a, both_b), (tok_a, tok_b), lanes),
        (
            (both_a, both_b),
            (tok_a, tok_b),
            slice(hidden_wide + lanes.start, hidden_wide + lanes.stop),
        ),
        ((hid_a, hid_b), (grad_a, grad_b), lanes),
    ):
        yield contract(pair[0][:, at], rows[0][...], 0, 0) + contract(
            pair[1][:, at], rows[1][...], 0, 0
        )


def peer_kernel(*refs):
    first, second, out_ref = refs[0:4], refs[4:8], refs[8]
    size = out_ref.shape[1]
    for number, part in enumerate(weight_products((first, second), slice(PEER, PEER + size))):
        out_ref[number] = part.astype(low)


def own_kernel(*refs):
    first, second, got_ref, outs = refs[0:4], refs[4:8], refs[8], refs[9:12]
    size = got_ref.shape[1]
    for number, part in enumerate(weight_products((first, second), slice(0, size))):
        outs[number][...] = (part + got_ref[number].astype(full)).astype(low)


def weight_grads(kernel, first, second, hidden, width, got=()):
    shape = lambda *lead: jax.ShapeDtypeStruct((*lead, hidden, width), low)
    outs = [shape()] * 3 if got else shape(3)
    return pl.pallas_call(
        kernel,
        in_specs=in_vmem(8 + len(got)),
        out_specs=in_vmem(3) if got else in_vmem(1)[0],
        out_shape=outs,
        compiler_params=small_params(48),
        cost_estimate=pl.CostEstimate(
            flops=12 * first[2].shape[0] * width * hidden,
            bytes_accessed=16 * first[2].shape[0] * width,
            transcendentals=0,
        ),
    )(*first, *second, *got)


def by_parity(rows, exp_count):
    groups = [list(range(parity, exp_count, 2)) for parity in range(2)]
    chunks = rows.reshape(exp_count // 2, CHUNK, PIECE)
    return lax.all_to_all(
        chunks, "exp", split_axis=0, concat_axis=0, axis_index_groups=groups, tiled=True
    ).reshape(rows.shape)


def local(tokens, expert_ids, gate_values, out_grad, gate_weight, up_weight, down_weight):
    exp_count = lax.axis_size("exp")
    rep = lax.axis_index("rep").astype(jnp.int32)
    block, core = (rep // 2).reshape(1), (rep % 2).reshape(1)
    raw_rows = exp_count // 2 * CHUNK
    hidden, width = gate_weight.shape[1:]
    ids, gates = expert_ids.T, gate_values.T
    first = rep < 2

    lower = jnp.concatenate([tokens[:HALF], out_grad[:HALF]], axis=1)
    upper = jnp.concatenate([tokens[HALF:], out_grad[HALF:]], axis=1)
    away = jnp.where(first, upper, lower)
    away, gate_weight, up_weight, down_weight = lax.optimization_barrier(
        (away, gate_weight, up_weight, down_weight)
    )
    got_rows = exchanged(away, "rep", 2)
    peer_gate, peer_up, peer_down = [
        exchanged(w, "rep", 2) for w in (gate_weight, up_weight, down_weight)
    ]
    packed = pack(block, ids, gates, jnp.where(first, lower, upper), got_rows, raw_rows)
    mine = by_parity(packed, exp_count)
    mine, peer_gate, peer_up = lax.optimization_barrier((mine, peer_gate, peer_up))
    next_mine = exchanged(mine, "exp", 1)
    beside = exchanged(mine, "rep", 1)
    gap = jnp.zeros((PEER - hidden, width), low)
    weights = jnp.stack(
        [
            jnp.concatenate([own[0], gap, peer[0], gap], axis=0)
            for own, peer in (
                (gate_weight, peer_gate),
                (up_weight, peer_up),
                (down_weight, peer_down),
            )
        ]
    )
    keep_a, send_a, tok_a, grad_a, hid_a, both_a = expert(core, mine, beside, weights)
    got_a = exchanged(send_a, "rep", 1)
    next_mine, got_a = lax.optimization_barrier((next_mine, got_a))
    next_beside = exchanged(next_mine, "rep", 1)
    keep_b, send_b, tok_b, grad_b, hid_b, both_b = expert(core, next_mine, next_beside, weights)
    got_b = exchanged(send_b, "rep", 1)
    sum_b = (keep_b.astype(full) + got_b.astype(full)).astype(low)
    sum_b, hid_b, both_b = lax.optimization_barrier((sum_b, hid_b, both_b))
    got_sum = exchanged(sum_b, "exp", 1)
    rows_a, rows_b = (hid_a, both_a, tok_a, grad_a), (hid_b, both_b, tok_b, grad_b)
    peers = weight_grads(peer_kernel, rows_a, rows_b, hidden, width)
    got_peers = exchanged(peers, "rep", 2)
    total = (
        keep_a.astype(full) + got_a.astype(full) + got_sum.astype(full)
    ).astype(low)
    returned = by_parity(total, exp_count)
    gate_grad, up_grad, down_grad = weight_grads(
        own_kernel, rows_a, rows_b, hidden, width, (got_peers,)
    )
    returned, gate_grad, up_grad, down_grad = lax.optimization_barrier(
        (returned, gate_grad, up_grad, down_grad)
    )
    kept, sent = combine(block, ids, gates, returned)
    got = exchanged(sent, "rep", 2)
    result = jnp.where(
        first, jnp.concatenate([kept, got], axis=0), jnp.concatenate([got, kept], axis=0)
    )
    layer_out, input_grad = result[:, :QUARTER], result[:, QUARTER:]
    return (layer_out, input_grad, gate_grad[None], up_grad[None], down_grad[None])


def solution(mesh):
    in_specs = (
        P("exp", "rep"),
        P("exp", None),
        P("exp", None),
        P("exp", "rep"),
        P("exp", "rep", None),
        P("exp", "rep", None),
        P("exp", "rep", None),
    )
    out_specs = (
        P("exp", "rep"),
        P("exp", "rep"),
        P("exp", "rep", None),
        P("exp", "rep", None),
        P("exp", "rep", None),
    )
    return jax.shard_map(local, mesh=mesh, in_specs=in_specs, out_specs=out_specs, check_vma=False)
```

time: 393 us -> 243 us (0.62)
  waiting for transfers between devices: 194 us -> 114 us
  matrix products: 34.9 us -> 0 us
  Pallas kernels: 0 us -> 34.5 us
  local copies, waits for them, and re-layouts: 41 us -> 12.2 us
  blocking collectives: 25 us -> 0 us
  between operations: 14.4 us -> 0.97 us
  other arithmetic: 14 us -> 7.79 us
  starting transfers between devices: 66.6 us -> 71.8 us
    unnamed x4 -> x0, waiting for transfers between devices: 57 us -> none
    all_to_all x4 -> x2, waiting for transfers between devices: 56.3 us -> 0.01 us  [by_parity(): lax.all_to_all(chunks, 'exp', split_axis=0, concat_axis=0, axis_index_gro...]
    dot_general x13 -> x0, matrix products: 34.9 us -> none  [the longest x5 17.4 us: matmul(): return jnp.dot(left, right, preferred_element_type=jnp.float32)]
    pallas_call x0 -> x6, Pallas kernels: none -> 34.5 us  [the longest x2 21.6 us: expert(): pl.pallas_call(expert_kernel, in_specs=[scalar()] + in_vmem(3), out_specs...]
    ppermute x6 -> x12, waiting for transfers between devices: 81.1 us -> 114 us  [exchanged(): return lax.ppermute(block, axis, [(i, i ^ distance) for i in range(count)])]
    ppermute x6 -> x12, starting transfers between devices: 15.8 us -> 42.4 us  [exchanged(): return lax.ppermute(block, axis, [(i, i ^ distance) for i in range(count)])]
    all_gather x2 -> x0, blocking collectives: 25 us -> none  [the longest x1 14.5 us: local(): full_tokens = lax.all_gather(tokens, 'rep', axis=1, tiled=True)]
    all_to_all x4 -> x2, starting transfers between devices: 50.8 us -> 29.4 us  [by_parity(): lax.all_to_all(chunks, 'exp', split_axis=0, concat_axis=0, axis_index_gro...]
  transfers between devices with their start and end apart: 12 -> 14, of which waited for: 7 -> 11; matrix products, arithmetic and copies ran while one was open for 17% -> 2% of each run, Pallas kernels for 0% -> 8%
where the time goes in v3:
time: 243 us; the launch traced here: 241 us
  waiting for transfers between devices  114 us (47%)
  starting transfers between devices  71.8 us (30%)
  Pallas kernels  34.5 us (14%)
  local copies, waits for them, and re-layouts  12.2 us (5%)
  other arithmetic  7.79 us (3%)
    ppermute x12, waiting for transfers between devices, exchanged(): return lax.ppermute(block, axis, [(i, i ^ distance) for i in range(count)])  114 us
    ppermute x12, starting transfers between devices, exchanged(): return lax.ppermute(block, axis, [(i, i ^ distance) for i in range(count)])  42.4 us
    all_to_all x2, starting transfers between devices, by_parity(): lax.all_to_all(chunks, 'exp', split_axis=0, concat_axis=0, axis_index_gro...  29.4 us
    pallas_call x2, Pallas kernels, expert(): pl.pallas_call(expert_kernel, in_specs=[scalar()] + in_vmem(3), out_specs...  21.6 us
    unnamed x46, local copies, waits for them, and re-layouts  9.87 us
    pallas_call x2, Pallas kernels, weight_grads(): pl.pallas_call(kernel, in_specs=in_vmem(8 + len(got)), out_specs=in_vmem(...  7.52 us
  transfers between devices with their start and end apart: 14, of which 11 were waited for; matrix products, arithmetic and copies ran while one was open for 2% of the time, Pallas kernels for 8%

profile of v3, /device:TPU:1, one launch (start us, length us, event | category | flops | bytes accessed | tf_op | source)
XLA Modules:
  0.0 241.3 jit_solution(5639009591034553166)
XLA Ops:
  0.6 0.0 copy-start.17
  0.6 1.1 fusion.7
  1.7 0.1 copy.18
  1.8 0.0 copy-start.16
  1.9 0.1 copy.20
  2.0 1.1 fusion.8
  3.0 0.1 copy.19
  3.2 0.0 copy-start.15
  3.2 0.1 copy.21
  3.3 0.1 broadcast_select_fusion
  3.4 5.5 %collective-permute-start = (bf16[64,720]{1,0:T(8,128)(2,1)S(1)}, bf16[64,720]{1,0:T(8,128)(2,1)S(1)}, u32[]{:S(2)}, u32[]{:S(2)}) collective-permute-start(bf16[64,720]{1,0:T(8,128)(2,1)S(1)} %get-tuple-element.38), channel_id=1, source_target_pairs={{0,256},{128,384},{256,0},{384,128},{1,257},{129,385},{257,1},{385... | collective-permute-start | bytes 276488 | tf_op jit(solution)/shard_map/ppermute | solution.py:24
  8.9 2.0 collective-permute-done.got_ref
  10.9 0.7 copy-done.8
  11.6 0.7 copy-done.10
  12.2 2.7 %shard_map.110 = bf16[1024,512]{1,0:T(8,128)(2,1)} custom-call(s32[1]{0:T(128)} %bitcast.block_ref, s32[4,128]{1,0:T(4,128)S(1)} %bitcast.23, f32[4,128]{1,0:T(4,128)S(1)} %bitcast.25, bf16[64,720]{1,0:T(8,128)(2,1)S(1)} %get-tuple-element.82.own_ref, bf16[64,720]{1,0:T(8,128)(2,1)S(1)} %collective-permute-done.got_ref), custom_call_target="tpu_custom_call" | custom-call | flops 402653184 | bytes 1048576 | tf_op jit(solution)/shard_map/pallas_call | solution.py:106
  14.9 17.4 %all-to-all-start = ((bf16[64,16,512]{2,1,0:T(8,128)(2,1)}), bf16[64,16,512]{2,1,0:T(8,128)(2,1)S(1)}, u32[]{:S(2)}, u32[]{:S(2)}) async-start(bf16[64,16,512]{2,1,0:T(8,128)(2,1)} %bitcast.4), calls=%async_computation | async-start | bytes 2097152 | tf_op jit(solution)/shard_map/all_to_all | solution.py:305
  32.4 0.0 copy-done.15
  32.4 4.4 %collective-permute-start.1 = (bf16[1,180,1440]{2,1,0:T(8,128)(2,1)S(1)}, bf16[1,180,1440]{2,1,0:T(8,128)(2,1)S(1)}, u32[]{:S(2)}, u32[]{:S(2)}) collective-permute-start(bf16[1,180,1440]{2,1,0:T(8,128)(2,1)S(1)} %copy-done.15), channel_id=1, source_target_pairs={{0,256},{128,384},{256,0},{384,128},{1,257},{129,385},{257,1},{385... | collective-permute-start | bytes 1555208 | tf_op jit(solution)/shard_map/ppermute | solution.py:24
  36.7 0.0 copy-done.17
  36.8 2.4 %collective-permute-start.2 = (bf16[1,180,1440]{2,1,0:T(8,128)(2,1)S(1)}, bf16[1,180,1440]{2,1,0:T(8,128)(2,1)}, u32[]{:S(2)}, u32[]{:S(2)}) collective-permute-start(bf16[1,180,1440]{2,1,0:T(8,128)(2,1)S(1)} %copy-done.17), channel_id=1, source_target_pairs={{0,256},{128,384},{256,0},{384,128},{1,257},{129,385},{257,1},{385... | collective-permute-start | bytes 1555208 | tf_op jit(solution)/shard_map/ppermute | solution.py:24
  39.2 0.0 copy-done.16
  39.2 4.4 %collective-permute-start.4 = (bf16[1,180,1440]{2,1,0:T(8,128)(2,1)S(1)}, bf16[1,180,1440]{2,1,0:T(8,128)(2,1)}, u32[]{:S(2)}, u32[]{:S(2)}) collective-permute-start(bf16[1,180,1440]{2,1,0:T(8,128)(2,1)S(1)} %copy-done.16), channel_id=1, source_target_pairs={{0,256},{128,384},{256,0},{384,128},{1,257},{129,385},{257,1},{385... | collective-permute-start | bytes 1555208 | tf_op jit(solution)/shard_map/ppermute | solution.py:24
  43.6 11.3 %collective-permute-done.1 = bf16[1,180,1440]{2,1,0:T(8,128)(2,1)S(1)} collective-permute-done((bf16[1,180,1440]{2,1,0:T(8,128)(2,1)S(1)}, bf16[1,180,1440]{2,1,0:T(8,128)(2,1)S(1)}, u32[]{:S(2)}, u32[]{:S(2)}) %collective-permute-start.1) | collective-permute-done | bytes 518432 | tf_op jit(solution)/shard_map/ppermute | solution.py:24
  54.8 17.3 %collective-permute-done.2 = bf16[1,180,1440]{2,1,0:T(8,128)(2,1)} collective-permute-done((bf16[1,180,1440]{2,1,0:T(8,128)(2,1)S(1)}, bf16[1,180,1440]{2,1,0:T(8,128)(2,1)}, u32[]{:S(2)}, u32[]{:S(2)}) %collective-permute-start.2) | collective-permute-done | bytes 518432 | tf_op jit(solution)/shard_map/ppermute | solution.py:24
  72.1 0.0 all-to-all-done
  72.1 5.1 %collective-permute-start.3 = (bf16[1024,512]{1,0:T(8,128)(2,1)S(1)}, bf16[1024,512]{1,0:T(8,128)(2,1)}, u32[]{:S(2)}, u32[]{:S(2)}) collective-permute-start(bf16[1024,512]{1,0:T(8,128)(2,1)S(1)} %bitcast.28), channel_id=1, source_target_pairs={{0,128},{128,0},{256,384},{384,256},{1,129},{129,1},{257,385},{385... | collective-permute-start | bytes 3145736 | tf_op jit(solution)/shard_map/ppermute | solution.py:24
  77.2 2.5 %collective-permute-start.5 = (bf16[1024,512]{1,0:T(8,128)(2,1)S(1)}, bf16[1024,512]{1,0:T(8,128)(2,1)S(1)}, u32[]{:S(2)}, u32[]{:S(2)}) collective-permute-start(bf16[1024,512]{1,0:T(8,128)(2,1)S(1)} %bitcast.29), channel_id=1, source_target_pairs={{0,1},{1,0},{2,3},{3,2},{4,5},{5,4},{6,7},{7,6},{8,9},{9,8},{10,11... | collective-permute-start | bytes 3145736 | tf_op jit(solution)/shard_map/ppermute | solution.py:24
  79.7 4.5 %collective-permute-done.4 = bf16[1,180,1440]{2,1,0:T(8,128)(2,1)} collective-permute-done((bf16[1,180,1440]{2,1,0:T(8,128)(2,1)S(1)}, bf16[1,180,1440]{2,1,0:T(8,128)(2,1)}, u32[]{:S(2)}, u32[]{:S(2)}) %collective-permute-start.4) | collective-permute-done | bytes 518432 | tf_op jit(solution)/shard_map/ppermute | solution.py:24
  84.2 2.2 fusion.3
  86.5 0.0 copy-done.13
  86.5 2.5 %pad_maximum_fusion.w_ref = bf16[3,512,1440]{2,1,0:T(8,128)(2,1)} fusion(bf16[1,512,1440]{2,1,0:T(8,128)(2,1)S(1)} %get-tuple-element.77, bf16[1,512,1440]{2,1,0:T(8,128)(2,1)S(1)} %get-tuple-element.78, bf16[1,512,1440]{2,1,0:T(8,128)(2,1)S(1)} %get-tuple-element.76), kind=kLoop, calls=%fused_computation | loop fusion | flops 4423680 | bytes 8847360 | tf_op jit(solution)/shard_map/stack | solution.py:335
  88.9 0.0 collective-permute-done.3.other_ref
  88.9 10.7 %shard_map.111 = (bf16[1024,512]{1,0:T(8,128)(2,1)}, bf16[1024,512]{1,0:T(8,128)(2,1)}, bf16[320,1440]{1,0:T(8,128)(2,1)}, bf16[320,1440]{1,0:T(8,128)(2,1)}, bf...) custom-call(s32[1]{0:T(128)} %bitcast.3.core_ref, bf16[1024,512]{1,0:T(8,128)(2,1)} %bitcast.30, ...), custom_call_target="tpu_custom_call" | custom-call | flops 2831155200 | bytes 7372800 | tf_op jit(solution)/shard_map/pallas_call | solution.py:236
  99.7 3.6 %collective-permute-start.6 = (bf16[1024,512]{1,0:T(8,128)(2,1)}, bf16[1024,512]{1,0:T(8,128)(2,1)S(1)}, u32[]{:S(2)}, u32[]{:S(2)}) collective-permute-start(bf16[1024,512]{1,0:T(8,128)(2,1)} %get-tuple-element.46), channel_id=1, source_target_pairs={{0,128},{128,0},{256,384},{384,256},{1,129},{129,1},{257,385},{385... | collective-permute-start | bytes 3145736 | tf_op jit(solution)/shard_map/ppermute | solution.py:24
  103.3 0.6 collective-permute-done.5.mine_ref
  103.9 1.9 collective-permute-done.6
  105.8 2.3 collective-permute-start.7
  108.1 2.3 collective-permute-done.7.other_ref
  110.3 1.0 copy-done.19
  111.3 10.9 %shard_map.112 = (bf16[1024,512]{1,0:T(8,128)(2,1)}, bf16[1024,512]{1,0:T(8,128)(2,1)}, bf16[320,1440]{1,0:T(8,128)(2,1)}, bf16[320,1440]{1,0:T(8,128)(2,1)}, bf...) custom-call(s32[1]{0:T(128)} %bitcast.3.core_ref, bf16[1024,512]{1,0:T(8,128)(2,1)} %copy-done.18, ...), custom_call_target="tpu_custom_call" | custom-call | flops 2831155200 | bytes 7372800 | tf_op jit(solution)/shard_map/pallas_call | solution.py:236
  122.2 2.4 collective-permute-start.8
  124.6 2.5 %collective-permute-done.8 = bf16[1024,512]{1,0:T(8,128)(2,1)S(1)} collective-permute-done((bf16[1024,512]{1,0:T(8,128)(2,1)}, bf16[1024,512]{1,0:T(8,128)(2,1)S(1)}, u32[]{:S(2)}, u32[]{:S(2)}) %collective-permute-start.8) | collective-permute-done | bytes 1048608 | tf_op jit(solution)/shard_map/ppermute | solution.py:24
  127.1 1.5 add_convert_fusion.1
  128.7 2.3 collective-permute-start.9
  131.0 24.0 %collective-permute-done.9 = bf16[1024,512]{1,0:T(8,128)(2,1)S(1)} collective-permute-done((bf16[1024,512]{1,0:T(8,128)(2,1)S(1)}, bf16[1024,512]{1,0:T(8,128)(2,1)S(1)}, u32[]{:S(2)}, u32[]{:S(2)}) %collective-permute-start.9) | collective-permute-done | bytes 1048608 | tf_op jit(solution)/shard_map/ppermute | solution.py:24
  155.0 1.4 add_convert_fusion
  156.4 11.9 %all-to-all-start.1 = ((bf16[64,16,512]{2,1,0:T(8,128)(2,1)}), bf16[64,16,512]{2,1,0:T(8,128)(2,1)}, u32[]{:S(2)}, u32[]{:S(2)}) async-start(bf16[64,16,512]{2,1,0:T(8,128)(2,1)} %bitcast.27), calls=%async_computation.1 | async-start | bytes 2097152 | tf_op jit(solution)/shard_map/all_to_all | solution.py:305
  168.4 1.2 copy-done.3
  169.6 1.1 copy-done.4
  170.7 1.1 copy-done.5
  171.8 1.0 copy-done.7
  172.8 3.2 %shard_map.113 = bf16[3,180,1440]{2,1,0:T(8,128)(2,1)} custom-call(bf16[320,512]{1,0:T(8,128)(2,1)S(1)} %copy-done.6, bf16[320,1024]{1,0:T(8,128)(2,1)S(1)} %copy-done.4, bf16[320,1440]{1,0:T(8,128)(2,1)S(1)} %copy-done, bf16[320,1440]{1,0:T(8,128)(2,1)S(1)} %copy-done.1, bf16[320,512]{1,0:T(8,128)(2,1)S(1)} %copy-done.7, bf16[320,1024]{1,0:T(8,128)(2,1)S(1)} %copy-done.5, ...), custom_call_target="tpu_custom_call" | custom-call | flops 995328000 | bytes 7372800 | tf_op jit(solution)/shard_map/pallas_call | solution.py:288
  176.0 4.3 %collective-permute-start.10 = (bf16[3,180,1440]{2,1,0:T(8,128)(2,1)}, bf16[3,180,1440]{2,1,0:T(8,128)(2,1)S(1)}, u32[]{:S(2)}, u32[]{:S(2)}) collective-permute-start(bf16[3,180,1440]{2,1,0:T(8,128)(2,1)} %shard_map.113), channel_id=1, source_target_pairs={{0,256},{128,384},{256,0},{384,128},{1,257},{129,385},{257,1},{385... | collective-permute-start | bytes 4665608 | tf_op jit(solution)/shard_map/ppermute | solution.py:24
  180.3 44.3 %collective-permute-done.10.refs_8_ = bf16[3,180,1440]{2,1,0:T(8,128)(2,1)S(1)} collective-permute-done((bf16[3,180,1440]{2,1,0:T(8,128)(2,1)}, bf16[3,180,1440]{2,1,0:T(8,128)(2,1)S(1)}, u32[]{:S(2)}, u32[]{:S(2)}) %collective-permute-start.10) | collective-permute-done | bytes 1555232 | tf_op jit(solution)/shard_map/ppermute | solution.py:24
  224.6 1.2 copy-done.12
  225.8 4.3 %shard_map.114 = (bf16[180,1440]{1,0:T(8,128)(2,1)}, bf16[180,1440]{1,0:T(8,128)(2,1)}, bf16[180,1440]{1,0:T(8,128)(2,1)}) custom-call(bf16[320,512]{1,0:T(8,128)(2,1)S(1)} %copy-done.6, bf16[320,1024]{1,0:T(8,128)(2,1)S(1)} %copy-done.4, bf16[320,1440]{1,0:T(8,128)(2,1)S(1)} %copy-done, bf16[320,1440]{1,0:T(8,128)(2,1)S(1)} %copy-done.1, ...), custom_call_target="tpu_custom_call" | custom-call | flops 995328000 | bytes 7372800 | tf_op jit(solution)/shard_map/pallas_call | solution.py:288
  230.1 0.0 all-to-all-done.1
  230.1 0.0 copy-done.11
  230.1 2.7 %shard_map.115 = (bf16[64,720]{1,0:T(8,128)(2,1)S(1)}, bf16[64,720]{1,0:T(8,128)(2,1)S(1)}) custom-call(s32[1]{0:T(128)} %bitcast.block_ref, s32[4,128]{1,0:T(4,128)S(1)} %bitcast.24, f32[4,128]{1,0:T(4,128)S(1)} %bitcast.26, bf16[1024,512]{1,0:T(8,128)(2,1)} %bitcast.16.raw_ref), custom_call_target="tpu_custom_call" | custom-call | flops 536870912 | bytes 1048576 | tf_op jit(solution)/shard_map/pallas_call | solution.py:146
  232.8 3.3 %collective-permute-start.11 = (bf16[64,720]{1,0:T(8,128)(2,1)S(1)}, bf16[64,720]{1,0:T(8,128)(2,1)S(1)}, u32[]{:S(2)}, u32[]{:S(2)}) collective-permute-start(bf16[64,720]{1,0:T(8,128)(2,1)S(1)} %get-tuple-element.67), channel_id=1, source_target_pairs={{0,256},{128,384},{256,0},{384,128},{1,257},{129,385},{257,1},{385... | collective-permute-start | bytes 276488 | tf_op jit(solution)/shard_map/ppermute | solution.py:24
  236.1 3.6 %collective-permute-done.11 = bf16[64,720]{1,0:T(8,128)(2,1)S(1)} collective-permute-done((bf16[64,720]{1,0:T(8,128)(2,1)S(1)}, bf16[64,720]{1,0:T(8,128)(2,1)S(1)}, u32[]{:S(2)}, u32[]{:S(2)}) %collective-permute-start.11) | collective-permute-done | bytes 92192 | tf_op jit(solution)/shard_map/ppermute | solution.py:24
  239.7 0.1 fusion.6
  239.8 0.7 copy.17
  240.5 0.7 copy.16
  (26 shorter events, 0.1 us)
Async XLA Ops:
  0.6 36.1 %copy-start.17 = (bf16[1,180,1440]{2,1,0:T(8,128)(2,1)S(1)}, bf16[1,180,1440]{2,1,0:T(8,128)(2,1)}, u32[]{:S(2)}) copy-start(bf16[1,180,1440]{2,1,0:T(8,128)(2,1)} %param.12) | copy-start | bytes 1555204
  1.8 37.3 %copy-start.16 = (bf16[1,180,1440]{2,1,0:T(8,128)(2,1)S(1)}, bf16[1,180,1440]{2,1,0:T(8,128)(2,1)}, u32[]{:S(2)}) copy-start(bf16[1,180,1440]{2,1,0:T(8,128)(2,1)} %param.13) | copy-start | bytes 1555204
  3.2 29.2 %copy-start.15 = (bf16[1,180,1440]{2,1,0:T(8,128)(2,1)S(1)}, bf16[1,180,1440]{2,1,0:T(8,128)(2,1)}, u32[]{:S(2)}) copy-start(bf16[1,180,1440]{2,1,0:T(8,128)(2,1)} %param.11) | copy-start | bytes 1555204
  3.4 7.5 %collective-permute-start = (bf16[64,720]{1,0:T(8,128)(2,1)S(1)}, bf16[64,720]{1,0:T(8,128)(2,1)S(1)}, u32[]{:S(2)}, u32[]{:S(2)}) collective-permute-start(bf16[64,720]{1,0:T(8,128)(2,1)S(1)} %get-tuple-element.38), channel_id=1, source_target_pairs={{0,256},{128,384},{256,0},{384,128},{1,257},{129,385},{257,1},{385... | collective-permute-start | bytes 276488 | tf_op jit(solution)/shard_map/ppermute | solution.py:24
  10.9 0.7 copy-start.8
  11.6 0.7 copy-start.10
  14.9 57.2 %all-to-all-start = ((bf16[64,16,512]{2,1,0:T(8,128)(2,1)}), bf16[64,16,512]{2,1,0:T(8,128)(2,1)S(1)}, u32[]{:S(2)}, u32[]{:S(2)}) async-start(bf16[64,16,512]{2,1,0:T(8,128)(2,1)} %bitcast.4), calls=%async_computation | async-start | bytes 2097152 | tf_op jit(solution)/shard_map/all_to_all | solution.py:305
  32.4 22.5 %collective-permute-start.1 = (bf16[1,180,1440]{2,1,0:T(8,128)(2,1)S(1)}, bf16[1,180,1440]{2,1,0:T(8,128)(2,1)S(1)}, u32[]{:S(2)}, u32[]{:S(2)}) collective-permute-start(bf16[1,180,1440]{2,1,0:T(8,128)(2,1)S(1)} %copy-done.15), channel_id=1, source_target_pairs={{0,256},{128,384},{256,0},{384,128},{1,257},{129,385},{257,1},{385... | collective-permute-start | bytes 1555208 | tf_op jit(solution)/shard_map/ppermute | solution.py:24
  36.8 35.3 %collective-permute-start.2 = (bf16[1,180,1440]{2,1,0:T(8,128)(2,1)S(1)}, bf16[1,180,1440]{2,1,0:T(8,128)(2,1)}, u32[]{:S(2)}, u32[]{:S(2)}) collective-permute-start(bf16[1,180,1440]{2,1,0:T(8,128)(2,1)S(1)} %copy-done.17), channel_id=1, source_target_pairs={{0,256},{128,384},{256,0},{384,128},{1,257},{129,385},{257,1},{385... | collective-permute-start | bytes 1555208 | tf_op jit(solution)/shard_map/ppermute | solution.py:24
  39.2 45.0 %collective-permute-start.4 = (bf16[1,180,1440]{2,1,0:T(8,128)(2,1)S(1)}, bf16[1,180,1440]{2,1,0:T(8,128)(2,1)}, u32[]{:S(2)}, u32[]{:S(2)}) collective-permute-start(bf16[1,180,1440]{2,1,0:T(8,128)(2,1)S(1)} %copy-done.16), channel_id=1, source_target_pairs={{0,256},{128,384},{256,0},{384,128},{1,257},{129,385},{257,1},{385... | collective-permute-start | bytes 1555208 | tf_op jit(solution)/shard_map/ppermute | solution.py:24
  72.1 14.4 %copy-start.13 = (bf16[64,16,512]{2,1,0:T(8,128)(2,1)}, bf16[64,16,512]{2,1,0:T(8,128)(2,1)S(1)}, u32[]{:S(2)}) copy-start(bf16[64,16,512]{2,1,0:T(8,128)(2,1)S(1)} %all-to-all-done) | copy-start | bytes 3145732
  72.1 16.8 %collective-permute-start.3 = (bf16[1024,512]{1,0:T(8,128)(2,1)S(1)}, bf16[1024,512]{1,0:T(8,128)(2,1)}, u32[]{:S(2)}, u32[]{:S(2)}) collective-permute-start(bf16[1024,512]{1,0:T(8,128)(2,1)S(1)} %bitcast.28), channel_id=1, source_target_pairs={{0,128},{128,0},{256,384},{384,256},{1,129},{129,1},{257,385},{385... | collective-permute-start | bytes 3145736 | tf_op jit(solution)/shard_map/ppermute | solution.py:24
  77.2 26.7 %collective-permute-start.5 = (bf16[1024,512]{1,0:T(8,128)(2,1)S(1)}, bf16[1024,512]{1,0:T(8,128)(2,1)S(1)}, u32[]{:S(2)}, u32[]{:S(2)}) collective-permute-start(bf16[1024,512]{1,0:T(8,128)(2,1)S(1)} %bitcast.29), channel_id=1, source_target_pairs={{0,1},{1,0},{2,3},{3,2},{4,5},{5,4},{6,7},{7,6},{8,9},{9,8},{10,11... | collective-permute-start | bytes 3145736 | tf_op jit(solution)/shard_map/ppermute | solution.py:24
  99.7 6.1 %collective-permute-start.6 = (bf16[1024,512]{1,0:T(8,128)(2,1)}, bf16[1024,512]{1,0:T(8,128)(2,1)S(1)}, u32[]{:S(2)}, u32[]{:S(2)}) collective-permute-start(bf16[1024,512]{1,0:T(8,128)(2,1)} %get-tuple-element.46), channel_id=1, source_target_pairs={{0,128},{128,0},{256,384},{384,256},{1,129},{129,1},{257,385},{385... | collective-permute-start | bytes 3145736 | tf_op jit(solution)/shard_map/ppermute | solution.py:24
  103.9 6.5 %copy-start.18 = (bf16[1024,512]{1,0:T(8,128)(2,1)}, bf16[1024,512]{1,0:T(8,128)(2,1)S(1)}, u32[]{:S(2)}) copy-start(bf16[1024,512]{1,0:T(8,128)(2,1)S(1)} %collective-permute-done.5.mine_ref) | copy-start | bytes 3145732
  105.8 4.5 %collective-permute-start.7 = (bf16[1024,512]{1,0:T(8,128)(2,1)S(1)}, bf16[1024,512]{1,0:T(8,128)(2,1)S(1)}, u32[]{:S(2)}, u32[]{:S(2)}) collective-permute-start(bf16[1024,512]{1,0:T(8,128)(2,1)S(1)} %collective-permute-done.5.mine_ref), channel_id=1, source_target_pairs={{0,128},{128,0},{256,384},{384,256},{1,129},{129,1},{257,385},{385... | collective-permute-start | bytes 3145736 | tf_op jit(solution)/shard_map/ppermute | solution.py:24
  110.3 1.0 copy-start.19
  122.2 32.7 %copy-start.14 = (bf16[1024,512]{1,0:T(8,128)(2,1)S(1)}, bf16[1024,512]{1,0:T(8,128)(2,1)}, u32[]{:S(2)}) copy-start(bf16[1024,512]{1,0:T(8,128)(2,1)} %get-tuple-element.45) | copy-start | bytes 3145732
  122.2 4.9 %collective-permute-start.8 = (bf16[1024,512]{1,0:T(8,128)(2,1)}, bf16[1024,512]{1,0:T(8,128)(2,1)S(1)}, u32[]{:S(2)}, u32[]{:S(2)}) collective-permute-start(bf16[1024,512]{1,0:T(8,128)(2,1)} %get-tuple-element.50), channel_id=1, source_target_pairs={{0,128},{128,0},{256,384},{384,256},{1,129},{129,1},{257,385},{385... | collective-permute-start | bytes 3145736 | tf_op jit(solution)/shard_map/ppermute | solution.py:24
  128.7 26.3 %collective-permute-start.9 = (bf16[1024,512]{1,0:T(8,128)(2,1)S(1)}, bf16[1024,512]{1,0:T(8,128)(2,1)S(1)}, u32[]{:S(2)}, u32[]{:S(2)}) collective-permute-start(bf16[1024,512]{1,0:T(8,128)(2,1)S(1)} %add_convert_fusion.1), channel_id=1, source_target_pairs={{0,1},{1,0},{2,3},{3,2},{4,5},{5,4},{6,7},{7,6},{8,9},{9,8},{10,11... | collective-permute-start | bytes 3145736 | tf_op jit(solution)/shard_map/ppermute | solution.py:24
  155.0 13.4 %copy-start.2 = (bf16[320,1440]{1,0:T(8,128)(2,1)S(1)}, bf16[320,1440]{1,0:T(8,128)(2,1)}, u32[]{:S(2)}) copy-start(bf16[320,1440]{1,0:T(8,128)(2,1)} %get-tuple-element.60.refs_6_) | copy-start | bytes 2764804
  155.0 13.4 %copy-start.6 = (bf16[320,512]{1,0:T(8,128)(2,1)S(1)}, bf16[320,512]{1,0:T(8,128)(2,1)}, u32[]{:S(2)}) copy-start(bf16[320,512]{1,0:T(8,128)(2,1)} %get-tuple-element.54.refs_0_) | copy-start | bytes 983044
  156.4 12.0 %copy-start = (bf16[320,1440]{1,0:T(8,128)(2,1)S(1)}, bf16[320,1440]{1,0:T(8,128)(2,1)}, u32[]{:S(2)}) copy-start(bf16[320,1440]{1,0:T(8,128)(2,1)} %get-tuple-element.56.refs_2_) | copy-start | bytes 2764804
  156.4 12.0 %copy-start.1 = (bf16[320,1440]{1,0:T(8,128)(2,1)S(1)}, bf16[320,1440]{1,0:T(8,128)(2,1)}, u32[]{:S(2)}) copy-start(bf16[320,1440]{1,0:T(8,128)(2,1)} %get-tuple-element.57.refs_3_) | copy-start | bytes 2764804
  156.4 73.7 %all-to-all-start.1 = ((bf16[64,16,512]{2,1,0:T(8,128)(2,1)}), bf16[64,16,512]{2,1,0:T(8,128)(2,1)}, u32[]{:S(2)}, u32[]{:S(2)}) async-start(bf16[64,16,512]{2,1,0:T(8,128)(2,1)} %bitcast.27), calls=%async_computation.1 | async-start | bytes 2097152 | tf_op jit(solution)/shard_map/all_to_all | solution.py:305
  168.4 1.2 copy-start.3
  169.6 1.1 copy-start.4
  170.7 1.1 copy-start.5
  171.8 1.0 copy-start.7
  176.0 54.1 %copy-start.9 = (s32[128,4]{0,1:T(4,128)S(1)}, s32[128,4]{0,1:T(4,128)}, u32[]{:S(2)}) copy-start(s32[128,4]{0,1:T(4,128)} %param.8) | copy-start | bytes 6148
  176.0 54.1 %copy-start.11 = (f32[128,4]{0,1:T(4,128)S(1)}, f32[128,4]{0,1:T(4,128)}, u32[]{:S(2)}) copy-start(f32[128,4]{0,1:T(4,128)} %param.9) | copy-start | bytes 6148
  176.0 48.6 %collective-permute-start.10 = (bf16[3,180,1440]{2,1,0:T(8,128)(2,1)}, bf16[3,180,1440]{2,1,0:T(8,128)(2,1)S(1)}, u32[]{:S(2)}, u32[]{:S(2)}) collective-permute-start(bf16[3,180,1440]{2,1,0:T(8,128)(2,1)} %shard_map.113), channel_id=1, source_target_pairs={{0,256},{128,384},{256,0},{384,128},{1,257},{129,385},{257,1},{385... | collective-permute-start | bytes 4665608 | tf_op jit(solution)/shard_map/ppermute | solution.py:24
  224.6 1.2 copy-start.12
  232.8 6.9 %collective-permute-start.11 = (bf16[64,720]{1,0:T(8,128)(2,1)S(1)}, bf16[64,720]{1,0:T(8,128)(2,1)S(1)}, u32[]{:S(2)}, u32[]{:S(2)}) collective-permute-start(bf16[64,720]{1,0:T(8,128)(2,1)S(1)} %get-tuple-element.67), channel_id=1, source_target_pairs={{0,256},{128,384},{256,0},{384,128},{1,257},{129,385},{257,1},{385... | collective-permute-start | bytes 276488 | tf_op jit(solution)/shard_map/ppermute | solution.py:24

commit v4 on v3

v4 whole, which is shorter than its diff:
```python
import jax
import jax.numpy as jnp
from jax import lax
from jax.experimental import pallas as pl
from jax.experimental.pallas import tpu as pltpu
from jax.sharding import PartitionSpec as P

swish_alpha = 1.702
low = jnp.bfloat16
full = jnp.float32
HALF = 64
SLOTS = 5
QUARTER = 360
STRIDE = 384
PIECE = 512
CHUNK = 8
GROUP = 32
PEER = 256


def exchanged(block, axis, distance):
    count = lax.axis_size(axis)
    return lax.ppermute(block, axis, [(i, i ^ distance) for i in range(count)])


def contract(left, right, left_dim, right_dim):
    return lax.dot_general(
        left, right, (((left_dim,), (right_dim,)), ((), ())), preferred_element_type=full
    )


def iota(shape, dim):
    return lax.broadcasted_iota(jnp.int32, shape, dim)


def ones_at(mask):
    return jnp.where(mask, 1.0, 0.0)


def placed(ids, gates, experts):
    tokens = ids.shape[1]
    named = jnp.zeros((experts, tokens), full)
    gate = jnp.zeros((experts, tokens), full)
    for k in range(ids.shape[0]):
        hit = ids[k : k + 1, :] == iota((experts, tokens), 0)
        named = named + jnp.where(hit, 1.0, 0.0)
        gate = gate + jnp.where(hit, gates[k : k + 1, :], 0.0)
    first, later = iota((tokens, tokens), 0), iota((tokens, tokens), 1)
    before = ones_at((first < later) & (first // HALF == later // HALF)).astype(low)
    number = jnp.where(named > 0.0, contract(named.astype(low), before, 1, 0) + 1.0, 0.0)

    def spread(part):
        part = jnp.broadcast_to(part[:, None, :], (experts, CHUNK, tokens))
        part = part.reshape(experts * CHUNK, tokens)
        return jnp.concatenate([part, part], axis=0)

    number, gate = spread(number), spread(gate)
    shape = number.shape
    row = iota(shape, 0) % CHUNK
    number = jnp.where(iota(shape, 0) // (experts * CHUNK) == iota(shape, 1) // HALF, number, 0.0)
    slot = row.astype(full) + 1.0
    rest = 2.0 * (row - SLOTS).astype(full) + 1.0
    main = (row < SLOTS) & (number == slot)
    even = (row >= SLOTS) & (number == rest)
    odd = (row >= SLOTS) & (number == rest + 1.0)
    return main, even, odd, gate


def pack_kernel(ids_ref, gates_ref, tok_ref, grad_ref, raw_ref, x_ref):
    experts = raw_ref.shape[0] // (2 * CHUNK)
    x_ref[...] = jnp.zeros_like(x_ref)
    x_ref[:QUARTER, :] = tok_ref[...]
    x_ref[STRIDE : STRIDE + QUARTER, :] = grad_ref[...]
    main, even, odd, gate = placed(ids_ref[...], gates_ref[...], experts)
    main1, even1, odd1 = ones_at(main), ones_at(even), ones_at(odd)
    total = lambda block: jnp.sum(block, axis=1, keepdims=True)
    main_gate, even_gate, odd_gate = total(main1 * gate), total(even1 * gate), total(odd1 * gate)
    head = iota(main_gate.shape, 0) % CHUNK < SLOTS
    main1, even1, odd1 = main1.astype(low), even1.astype(low), odd1.astype(low)
    tail = x_ref[512:768, :]
    left = contract(main1, x_ref[0:256, :], 1, 1) + contract(even1, tail, 1, 1)
    right = contract(main1, x_ref[256:512, :], 1, 1) + contract(odd1, tail, 1, 1)
    raw_ref[:, 0:256] = (left * jnp.where(head, 1.0, even_gate)).astype(low)
    raw_ref[:, 256:384] = (right[:, :128] * jnp.where(head, 1.0, odd_gate)).astype(low)
    raw_ref[:, 384:512] = (right[:, 128:] * jnp.where(head, main_gate, odd_gate)).astype(low)


def small_params(size=12):
    return pltpu.CompilerParams(vmem_limit_bytes=size << 20)


def in_vmem(count):
    return [pl.BlockSpec(memory_space=pltpu.VMEM)] * count


def scalar():
    return pl.BlockSpec(memory_space=pltpu.SMEM)


def pack(ids, gates, tok, grad, rows):
    return pl.pallas_call(
        pack_kernel,
        in_specs=in_vmem(4),
        out_specs=in_vmem(1)[0],
        out_shape=jax.ShapeDtypeStruct((rows, PIECE), low),
        scratch_shapes=[pltpu.VMEM((2 * STRIDE, tok.shape[1]), low)],
        compiler_params=small_params(),
        cost_estimate=pl.CostEstimate(
            flops=8 * rows * 128 * 512, bytes_accessed=2 * rows * 512, transcendentals=0
        ),
    )(ids, gates, tok, grad)


def combine_kernel(ids_ref, gates_ref, raw_ref, out_ref, in_ref):
    experts = raw_ref.shape[0] // (2 * CHUNK)
    main, even, odd, gate = placed(ids_ref[...], gates_ref[...], experts)
    weight = jnp.where(main, gate, 0.0)
    high = weight.astype(low)
    rest = (weight - high.astype(full)).astype(low)
    main1, even1, odd1 = [ones_at(mask).astype(low) for mask in (main, even, odd)]
    out = contract(raw_ref[:, :384], high, 0, 0) + contract(raw_ref[:, :384], rest, 0, 0)
    out_ref[...] = out[:QUARTER].astype(low)
    first = contract(raw_ref[:, 384:512], main1, 0, 0)
    second = contract(raw_ref[:, 0:256], even1, 0, 0) + contract(raw_ref[:, 256:512], odd1, 0, 0)
    in_ref[0:128, :] = first.astype(low)
    in_ref[128:QUARTER, :] = second[: QUARTER - 128].astype(low)


def combine(ids, gates, raw):
    rows = raw.shape[0]
    return pl.pallas_call(
        combine_kernel,
        in_specs=in_vmem(3),
        out_specs=in_vmem(2),
        out_shape=[jax.ShapeDtypeStruct((QUARTER, ids.shape[1]), low)] * 2,
        compiler_params=small_params(),
        cost_estimate=pl.CostEstimate(
            flops=8 * rows * 128 * 512, bytes_accessed=2 * rows * 512, transcendentals=0
        ),
    )(ids, gates, raw)


def selection():
    shape = (GROUP * SLOTS, GROUP * CHUNK)
    dense, raw = iota(shape, 0), iota(shape, 1)
    slot, row = dense % SLOTS, raw % CHUNK
    same = dense // SLOTS == raw // CHUNK
    main = same & (row == slot)
    rest = same & (row == SLOTS + slot // 2)
    masks = (main, rest & (slot % 2 == 0), rest & (slot % 2 == 1))
    return jnp.concatenate([ones_at(mask).astype(low) for mask in masks], axis=0)


def expert_kernel(
    core_ref, mine_ref, other_ref, w_ref,
    keep_ref, send_ref, tok_ref, grad_ref, hid_ref, both_ref,
    dense, out_rows, in_rows,
):
    core = core_ref[0]
    chosen = selection()
    many, wide = GROUP * SLOTS, GROUP * CHUNK
    half = mine_ref.shape[0] // 2
    places = [
        (source, pair, slice(g * many, (g + 1) * many), slice(pair * half + g * wide, pair * half + (g + 1) * wide))
        for source in range(2)
        for pair in range(2)
        for g in range(half // wide)
    ]
    for source, pair, at, raw_at in places:
        found = contract(chosen, (mine_ref, other_ref)[source][raw_at, :], 1, 0)
        dense[source, pair, at, 0:512] = found[:many].astype(low)
        dense[source, pair, at, 512:768] = (
            found[many : 2 * many, :256] + found[2 * many :, 256:]
        ).astype(low)
    for mine in range(2):

        @pl.when(core == mine)
        def _():
            for source in range(2):
                for pair in range(2):
                    start = QUARTER * (2 * pair + (mine ^ source))
                    tok_ref[:, start : start + QUARTER] = dense[source, pair, :, 0:QUARTER]
                    grad_ref[:, start : start + QUARTER] = dense[
                        source, pair, :, STRIDE : STRIDE + QUARTER
                    ]

    tok = tok_ref[...]
    pre_gate = contract(tok, w_ref[0], 1, 1)
    pre_up = contract(tok, w_ref[1], 1, 1)
    grad_hidden = contract(grad_ref[...], w_ref[2], 1, 1)
    hidden_wide = pre_gate.shape[1]
    sig = jax.nn.sigmoid(swish_alpha * pre_gate)
    swish = pre_gate * sig
    hid_ref[...] = ((pre_up + 1.0) * swish).astype(low)
    both_ref[:, hidden_wide:] = (grad_hidden * swish).astype(low)
    slope = sig + swish_alpha * swish * (1.0 - sig)
    both_ref[:, :hidden_wide] = (grad_hidden * (pre_up + 1.0) * slope).astype(low)
    out_rows[...] = contract(hid_ref[...], w_ref[2], 1, 0).astype(low)
    in_rows[...] = contract(
        both_ref[...], w_ref[0:2].reshape(2 * hidden_wide, w_ref.shape[2]), 1, 0
    ).astype(low)
    for mine in range(2):

        @pl.when(core == mine)
        def _():
            for source in range(2):
                for pair in range(2):
                    start = QUARTER * (2 * pair + (mine ^ source))
                    dense[source, pair, :, 0:QUARTER] = out_rows[:, start : start + QUARTER]
                    dense[source, pair, :, STRIDE : STRIDE + QUARTER] = in_rows[
                        :, start : start + QUARTER
                    ]

    for source, pair, at, raw_at in places:
        head = contract(chosen[:many], dense[source, pair, at, 0:512], 0, 0)
        tail = dense[source, pair, at, 512:768]
        raw_ref = (keep_ref, send_ref)[source]
        raw_ref[raw_at, 0:256] = (
            head[:, :256] + contract(chosen[many : 2 * many], tail, 0, 0)
        ).astype(low)
        raw_ref[raw_at, 256:512] = (
            head[:, 256:] + contract(chosen[2 * many :], tail, 0, 0)
        ).astype(low)


def expert(core, mine, other, weights):
    raw_rows = mine.shape[0]
    count = raw_rows // (2 * CHUNK) * SLOTS
    hidden, width = weights.shape[1:]
    shape = lambda cols: jax.ShapeDtypeStruct((count, cols), low)
    return pl.pallas_call(
        expert_kernel,
        in_specs=[scalar()] + in_vmem(3),
        out_specs=in_vmem(6),
        out_shape=[jax.ShapeDtypeStruct((raw_rows, PIECE), low)] * 2
        + [shape(width)] * 2
        + [shape(hidden), shape(2 * hidden)],
        scratch_shapes=[pltpu.VMEM((2, 2, count, 2 * STRIDE), low)]
        + [pltpu.VMEM((count, width), low)] * 2,
        compiler_params=small_params(30),
        cost_estimate=pl.CostEstimate(
            flops=12 * count * width * hidden,
            bytes_accessed=16 * count * width,
            transcendentals=count * hidden,
        ),
    )(core, mine, other, weights)


def weight_products(refs, lanes):
    (hid_a, both_a, tok_a, grad_a), (hid_b, both_b, tok_b, grad_b) = refs
    hidden_wide = hid_a.shape[1]
    for pair, rows, at in (
        ((both_a, both_b), (tok_a, tok_b), lanes),
        (
            (both_a, both_b),
            (tok_a, tok_b),
            slice(hidden_wide + lanes.start, hidden_wide + lanes.stop),
        ),
        ((hid_a, hid_b), (grad_a, grad_b), lanes),
    ):
        yield contract(pair[0][:, at], rows[0][...], 0, 0) + contract(
            pair[1][:, at], rows[1][...], 0, 0
        )


def peer_kernel(*refs):
    first, second, outs = refs[0:4], refs[4:8], refs[8:11]
    size = outs[0].shape[0]
    for number, part in enumerate(weight_products((first, second), slice(PEER, PEER + size))):
        outs[number][...] = part.astype(low)


def own_kernel(*refs):
    first, second, got, outs = refs[0:4], refs[4:8], refs[8:11], refs[11:14]
    size = outs[0].shape[0]
    for number, part in enumerate(weight_products((first, second), slice(0, size))):
        outs[number][...] = (part + got[number][...].astype(full)).astype(low)


def weight_grads(kernel, first, second, hidden, width, got=()):
    outs = [jax.ShapeDtypeStruct((hidden, width), low)] * 3
    return pl.pallas_call(
        kernel,
        in_specs=in_vmem(8 + len(got)),
        out_specs=in_vmem(3),
        out_shape=outs,
        compiler_params=small_params(18),
        cost_estimate=pl.CostEstimate(
            flops=12 * first[2].shape[0] * width * hidden,
            bytes_accessed=16 * first[2].shape[0] * width,
            transcendentals=0,
        ),
    )(*first, *second, *got)


def by_parity(rows, exp_count):
    groups = [
        [(2 * high + core) * exp_count + place for high in range(2) for place in range(parity, exp_count, 2)]
        for core in range(2)
        for parity in range(2)
    ]
    chunks = rows.reshape(exp_count, CHUNK, PIECE)
    return lax.all_to_all(
        chunks, ("rep", "exp"), split_axis=0, concat_axis=0, axis_index_groups=groups, tiled=True
    ).reshape(rows.shape)


def local(tokens, expert_ids, gate_values, out_grad, gate_weight, up_weight, down_weight):
    exp_count = lax.axis_size("exp")
    core = (lax.axis_index("rep").astype(jnp.int32) % 2).reshape(1)
    hidden, width = gate_weight.shape[1:]
    ids, gates = expert_ids.T, gate_values.T

    peer_gate, peer_up, peer_down = [
        exchanged(w, "rep", 2) for w in (gate_weight, up_weight, down_weight)
    ]
    packed = pack(ids, gates, tokens.T, out_grad.T, exp_count * CHUNK)
    mine = by_parity(packed, exp_count)
    next_mine = exchanged(mine, "exp", 1)
    beside = exchanged(mine, "rep", 1)
    gap = jnp.zeros((PEER - hidden, width), low)
    weights = jnp.stack(
        [
            jnp.concatenate([own[0], gap, peer[0], gap], axis=0)
            for own, peer in (
                (gate_weight, peer_gate),
                (up_weight, peer_up),
                (down_weight, peer_down),
            )
        ]
    )
    keep_a, send_a, tok_a, grad_a, hid_a, both_a = expert(core, mine, beside, weights)
    got_a = exchanged(send_a, "rep", 1)
    next_mine, got_a = lax.optimization_barrier((next_mine, got_a))
    next_beside = exchanged(next_mine, "rep", 1)
    keep_b, send_b, tok_b, grad_b, hid_b, both_b = expert(core, next_mine, next_beside, weights)
    got_b = exchanged(send_b, "rep", 1)
    sum_b = (keep_b.astype(full) + got_b.astype(full)).astype(low)
    sum_b, hid_b, both_b = lax.optimization_barrier((sum_b, hid_b, both_b))
    got_sum = exchanged(sum_b, "exp", 1)
    rows_a, rows_b = (hid_a, both_a, tok_a, grad_a), (hid_b, both_b, tok_b, grad_b)
    peers = weight_grads(peer_kernel, rows_a, rows_b, hidden, width)
    got_peers = [exchanged(part, "rep", 2) for part in peers]
    total = (
        keep_a.astype(full) + got_a.astype(full) + got_sum.astype(full)
    ).astype(low)
    total, got_peers[0] = lax.optimization_barrier((total, got_peers[0]))
    returned = by_parity(total, exp_count)
    gate_grad, up_grad, down_grad = weight_grads(
        own_kernel, rows_a, rows_b, hidden, width, got_peers
    )
    returned, gate_grad, up_grad, down_grad = lax.optimization_barrier(
        (returned, gate_grad, up_grad, down_grad)
    )
    layer_out, input_grad = combine(ids, gates, returned)
    return (layer_out.T, input_grad.T, gate_grad[None], up_grad[None], down_grad[None])


def solution(mesh):
    in_specs = (
        P("exp", "rep"),
        P("exp", None),
        P("exp", None),
        P("exp", "rep"),
        P("exp", "rep", None),
        P("exp", "rep", None),
        P("exp", "rep", None),
    )
    out_specs = (
        P("exp", "rep"),
        P("exp", "rep"),
        P("exp", "rep", None),
        P("exp", "rep", None),
        P("exp", "rep", None),
    )
    return jax.shard_map(local, mesh=mesh, in_specs=in_specs, out_specs=out_specs, check_vma=False)
```

time: 243 us -> 221 us (0.909)
  waiting for transfers between devices: 114 us -> 99.8 us
  Pallas kernels: 34.5 us -> 25.7 us
  starting transfers between devices: 71.8 us -> 76.1 us
  other arithmetic: 7.79 us -> 4.51 us
    ppermute x12, waiting for transfers between devices: 114 us -> 78.5 us  [exchanged(): return lax.ppermute(block, axis, [(i, i ^ distance) for i in range(count)])]
    all_to_all x2, waiting for transfers between devices: 0.01 us -> 21.3 us  [by_parity(): lax.all_to_all(chunks, ('rep', 'exp'), split_axis=0, concat_axis=0, axis_...]
    all_to_all x2, starting transfers between devices: 29.4 us -> 35.5 us  [by_parity(): lax.all_to_all(chunks, ('rep', 'exp'), split_axis=0, concat_axis=0, axis_...]
    pallas_call x2, Pallas kernels: 21.6 us -> 15.7 us  [expert(): pl.pallas_call(expert_kernel, in_specs=[scalar()] + in_vmem(3), out_specs...]
    unnamed x46, local copies, waits for them, and re-layouts: 9.87 us -> 13.2 us
    pallas_call x2, Pallas kernels: 7.52 us -> 4.86 us  [weight_grads(): pl.pallas_call(kernel, in_specs=in_vmem(8 + len(got)), out_specs=in_vmem(...]
  transfers between devices with their start and end apart: 14 -> 14, of which waited for: 11 -> 9; matrix products, arithmetic and copies ran while one was open for 2% -> 2% of each run, Pallas kernels for 8% -> 6%
where the time goes in v4:
time: 221 us; the launch traced here: 220 us
  waiting for transfers between devices  99.8 us (45%)
  starting transfers between devices  76.1 us (34%)
  Pallas kernels  25.7 us (12%)
  local copies, waits for them, and re-layouts  13.2 us (6%)
  other arithmetic  4.51 us (2%)
    ppermute x12, waiting for transfers between devices, exchanged(): return lax.ppermute(block, axis, [(i, i ^ distance) for i in range(count)])  78.5 us
    ppermute x12, starting transfers between devices, exchanged(): return lax.ppermute(block, axis, [(i, i ^ distance) for i in range(count)])  40.5 us
    all_to_all x2, starting transfers between devices, by_parity(): lax.all_to_all(chunks, ('rep', 'exp'), split_axis=0, concat_axis=0, axis_...  35.5 us
    all_to_all x2, waiting for transfers between devices, by_parity(): lax.all_to_all(chunks, ('rep', 'exp'), split_axis=0, concat_axis=0, axis_...  21.3 us
    pallas_call x2, Pallas kernels, expert(): pl.pallas_call(expert_kernel, in_specs=[scalar()] + in_vmem(3), out_specs...  15.7 us
    unnamed x46, local copies, waits for them, and re-layouts  13.2 us
    pallas_call x2, Pallas kernels, weight_grads(): pl.pallas_call(kernel, in_specs=in_vmem(8 + len(got)), out_specs=in_vmem(...  4.86 us
  transfers between devices with their start and end apart: 14, of which 9 were waited for; matrix products, arithmetic and copies ran while one was open for 2% of the time, Pallas kernels for 6%

profile of v4, /device:TPU:1, one launch (start us, length us, event | category | flops | bytes accessed | tf_op | source)
XLA Modules:
  0.0 220.2 jit_solution(9448142601958038594)
XLA Ops:
  0.6 0.0 copy-start.14
  0.6 0.9 copy-done.14
  1.5 0.9 copy-done.15
  2.4 0.7 copy-done.16
  3.1 0.7 copy-done.18
  3.8 2.0 shard_map.110
  5.8 21.3 %all-to-all-start = ((bf16[128,8,512]{2,1,0:T(8,128)(2,1)}), bf16[128,8,512]{2,1,0:T(8,128)(2,1)}, u32[]{:S(2)}, u32[]{:S(2)}) async-start(bf16[128,8,512]{2,1,0:T(8,128)(2,1)} %bitcast.5), calls=%async_computation | async-start | bytes 2097152 | tf_op jit(solution)/shard_map/all_to_all | solution.py:303
  27.2 0.0 copy-done.20
  27.2 4.2 %collective-permute-start.1 = (bf16[1,180,1440]{2,1,0:T(8,128)(2,1)S(1)}, bf16[1,180,1440]{2,1,0:T(8,128)(2,1)S(1)}, u32[]{:S(2)}, u32[]{:S(2)}) collective-permute-start(bf16[1,180,1440]{2,1,0:T(8,128)(2,1)S(1)} %copy-done.20), channel_id=1, source_target_pairs={{0,256},{128,384},{256,0},{384,128},{1,257},{129,385},{257,1},{385... | collective-permute-start | bytes 1555208 | tf_op jit(solution)/shard_map/ppermute | solution.py:23
  31.4 0.0 copy-done.22
  31.4 2.6 %collective-permute-start.2 = (bf16[1,180,1440]{2,1,0:T(8,128)(2,1)S(1)}, bf16[1,180,1440]{2,1,0:T(8,128)(2,1)}, u32[]{:S(2)}, u32[]{:S(2)}) collective-permute-start(bf16[1,180,1440]{2,1,0:T(8,128)(2,1)S(1)} %copy-done.22), channel_id=1, source_target_pairs={{0,256},{128,384},{256,0},{384,128},{1,257},{129,385},{257,1},{385... | collective-permute-start | bytes 1555208 | tf_op jit(solution)/shard_map/ppermute | solution.py:23
  34.0 4.2 %collective-permute-start.3 = (bf16[1,180,1440]{2,1,0:T(8,128)(2,1)S(1)}, bf16[1,180,1440]{2,1,0:T(8,128)(2,1)}, u32[]{:S(2)}, u32[]{:S(2)}) collective-permute-start(bf16[1,180,1440]{2,1,0:T(8,128)(2,1)S(1)} %copy-done.21), channel_id=1, source_target_pairs={{0,256},{128,384},{256,0},{384,128},{1,257},{129,385},{257,1},{385... | collective-permute-start | bytes 1555208 | tf_op jit(solution)/shard_map/ppermute | solution.py:23
  38.3 21.2 %all-to-all-done = bf16[128,8,512]{2,1,0:T(8,128)(2,1)} async-done(((bf16[128,8,512]{2,1,0:T(8,128)(2,1)}), bf16[128,8,512]{2,1,0:T(8,128)(2,1)}, u32[]{:S(2)}, u32[]{:S(2)}) %all-to-all-start) | async-done | bytes 1048608 | tf_op jit(solution)/shard_map/all_to_all | solution.py:303
  59.5 3.9 %collective-permute-start = (bf16[1024,512]{1,0:T(8,128)(2,1)}, bf16[1024,512]{1,0:T(8,128)(2,1)S(1)}, u32[]{:S(2)}, u32[]{:S(2)}) collective-permute-start(bf16[1024,512]{1,0:T(8,128)(2,1)} %bitcast.6.mine_ref), channel_id=1, source_target_pairs={{0,128},{128,0},{256,384},{384,256},{1,129},{129,1},{257,385},{385... | collective-permute-start | bytes 3145736 | tf_op jit(solution)/shard_map/ppermute | solution.py:23
  63.4 0.0 collective-permute-done.1
  63.5 3.6 %collective-permute-done.2 = bf16[1,180,1440]{2,1,0:T(8,128)(2,1)} collective-permute-done((bf16[1,180,1440]{2,1,0:T(8,128)(2,1)S(1)}, bf16[1,180,1440]{2,1,0:T(8,128)(2,1)}, u32[]{:S(2)}, u32[]{:S(2)}) %collective-permute-start.2) | collective-permute-done | bytes 518432 | tf_op jit(solution)/shard_map/ppermute | solution.py:23
  67.1 12.1 %collective-permute-done.3 = bf16[1,180,1440]{2,1,0:T(8,128)(2,1)} collective-permute-done((bf16[1,180,1440]{2,1,0:T(8,128)(2,1)S(1)}, bf16[1,180,1440]{2,1,0:T(8,128)(2,1)}, u32[]{:S(2)}, u32[]{:S(2)}) %collective-permute-start.3) | collective-permute-done | bytes 518432 | tf_op jit(solution)/shard_map/ppermute | solution.py:23
  79.2 2.2 %fusion.3 = (bf16[1,512,1440]{2,1,0:T(8,128)(2,1)S(1)}, bf16[1,512,1440]{2,1,0:T(8,128)(2,1)S(1)}, bf16[1,512,1440]{2,1,0:T(8,128)(2,1)S(1)}) fusion(bf16[76,1440]{1,0:T(8,128)(2,1)S(1)} %broadcast_in_dim.12, bf16[180,1440]{1,0:T(8,128)(2,1)S(1)} %bitcast.36, bf16[180,1440]{1,0:T(8,128)(2,1)S(1)} %bitcast.33, bf16[180,1440]{1,0:T(8,128)(2,1)} %bitcast.14, ...), kind=kLoop, calls=%fused_computation.12 | loop fusion | flops 14745600 | bytes 7752960 | tf_op jit(solution)/shard_map/stack | solution.py:322
  81.4 0.6 pad_maximum_fusion.w_ref
  82.0 2.5 %collective-permute-start.4 = (bf16[1024,512]{1,0:T(8,128)(2,1)}, bf16[1024,512]{1,0:T(8,128)(2,1)S(1)}, u32[]{:S(2)}, u32[]{:S(2)}) collective-permute-start(bf16[1024,512]{1,0:T(8,128)(2,1)} %bitcast.6.mine_ref), channel_id=1, source_target_pairs={{0,1},{1,0},{2,3},{3,2},{4,5},{5,4},{6,7},{7,6},{8,9},{9,8},{10,11... | collective-permute-start | bytes 3145736 | tf_op jit(solution)/shard_map/ppermute | solution.py:23
  84.5 0.0 collective-permute-done.other_ref
  84.5 0.0 copy-start.10
  84.5 1.0 copy-done.10
  85.5 1.2 copy-done.11
  86.7 8.5 %shard_map.111 = (bf16[1024,512]{1,0:T(8,128)(2,1)S(1)}, bf16[1024,512]{1,0:T(8,128)(2,1)S(1)}, bf16[320,1440]{1,0:T(8,128)(2,1)S(1)}, bf16[320,1440]{1,0:T(8,12...) custom-call(s32[1]{0:T(128)} %bitcast.2.core_ref, bf16[1024,512]{1,0:T(8,128)(2,1)} %bitcast.6.mine_ref, ...), custom_call_target="tpu_custom_call" | custom-call | flops 2831155200 | bytes 7372800 | tf_op jit(solution)/shard_map/pallas_call | solution.py:231
  95.2 3.6 %collective-permute-start.5 = (bf16[1024,512]{1,0:T(8,128)(2,1)S(1)}, bf16[1024,512]{1,0:T(8,128)(2,1)S(1)}, u32[]{:S(2)}, u32[]{:S(2)}) collective-permute-start(bf16[1024,512]{1,0:T(8,128)(2,1)S(1)} %get-tuple-element.37), channel_id=1, source_target_pairs={{0,128},{128,0},{256,384},{384,256},{1,129},{129,1},{257,385},{385... | collective-permute-start | bytes 3145736 | tf_op jit(solution)/shard_map/ppermute | solution.py:23
  98.8 8.5 %collective-permute-done.4.mine_ref = bf16[1024,512]{1,0:T(8,128)(2,1)S(1)} collective-permute-done((bf16[1024,512]{1,0:T(8,128)(2,1)}, bf16[1024,512]{1,0:T(8,128)(2,1)S(1)}, u32[]{:S(2)}, u32[]{:S(2)}) %collective-permute-start.4) | collective-permute-done | bytes 1048608 | tf_op jit(solution)/shard_map/ppermute | solution.py:23
  107.3 0.0 collective-permute-done.5
  107.3 4.5 %collective-permute-start.6 = (bf16[1024,512]{1,0:T(8,128)(2,1)S(1)}, bf16[1024,512]{1,0:T(8,128)(2,1)S(1)}, u32[]{:S(2)}, u32[]{:S(2)}) collective-permute-start(bf16[1024,512]{1,0:T(8,128)(2,1)S(1)} %collective-permute-done.4.mine_ref), channel_id=1, source_target_pairs={{0,128},{128,0},{256,384},{384,256},{1,129},{129,1},{257,385},{385... | collective-permute-start | bytes 3145736 | tf_op jit(solution)/shard_map/ppermute | solution.py:23
  111.8 2.1 collective-permute-done.6.other_ref
  113.9 7.2 %shard_map.112 = (bf16[1024,512]{1,0:T(8,128)(2,1)S(1)}, bf16[1024,512]{1,0:T(8,128)(2,1)S(1)}, bf16[320,1440]{1,0:T(8,128)(2,1)S(1)}, bf16[320,1440]{1,0:T(8,12...) custom-call(s32[1]{0:T(128)} %bitcast.2.core_ref, ...), custom_call_target="tpu_custom_call" | custom-call | flops 2831155200 | bytes 7372800 | tf_op jit(solution)/shard_map/pallas_call | solution.py:231
  121.1 0.0 copy-start
  121.1 0.0 copy-start.4
  121.1 0.0 copy-start.6
  121.2 2.2 %collective-permute-start.7 = (bf16[1024,512]{1,0:T(8,128)(2,1)S(1)}, bf16[1024,512]{1,0:T(8,128)(2,1)S(1)}, u32[]{:S(2)}, u32[]{:S(2)}) collective-permute-start(bf16[1024,512]{1,0:T(8,128)(2,1)S(1)} %get-tuple-element.41), channel_id=1, source_target_pairs={{0,128},{128,0},{256,384},{384,256},{1,129},{129,1},{257,385},{385... | collective-permute-start | bytes 3145736 | tf_op jit(solution)/shard_map/ppermute | solution.py:23
  123.4 2.3 %collective-permute-done.7 = bf16[1024,512]{1,0:T(8,128)(2,1)S(1)} collective-permute-done((bf16[1024,512]{1,0:T(8,128)(2,1)S(1)}, bf16[1024,512]{1,0:T(8,128)(2,1)S(1)}, u32[]{:S(2)}, u32[]{:S(2)}) %collective-permute-start.7) | collective-permute-done | bytes 1048608 | tf_op jit(solution)/shard_map/ppermute | solution.py:23
  125.7 0.3 add_convert_fusion.1
  126.0 2.5 %collective-permute-start.8 = (bf16[1024,512]{1,0:T(8,128)(2,1)S(1)}, bf16[1024,512]{1,0:T(8,128)(2,1)S(1)}, u32[]{:S(2)}, u32[]{:S(2)}) collective-permute-start(bf16[1024,512]{1,0:T(8,128)(2,1)S(1)} %add_convert_fusion.1), channel_id=1, source_target_pairs={{0,1},{1,0},{2,3},{3,2},{4,5},{5,4},{6,7},{7,6},{8,9},{9,8},{10,11... | collective-permute-start | bytes 3145736 | tf_op jit(solution)/shard_map/ppermute | solution.py:23
  128.5 2.0 shard_map.113
  130.5 0.0 copy-done
  130.5 0.0 copy-done.4
  130.5 0.0 copy-done.6
  130.5 0.0 copy-start.12
  130.5 0.8 copy-done.12
  131.3 0.8 copy-done.13
  132.1 3.4 %collective-permute-start.9 = (bf16[180,1440]{1,0:T(8,128)(2,1)S(1)}, bf16[180,1440]{1,0:T(8,128)(2,1)S(1)}, u32[]{:S(2)}, u32[]{:S(2)}) collective-permute-start(bf16[180,1440]{1,0:T(8,128)(2,1)S(1)} %get-tuple-element.53), channel_id=1, source_target_pairs={{0,256},{128,384},{256,0},{384,128},{1,257},{129,385},{257,1},{385... | collective-permute-start | bytes 1555208 | tf_op jit(solution)/shard_map/ppermute | solution.py:23
  135.6 16.7 %collective-permute-done.8 = bf16[1024,512]{1,0:T(8,128)(2,1)S(1)} collective-permute-done((bf16[1024,512]{1,0:T(8,128)(2,1)S(1)}, bf16[1024,512]{1,0:T(8,128)(2,1)S(1)}, u32[]{:S(2)}, u32[]{:S(2)}) %collective-permute-start.8) | collective-permute-done | bytes 1048608 | tf_op jit(solution)/shard_map/ppermute | solution.py:23
  152.3 1.4 add_convert_fusion
  153.7 0.0 collective-permute-done.9.refs_8_
  153.7 0.8 copy-done.8
  154.5 14.2 %all-to-all-start.1 = ((bf16[128,8,512]{2,1,0:T(8,128)(2,1)}), bf16[128,8,512]{2,1,0:T(8,128)(2,1)}, u32[]{:S(2)}, u32[]{:S(2)}) async-start(bf16[128,8,512]{2,1,0:T(8,128)(2,1)} %bitcast.32), calls=%async_computation.1 | async-start | bytes 2097152 | tf_op jit(solution)/shard_map/all_to_all | solution.py:303
  168.7 4.2 %collective-permute-start.10 = (bf16[180,1440]{1,0:T(8,128)(2,1)}, bf16[180,1440]{1,0:T(8,128)(2,1)S(1)}, u32[]{:S(2)}, u32[]{:S(2)}) collective-permute-start(bf16[180,1440]{1,0:T(8,128)(2,1)} %copy-done.13), channel_id=1, source_target_pairs={{0,256},{128,384},{256,0},{384,128},{1,257},{129,385},{257,1},{385... | collective-permute-start | bytes 1555208 | tf_op jit(solution)/shard_map/ppermute | solution.py:23
  172.9 2.8 %collective-permute-start.11 = (bf16[180,1440]{1,0:T(8,128)(2,1)}, bf16[180,1440]{1,0:T(8,128)(2,1)S(1)}, u32[]{:S(2)}, u32[]{:S(2)}) collective-permute-start(bf16[180,1440]{1,0:T(8,128)(2,1)} %copy-done.12), channel_id=1, source_target_pairs={{0,256},{128,384},{256,0},{384,128},{1,257},{129,385},{257,1},{385... | collective-permute-start | bytes 1555208 | tf_op jit(solution)/shard_map/ppermute | solution.py:23
  175.7 18.2 %collective-permute-done.10.refs_9_ = bf16[180,1440]{1,0:T(8,128)(2,1)S(1)} collective-permute-done((bf16[180,1440]{1,0:T(8,128)(2,1)}, bf16[180,1440]{1,0:T(8,128)(2,1)S(1)}, u32[]{:S(2)}, u32[]{:S(2)}) %collective-permute-start.10) | collective-permute-done | bytes 518432 | tf_op jit(solution)/shard_map/ppermute | solution.py:23
  193.9 14.9 %collective-permute-done.11.refs_10_ = bf16[180,1440]{1,0:T(8,128)(2,1)S(1)} collective-permute-done((bf16[180,1440]{1,0:T(8,128)(2,1)}, bf16[180,1440]{1,0:T(8,128)(2,1)S(1)}, u32[]{:S(2)}, u32[]{:S(2)}) %collective-permute-start.11) | collective-permute-done | bytes 518432 | tf_op jit(solution)/shard_map/ppermute | solution.py:23
  208.9 1.2 copy-done.1
  210.1 1.1 copy-done.3
  211.2 1.1 copy-done.5
  212.3 1.0 copy-done.7
  213.2 1.1 copy-done.9
  214.3 2.8 %shard_map.114 = (bf16[180,1440]{1,0:T(8,128)(2,1)}, bf16[180,1440]{1,0:T(8,128)(2,1)}, bf16[180,1440]{1,0:T(8,128)(2,1)}) custom-call(bf16[320,512]{1,0:T(8,128)(2,1)S(1)} %get-tuple-element.45.refs_0_, bf16[320,1024]{1,0:T(8,128)(2,1)S(1)} %copy-done.3, bf16[320,1440]{1,0:T(8,128)(2,1)S(1)} %get-tuple-element.47.refs_2_, ...), custom_call_target="tpu_custom_call" | custom-call | flops 995328000 | bytes 7372800 | tf_op jit(solution)/shard_map/pallas_call | solution.py:282
  217.1 0.0 all-to-all-done.1
  217.1 0.0 copy-done.19
  217.1 3.1 %shard_map.115 = (bf16[360,128]{1,0:T(8,128)(2,1)}, bf16[360,128]{1,0:T(8,128)(2,1)}) custom-call(s32[4,128]{1,0:T(4,128)S(1)} %bitcast.29, f32[4,128]{1,0:T(4,128)S(1)} %bitcast.31, bf16[1024,512]{1,0:T(8,128)(2,1)} %bitcast.17.raw_ref), custom_call_target="tpu_custom_call" | custom-call | flops 536870912 | bytes 1048576 | tf_op jit(solution)/shard_map/pallas_call | solution.py:131
  (21 shorter events, 0.1 us)
Async XLA Ops:
  0.6 0.9 copy-start.14
  1.5 0.9 copy-start.15
  2.4 0.7 copy-start.16
  3.1 0.7 copy-start.18
  3.8 23.4 %copy-start.20 = (bf16[1,180,1440]{2,1,0:T(8,128)(2,1)S(1)}, bf16[1,180,1440]{2,1,0:T(8,128)(2,1)}, u32[]{:S(2)}) copy-start(bf16[1,180,1440]{2,1,0:T(8,128)(2,1)} %param.11) | copy-start | bytes 1555204
  3.8 27.7 %copy-start.22 = (bf16[1,180,1440]{2,1,0:T(8,128)(2,1)S(1)}, bf16[1,180,1440]{2,1,0:T(8,128)(2,1)}, u32[]{:S(2)}) copy-start(bf16[1,180,1440]{2,1,0:T(8,128)(2,1)} %param.12) | copy-start | bytes 1555204
  3.8 30.2 %copy-start.21 = (bf16[1,180,1440]{2,1,0:T(8,128)(2,1)S(1)}, bf16[1,180,1440]{2,1,0:T(8,128)(2,1)}, u32[]{:S(2)}) copy-start(bf16[1,180,1440]{2,1,0:T(8,128)(2,1)} %param.13) | copy-start | bytes 1555204
  5.8 53.7 %all-to-all-start = ((bf16[128,8,512]{2,1,0:T(8,128)(2,1)}), bf16[128,8,512]{2,1,0:T(8,128)(2,1)}, u32[]{:S(2)}, u32[]{:S(2)}) async-start(bf16[128,8,512]{2,1,0:T(8,128)(2,1)} %bitcast.5), calls=%async_computation | async-start | bytes 2097152 | tf_op jit(solution)/shard_map/all_to_all | solution.py:303
  27.2 36.2 %collective-permute-start.1 = (bf16[1,180,1440]{2,1,0:T(8,128)(2,1)S(1)}, bf16[1,180,1440]{2,1,0:T(8,128)(2,1)S(1)}, u32[]{:S(2)}, u32[]{:S(2)}) collective-permute-start(bf16[1,180,1440]{2,1,0:T(8,128)(2,1)S(1)} %copy-done.20), channel_id=1, source_target_pairs={{0,256},{128,384},{256,0},{384,128},{1,257},{129,385},{257,1},{385... | collective-permute-start | bytes 1555208 | tf_op jit(solution)/shard_map/ppermute | solution.py:23
  31.4 35.6 %collective-permute-start.2 = (bf16[1,180,1440]{2,1,0:T(8,128)(2,1)S(1)}, bf16[1,180,1440]{2,1,0:T(8,128)(2,1)}, u32[]{:S(2)}, u32[]{:S(2)}) collective-permute-start(bf16[1,180,1440]{2,1,0:T(8,128)(2,1)S(1)} %copy-done.22), channel_id=1, source_target_pairs={{0,256},{128,384},{256,0},{384,128},{1,257},{129,385},{257,1},{385... | collective-permute-start | bytes 1555208 | tf_op jit(solution)/shard_map/ppermute | solution.py:23
  34.0 45.1 %collective-permute-start.3 = (bf16[1,180,1440]{2,1,0:T(8,128)(2,1)S(1)}, bf16[1,180,1440]{2,1,0:T(8,128)(2,1)}, u32[]{:S(2)}, u32[]{:S(2)}) collective-permute-start(bf16[1,180,1440]{2,1,0:T(8,128)(2,1)S(1)} %copy-done.21), channel_id=1, source_target_pairs={{0,256},{128,384},{256,0},{384,128},{1,257},{129,385},{257,1},{385... | collective-permute-start | bytes 1555208 | tf_op jit(solution)/shard_map/ppermute | solution.py:23
  59.5 25.0 %collective-permute-start = (bf16[1024,512]{1,0:T(8,128)(2,1)}, bf16[1024,512]{1,0:T(8,128)(2,1)S(1)}, u32[]{:S(2)}, u32[]{:S(2)}) collective-permute-start(bf16[1024,512]{1,0:T(8,128)(2,1)} %bitcast.6.mine_ref), channel_id=1, source_target_pairs={{0,128},{128,0},{256,384},{384,256},{1,129},{129,1},{257,385},{385... | collective-permute-start | bytes 3145736 | tf_op jit(solution)/shard_map/ppermute | solution.py:23
  82.0 25.3 %collective-permute-start.4 = (bf16[1024,512]{1,0:T(8,128)(2,1)}, bf16[1024,512]{1,0:T(8,128)(2,1)S(1)}, u32[]{:S(2)}, u32[]{:S(2)}) collective-permute-start(bf16[1024,512]{1,0:T(8,128)(2,1)} %bitcast.6.mine_ref), channel_id=1, source_target_pairs={{0,1},{1,0},{2,3},{3,2},{4,5},{5,4},{6,7},{7,6},{8,9},{9,8},{10,11... | collective-permute-start | bytes 3145736 | tf_op jit(solution)/shard_map/ppermute | solution.py:23
  84.5 1.0 copy-start.10
  85.5 1.2 copy-start.11
  95.2 33.3 %copy-start.2 = (bf16[320,1024]{1,0:T(8,128)(2,1)}, bf16[320,1024]{1,0:T(8,128)(2,1)S(1)}, u32[]{:S(2)}) copy-start(bf16[320,1024]{1,0:T(8,128)(2,1)S(1)} %get-tuple-element.46.refs_1_) | copy-start | bytes 1966084
  95.2 12.1 %collective-permute-start.5 = (bf16[1024,512]{1,0:T(8,128)(2,1)S(1)}, bf16[1024,512]{1,0:T(8,128)(2,1)S(1)}, u32[]{:S(2)}, u32[]{:S(2)}) collective-permute-start(bf16[1024,512]{1,0:T(8,128)(2,1)S(1)} %get-tuple-element.37), channel_id=1, source_target_pairs={{0,128},{128,0},{256,384},{384,256},{1,129},{129,1},{257,385},{385... | collective-permute-start | bytes 3145736 | tf_op jit(solution)/shard_map/ppermute | solution.py:23
  107.3 6.6 %collective-permute-start.6 = (bf16[1024,512]{1,0:T(8,128)(2,1)S(1)}, bf16[1024,512]{1,0:T(8,128)(2,1)S(1)}, u32[]{:S(2)}, u32[]{:S(2)}) collective-permute-start(bf16[1024,512]{1,0:T(8,128)(2,1)S(1)} %collective-permute-done.4.mine_ref), channel_id=1, source_target_pairs={{0,128},{128,0},{256,384},{384,256},{1,129},{129,1},{257,385},{385... | collective-permute-start | bytes 3145736 | tf_op jit(solution)/shard_map/ppermute | solution.py:23
  121.1 9.4 %copy-start = (bf16[320,1440]{1,0:T(8,128)(2,1)}, bf16[320,1440]{1,0:T(8,128)(2,1)S(1)}, u32[]{:S(2)}) copy-start(bf16[320,1440]{1,0:T(8,128)(2,1)S(1)} %get-tuple-element.52.refs_7_) | copy-start | bytes 2764804
  121.1 9.4 %copy-start.4 = (bf16[320,1024]{1,0:T(8,128)(2,1)}, bf16[320,1024]{1,0:T(8,128)(2,1)S(1)}, u32[]{:S(2)}) copy-start(bf16[320,1024]{1,0:T(8,128)(2,1)S(1)} %get-tuple-element.50.refs_5_) | copy-start | bytes 1966084
  121.1 9.4 %copy-start.6 = (bf16[320,512]{1,0:T(8,128)(2,1)}, bf16[320,512]{1,0:T(8,128)(2,1)S(1)}, u32[]{:S(2)}) copy-start(bf16[320,512]{1,0:T(8,128)(2,1)S(1)} %get-tuple-element.49.refs_4_) | copy-start | bytes 983044
  121.2 4.6 %collective-permute-start.7 = (bf16[1024,512]{1,0:T(8,128)(2,1)S(1)}, bf16[1024,512]{1,0:T(8,128)(2,1)S(1)}, u32[]{:S(2)}, u32[]{:S(2)}) collective-permute-start(bf16[1024,512]{1,0:T(8,128)(2,1)S(1)} %get-tuple-element.41), channel_id=1, source_target_pairs={{0,128},{128,0},{256,384},{384,256},{1,129},{129,1},{257,385},{385... | collective-permute-start | bytes 3145736 | tf_op jit(solution)/shard_map/ppermute | solution.py:23
  126.0 26.3 %collective-permute-start.8 = (bf16[1024,512]{1,0:T(8,128)(2,1)S(1)}, bf16[1024,512]{1,0:T(8,128)(2,1)S(1)}, u32[]{:S(2)}, u32[]{:S(2)}) collective-permute-start(bf16[1024,512]{1,0:T(8,128)(2,1)S(1)} %add_convert_fusion.1), channel_id=1, source_target_pairs={{0,1},{1,0},{2,3},{3,2},{4,5},{5,4},{6,7},{7,6},{8,9},{9,8},{10,11... | collective-permute-start | bytes 3145736 | tf_op jit(solution)/shard_map/ppermute | solution.py:23
  130.5 0.8 copy-start.12
  131.3 0.8 copy-start.13
  132.1 21.6 %collective-permute-start.9 = (bf16[180,1440]{1,0:T(8,128)(2,1)S(1)}, bf16[180,1440]{1,0:T(8,128)(2,1)S(1)}, u32[]{:S(2)}, u32[]{:S(2)}) collective-permute-start(bf16[180,1440]{1,0:T(8,128)(2,1)S(1)} %get-tuple-element.53), channel_id=1, source_target_pairs={{0,256},{128,384},{256,0},{384,128},{1,257},{129,385},{257,1},{385... | collective-permute-start | bytes 1555208 | tf_op jit(solution)/shard_map/ppermute | solution.py:23
  153.7 0.8 copy-start.8
  154.5 62.6 %all-to-all-start.1 = ((bf16[128,8,512]{2,1,0:T(8,128)(2,1)}), bf16[128,8,512]{2,1,0:T(8,128)(2,1)}, u32[]{:S(2)}, u32[]{:S(2)}) async-start(bf16[128,8,512]{2,1,0:T(8,128)(2,1)} %bitcast.32), calls=%async_computation.1 | async-start | bytes 2097152 | tf_op jit(solution)/shard_map/all_to_all | solution.py:303
  168.7 25.2 %collective-permute-start.10 = (bf16[180,1440]{1,0:T(8,128)(2,1)}, bf16[180,1440]{1,0:T(8,128)(2,1)S(1)}, u32[]{:S(2)}, u32[]{:S(2)}) collective-permute-start(bf16[180,1440]{1,0:T(8,128)(2,1)} %copy-done.13), channel_id=1, source_target_pairs={{0,256},{128,384},{256,0},{384,128},{1,257},{129,385},{257,1},{385... | collective-permute-start | bytes 1555208 | tf_op jit(solution)/shard_map/ppermute | solution.py:23
  172.9 35.9 %collective-permute-start.11 = (bf16[180,1440]{1,0:T(8,128)(2,1)}, bf16[180,1440]{1,0:T(8,128)(2,1)S(1)}, u32[]{:S(2)}, u32[]{:S(2)}) collective-permute-start(bf16[180,1440]{1,0:T(8,128)(2,1)} %copy-done.12), channel_id=1, source_target_pairs={{0,256},{128,384},{256,0},{384,128},{1,257},{129,385},{257,1},{385... | collective-permute-start | bytes 1555208 | tf_op jit(solution)/shard_map/ppermute | solution.py:23
  208.9 1.2 copy-start.1
  210.1 1.1 copy-start.3
  211.2 1.1 copy-start.5
  212.3 1.0 copy-start.7
  213.2 1.1 copy-start.9
  214.3 2.8 %copy-start.17 = (s32[128,4]{0,1:T(4,128)S(1)}, s32[128,4]{0,1:T(4,128)}, u32[]{:S(2)}) copy-start(s32[128,4]{0,1:T(4,128)} %param.8) | copy-start | bytes 6148
  214.3 2.9 %copy-start.19 = (f32[128,4]{0,1:T(4,128)S(1)}, f32[128,4]{0,1:T(4,128)}, u32[]{:S(2)}) copy-start(f32[128,4]{0,1:T(4,128)} %param.9) | copy-start | bytes 6148

commit v5 on v4

--- a/solution.py
+++ b/solution.py
@@ -1,3 +1,5 @@
+import functools
+
 import jax
 import jax.numpy as jnp
 from jax import lax
@@ -100,11 +102,10 @@
 def pack(ids, gates, tok, grad, rows):
     return pl.pallas_call(
         pack_kernel,
-        in_specs=in_vmem(4),
-        out_specs=in_vmem(1)[0],
+        grid=(1,),
         out_shape=jax.ShapeDtypeStruct((rows, PIECE), low),
         scratch_shapes=[pltpu.VMEM((2 * STRIDE, tok.shape[1]), low)],
-        compiler_params=small_params(),
+        compiler_params=small_params(60),
         cost_estimate=pl.CostEstimate(
             flops=8 * rows * 128 * 512, bytes_accessed=2 * rows * 512, transcendentals=0
         ),
@@ -237,7 +238,7 @@
         + [shape(hidden), shape(2 * hidden)],
         scratch_shapes=[pltpu.VMEM((2, 2, count, 2 * STRIDE), low)]
         + [pltpu.VMEM((count, width), low)] * 2,
-        compiler_params=small_params(30),
+        compiler_params=small_params(20),
         cost_estimate=pl.CostEstimate(
             flops=12 * count * width * hidden,
             bytes_accessed=16 * count * width,
@@ -263,34 +264,46 @@
         )
 
 
-def peer_kernel(*refs):
+def product_kernel(start, *refs):
     first, second, outs = refs[0:4], refs[4:8], refs[8:11]
     size = outs[0].shape[0]
-    for number, part in enumerate(weight_products((first, second), slice(PEER, PEER + size))):
-        outs[number][...] = part.astype(low)
-
-
-def own_kernel(*refs):
-    first, second, got, outs = refs[0:4], refs[4:8], refs[8:11], refs[11:14]
-    size = outs[0].shape[0]
-    for number, part in enumerate(weight_products((first, second), slice(0, size))):
-        outs[number][...] = (part + got[number][...].astype(full)).astype(low)
-
-
-def weight_grads(kernel, first, second, hidden, width, got=()):
-    outs = [jax.ShapeDtypeStruct((hidden, width), low)] * 3
-    return pl.pallas_call(
-        kernel,
-        in_specs=in_vmem(8 + len(got)),
+    for number, part in enumerate(weight_products((first, second), slice(start, start + size))):
+        outs[number][...] = part.astype(outs[number].dtype)
+
+
+def weight_grads(first, second, start, hidden, width, dtype):
+    return pl.pallas_call(
+        functools.partial(product_kernel, start),
+        in_specs=in_vmem(8),
         out_specs=in_vmem(3),
-        out_shape=outs,
+        out_shape=[jax.ShapeDtypeStruct((hidden, width), dtype)] * 3,
         compiler_params=small_params(18),
         cost_estimate=pl.CostEstimate(
             flops=12 * first[2].shape[0] * width * hidden,
             bytes_accessed=16 * first[2].shape[0] * width,
             transcendentals=0,
         ),
-    )(*first, *second, *got)
+    )(*first, *second)
+
+
+def total_kernel(*refs):
+    for number in range(3):
+        own, got, out = refs[number], refs[3 + number], refs[6 + number]
+        out[...] = (own[...] + got[...].astype(full)).astype(low)
+
+
+def weight_totals(owns, got):
+    hidden, width = owns[0].shape
+    return pl.pallas_call(
+        total_kernel,
+        in_specs=in_vmem(6),
+        out_specs=in_vmem(3),
+        out_shape=[jax.ShapeDtypeStruct((hidden, width), low)] * 3,
+        compiler_params=small_params(16),
+        cost_estimate=pl.CostEstimate(
+            flops=3 * hidden * width, bytes_accessed=24 * hidden * width, transcendentals=0
+        ),
+    )(*owns, *got)
 
 
 def by_parity(rows, exp_count):
@@ -316,6 +329,7 @@
     ]
     packed = pack(ids, gates, tokens.T, out_grad.T, exp_count * CHUNK)
     mine = by_parity(packed, exp_count)
+    mine, peer_gate = lax.optimization_barrier((mine, peer_gate))
     next_mine = exchanged(mine, "exp", 1)
     beside = exchanged(mine, "rep", 1)
     gap = jnp.zeros((PEER - hidden, width), low)
@@ -329,26 +343,28 @@
             )
         ]
     )
+    mine, beside, next_mine, weights = lax.optimization_barrier(
+        (mine, beside, next_mine, weights)
+    )
+    next_beside = exchanged(next_mine, "rep", 1)
     keep_a, send_a, tok_a, grad_a, hid_a, both_a = expert(core, mine, beside, weights)
     got_a = exchanged(send_a, "rep", 1)
-    next_mine, got_a = lax.optimization_barrier((next_mine, got_a))
-    next_beside = exchanged(next_mine, "rep", 1)
+    next_beside, send_a = lax.optimization_barrier((next_beside, send_a))
     keep_b, send_b, tok_b, grad_b, hid_b, both_b = expert(core, next_mine, next_beside, weights)
     got_b = exchanged(send_b, "rep", 1)
+    rows_a, rows_b = (hid_a, both_a, tok_a, grad_a), (hid_b, both_b, tok_b, grad_b)
+    peers = weight_grads(rows_a, rows_b, PEER, hidden, width, low)
+    got_b, *peers = lax.optimization_barrier((got_b, *peers))
     sum_b = (keep_b.astype(full) + got_b.astype(full)).astype(low)
-    sum_b, hid_b, both_b = lax.optimization_barrier((sum_b, hid_b, both_b))
     got_sum = exchanged(sum_b, "exp", 1)
-    rows_a, rows_b = (hid_a, both_a, tok_a, grad_a), (hid_b, both_b, tok_b, grad_b)
-    peers = weight_grads(peer_kernel, rows_a, rows_b, hidden, width)
     got_peers = [exchanged(part, "rep", 2) for part in peers]
+    owns = weight_grads(rows_a, rows_b, 0, hidden, width, full)
     total = (
         keep_a.astype(full) + got_a.astype(full) + got_sum.astype(full)
     ).astype(low)
-    total, got_peers[0] = lax.optimization_barrier((total, got_peers[0]))
+    total, owns, *got_peers[:2] = lax.optimization_barrier((total, owns, *got_peers[:2]))
     returned = by_parity(total, exp_count)
-    gate_grad, up_grad, down_grad = weight_grads(
-        own_kernel, rows_a, rows_b, hidden, width, got_peers
-    )
+    gate_grad, up_grad, down_grad = weight_totals(owns, got_peers)
     returned, gate_grad, up_grad, down_grad = lax.optimization_barrier(
         (returned, gate_grad, up_grad, down_grad)
     )

time: 221 us -> 193 us (0.87)
  waiting for transfers between devices: 99.8 us -> 77 us
  local copies, waits for them, and re-layouts: 13.2 us -> 6.1 us
  starting transfers between devices: 76.1 us -> 73.2 us
  other arithmetic: 4.51 us -> 6.74 us
    all_to_all x2, waiting for transfers between devices: 21.3 us -> 9.49 us  [by_parity(): lax.all_to_all(chunks, ('rep', 'exp'), split_axis=0, concat_axis=0, axis_...]
    ppermute x12, waiting for transfers between devices: 78.5 us -> 67.5 us  [exchanged(): return lax.ppermute(block, axis, [(i, i ^ distance) for i in range(count)])]
    unnamed x46 -> x20, local copies, waits for them, and re-layouts: 13.2 us -> 6.08 us
    another operation x2, other arithmetic: 2.81 us -> 5.04 us  [local(): jnp.stack([jnp.concatenate([own[0], gap, peer[0], gap], axis=0) for own,...]
    pallas_call x3 -> x4, Pallas kernels: 6.91 us -> 8.52 us  [the longest x2 4.04 us: weight_grads(): pl.pallas_call(functools.partial(product_kernel, start), in_specs=in_vmem...]
  transfers between devices with their start and end apart: 14 -> 14, of which waited for: 9 -> 7; matrix products, arithmetic and copies ran while one was open for 2% -> 4% of each run, Pallas kernels for 6% -> 7%
where the time goes in v5:
time: 193 us; the launch traced here: 191 us
  waiting for transfers between devices  77 us (40%)
  starting transfers between devices  73.2 us (38%)
  Pallas kernels  27.3 us (14%)
  other arithmetic  6.74 us (3%)
  local copies, waits for them, and re-layouts  6.1 us (3%)
    ppermute x12, waiting for transfers between devices, exchanged(): return lax.ppermute(block, axis, [(i, i ^ distance) for i in range(count)])  67.5 us
    ppermute x12, starting transfers between devices, exchanged(): return lax.ppermute(block, axis, [(i, i ^ distance) for i in range(count)])  39 us
    all_to_all x2, starting transfers between devices, by_parity(): lax.all_to_all(chunks, ('rep', 'exp'), split_axis=0, concat_axis=0, axis_...  34.2 us
    pallas_call x2, Pallas kernels, expert(): pl.pallas_call(expert_kernel, in_specs=[scalar()] + in_vmem(3), out_specs...  15.7 us
    all_to_all x2, waiting for transfers between devices, by_parity(): lax.all_to_all(chunks, ('rep', 'exp'), split_axis=0, concat_axis=0, axis_...  9.49 us
    unnamed x20, local copies, waits for them, and re-layouts  6.08 us
    another operation x2, other arithmetic, local(): jnp.stack([jnp.concatenate([own[0], gap, peer[0], gap], axis=0) for own,...  5.04 us
    pallas_call x2, Pallas kernels, weight_grads(): pl.pallas_call(functools.partial(product_kernel, start), in_specs=in_vmem...  4.04 us
  transfers between devices with their start and end apart: 14, of which 7 were waited for; matrix products, arithmetic and copies ran while one was open for 4% of the time, Pallas kernels for 7%

profile of v5, /device:TPU:1, one launch (start us, length us, event | category | flops | bytes accessed | tf_op | source)
XLA Modules:
  0.0 191.2 jit_solution(7544331088510431142)
XLA Ops:
  0.6 0.0 copy-start.9
  0.6 3.1 %shard_map.110 = bf16[1024,512]{1,0:T(8,128)(2,1)} custom-call(s32[4,128]{1,0:T(4,128)} %bitcast.29, f32[4,128]{1,0:T(4,128)} %bitcast.31, bf16[360,128]{1,0:T(8,128)(2,1)} %bitcast.39, bf16[360,128]{1,0:T(8,128)(2,1)} %bitcast.40), custom_call_target="tpu_custom_call" | custom-call | flops 536870912 | bytes 1048576 | tf_op jit(solution)/shard_map/pallas_call | solution.py:103
  3.7 20.8 %all-to-all-start = ((bf16[128,8,512]{2,1,0:T(8,128)(2,1)}), bf16[128,8,512]{2,1,0:T(8,128)(2,1)S(1)}, u32[]{:S(2)}, u32[]{:S(2)}) async-start(bf16[128,8,512]{2,1,0:T(8,128)(2,1)} %bitcast.34), calls=%async_computation | async-start | bytes 2097152 | tf_op jit(solution)/shard_map/all_to_all | solution.py:316
  24.5 0.0 copy-done.9
  24.5 4.3 %collective-permute-start = (bf16[1,180,1440]{2,1,0:T(8,128)(2,1)S(1)}, bf16[1,180,1440]{2,1,0:T(8,128)(2,1)}, u32[]{:S(2)}, u32[]{:S(2)}) collective-permute-start(bf16[1,180,1440]{2,1,0:T(8,128)(2,1)S(1)} %copy-done.9), channel_id=1, source_target_pairs={{0,256},{128,384},{256,0},{384,128},{1,257},{129,385},{257,1},{385... | collective-permute-start | bytes 1555208 | tf_op jit(solution)/shard_map/ppermute | solution.py:25
  28.9 2.5 %collective-permute-start.3 = (bf16[1,180,1440]{2,1,0:T(8,128)(2,1)}, bf16[1,180,1440]{2,1,0:T(8,128)(2,1)}, u32[]{:S(2)}, u32[]{:S(2)}) collective-permute-start(bf16[1,180,1440]{2,1,0:T(8,128)(2,1)} %param.12), channel_id=1, source_target_pairs={{0,256},{128,384},{256,0},{384,128},{1,257},{129,385},{257,1},{385... | collective-permute-start | bytes 1555208 | tf_op jit(solution)/shard_map/ppermute | solution.py:25
  31.3 4.3 %collective-permute-start.4 = (bf16[1,180,1440]{2,1,0:T(8,128)(2,1)}, bf16[1,180,1440]{2,1,0:T(8,128)(2,1)}, u32[]{:S(2)}, u32[]{:S(2)}) collective-permute-start(bf16[1,180,1440]{2,1,0:T(8,128)(2,1)} %param.13), channel_id=1, source_target_pairs={{0,256},{128,384},{256,0},{384,128},{1,257},{129,385},{257,1},{385... | collective-permute-start | bytes 1555208 | tf_op jit(solution)/shard_map/ppermute | solution.py:25
  35.7 12.1 %collective-permute-done = bf16[1,180,1440]{2,1,0:T(8,128)(2,1)} collective-permute-done((bf16[1,180,1440]{2,1,0:T(8,128)(2,1)S(1)}, bf16[1,180,1440]{2,1,0:T(8,128)(2,1)}, u32[]{:S(2)}, u32[]{:S(2)}) %collective-permute-start) | collective-permute-done | bytes 518432 | tf_op jit(solution)/shard_map/ppermute | solution.py:25
  47.8 9.5 %all-to-all-done = bf16[128,8,512]{2,1,0:T(8,128)(2,1)S(1)} async-done(((bf16[128,8,512]{2,1,0:T(8,128)(2,1)}), bf16[128,8,512]{2,1,0:T(8,128)(2,1)S(1)}, u32[]{:S(2)}, u32[]{:S(2)}) %all-to-all-start) | async-done | bytes 1048608 | tf_op jit(solution)/shard_map/all_to_all | solution.py:316
  57.3 1.9 collective-permute-start.2
  59.2 3.9 %collective-permute-start.1 = (bf16[1024,512]{1,0:T(8,128)(2,1)S(1)}, bf16[1024,512]{1,0:T(8,128)(2,1)S(1)}, u32[]{:S(2)}, u32[]{:S(2)}) collective-permute-start(bf16[1024,512]{1,0:T(8,128)(2,1)S(1)} %bitcast.27), channel_id=1, source_target_pairs={{0,128},{128,0},{256,384},{384,256},{1,129},{129,1},{257,385},{385... | collective-permute-start | bytes 3145736 | tf_op jit(solution)/shard_map/ppermute | solution.py:25
  63.1 1.5 collective-permute-done.3
  64.7 12.1 %collective-permute-done.4 = bf16[1,180,1440]{2,1,0:T(8,128)(2,1)} collective-permute-done((bf16[1,180,1440]{2,1,0:T(8,128)(2,1)}, bf16[1,180,1440]{2,1,0:T(8,128)(2,1)}, u32[]{:S(2)}, u32[]{:S(2)}) %collective-permute-start.4) | collective-permute-done | bytes 518432 | tf_op jit(solution)/shard_map/ppermute | solution.py:25
  76.8 2.5 %fusion.3 = (bf16[1,512,1440]{2,1,0:T(8,128)(2,1)S(1)}, bf16[1,512,1440]{2,1,0:T(8,128)(2,1)S(1)}, bf16[1,512,1440]{2,1,0:T(8,128)(2,1)S(1)}) fusion(bf16[76,1440]{1,0:T(8,128)(2,1)S(1)} %broadcast_in_dim.12, bf16[180,1440]{1,0:T(8,128)(2,1)} %bitcast.8, bf16[180,1440]{1,0:T(8,128)(2,1)} %bitcast.35, bf16[180,1440]{1,0:T(8,128)(2,1)} %bitcast.14, ...), kind=kLoop, calls=%fused_computation.12 | loop fusion | flops 14745600 | bytes 7752960 | tf_op jit(solution)/shard_map/stack | solution.py:336
  79.4 2.5 %pad_maximum_fusion.w_ref = bf16[3,512,1440]{2,1,0:T(8,128)(2,1)} fusion(bf16[1,512,1440]{2,1,0:T(8,128)(2,1)S(1)} %get-tuple-element.94, bf16[1,512,1440]{2,1,0:T(8,128)(2,1)S(1)} %get-tuple-element.95, bf16[1,512,1440]{2,1,0:T(8,128)(2,1)S(1)} %get-tuple-element.93), kind=kLoop, calls=%fused_computation | loop fusion | flops 4423680 | bytes 8847360 | tf_op jit(solution)/shard_map/stack | solution.py:336
  81.9 0.0 collective-permute-done.2.mine_ref
  81.9 0.0 collective-permute-done.1.other_ref
  81.9 4.8 %collective-permute-start.6 = (bf16[1024,512]{1,0:T(8,128)(2,1)S(1)}, bf16[1024,512]{1,0:T(8,128)(2,1)}, u32[]{:S(2)}, u32[]{:S(2)}) collective-permute-start(bf16[1024,512]{1,0:T(8,128)(2,1)S(1)} %collective-permute-done.2.mine_ref), channel_id=1, source_target_pairs={{0,128},{128,0},{256,384},{384,256},{1,129},{129,1},{257,385},{385... | collective-permute-start | bytes 3145736 | tf_op jit(solution)/shard_map/ppermute | solution.py:25
  86.7 0.0 copy-start
  86.7 2.3 %copy-done = bf16[3,512,1440]{2,1,0:T(8,128)(2,1)S(1)} copy-done((bf16[3,512,1440]{2,1,0:T(8,128)(2,1)S(1)}, bf16[3,512,1440]{2,1,0:T(8,128)(2,1)}, u32[]{:S(2)}) %copy-start) | copy-done | bytes 4423704
  89.0 0.0 copy-start.1
  89.0 7.3 %shard_map.111 = (bf16[1024,512]{1,0:T(8,128)(2,1)S(1)}, bf16[1024,512]{1,0:T(8,128)(2,1)S(1)}, bf16[320,1440]{1,0:T(8,128)(2,1)S(1)}, bf16[320,1440]{1,0:T(8,12...) custom-call(s32[1]{0:T(128)} %bitcast.2.core_ref, bf16[1024,512]{1,0:T(8,128)(2,1)S(1)} %bitcast.28, ...), custom_call_target="tpu_custom_call" | custom-call | flops 2831155200 | bytes 7372800 | tf_op jit(solution)/shard_map/pallas_call | solution.py:232
  96.3 0.0 collective-permute-done.6.other_ref
  96.4 0.0 copy-done.1
  96.4 8.4 %shard_map.112 = (bf16[1024,512]{1,0:T(8,128)(2,1)S(1)}, bf16[1024,512]{1,0:T(8,128)(2,1)S(1)}, bf16[320,1440]{1,0:T(8,128)(2,1)S(1)}, bf16[320,1440]{1,0:T(8,12...) custom-call(s32[1]{0:T(128)} %bitcast.2.core_ref, ...), custom_call_target="tpu_custom_call" | custom-call | flops 2831155200 | bytes 7372800 | tf_op jit(solution)/shard_map/pallas_call | solution.py:232
  104.8 1.9 %collective-permute-start.7 = (bf16[1024,512]{1,0:T(8,128)(2,1)S(1)}, bf16[1024,512]{1,0:T(8,128)(2,1)S(1)}, u32[]{:S(2)}, u32[]{:S(2)}) collective-permute-start(bf16[1024,512]{1,0:T(8,128)(2,1)S(1)} %get-tuple-element.59), channel_id=1, source_target_pairs={{0,128},{128,0},{256,384},{384,256},{1,129},{129,1},{257,385},{385... | collective-permute-start | bytes 3145736 | tf_op jit(solution)/shard_map/ppermute | solution.py:25
  106.7 2.4 %collective-permute-start.5 = (bf16[1024,512]{1,0:T(8,128)(2,1)S(1)}, bf16[1024,512]{1,0:T(8,128)(2,1)S(1)}, u32[]{:S(2)}, u32[]{:S(2)}) collective-permute-start(bf16[1024,512]{1,0:T(8,128)(2,1)S(1)} %get-tuple-element.55), channel_id=1, source_target_pairs={{0,128},{128,0},{256,384},{384,256},{1,129},{129,1},{257,385},{385... | collective-permute-start | bytes 3145736 | tf_op jit(solution)/shard_map/ppermute | solution.py:25
  109.1 2.0 %shard_map.113 = (bf16[180,1440]{1,0:T(8,128)(2,1)S(1)}, bf16[180,1440]{1,0:T(8,128)(2,1)S(1)}, bf16[180,1440]{1,0:T(8,128)(2,1)S(1)}) custom-call(bf16[320,512]{1,0:T(8,128)(2,1)S(1)} %get-tuple-element.60.refs_0_, bf16[320,1024]{1,0:T(8,128)(2,1)S(1)} %get-tuple-element.61.refs_1_, bf16[320,1440]{1,0:T(8,128)(2,1)S(1)} %get-tuple-element.62.refs_2_, ...), custom_call_target="tpu_custom_call" | custom-call | flops 995328000 | bytes 7372800 | tf_op jit(solution)/shard_map/pallas_call | solution.py:275
  111.1 0.0 copy-start.6
  111.2 0.0 collective-permute-done.7
  111.2 0.3 add_convert_fusion.1
  111.5 1.9 %collective-permute-start.8 = (bf16[1024,512]{1,0:T(8,128)(2,1)S(1)}, bf16[1024,512]{1,0:T(8,128)(2,1)S(1)}, u32[]{:S(2)}, u32[]{:S(2)}) collective-permute-start(bf16[1024,512]{1,0:T(8,128)(2,1)S(1)} %add_convert_fusion.1), channel_id=1, source_target_pairs={{0,1},{1,0},{2,3},{3,2},{4,5},{5,4},{6,7},{7,6},{8,9},{9,8},{10,11... | collective-permute-start | bytes 3145736 | tf_op jit(solution)/shard_map/ppermute | solution.py:25
  113.4 2.4 %collective-permute-start.9 = (bf16[180,1440]{1,0:T(8,128)(2,1)S(1)}, bf16[180,1440]{1,0:T(8,128)(2,1)S(1)}, u32[]{:S(2)}, u32[]{:S(2)}) collective-permute-start(bf16[180,1440]{1,0:T(8,128)(2,1)S(1)} %get-tuple-element.75), channel_id=1, source_target_pairs={{0,256},{128,384},{256,0},{384,128},{1,257},{129,385},{257,1},{385... | collective-permute-start | bytes 1555208 | tf_op jit(solution)/shard_map/ppermute | solution.py:25
  115.8 4.4 %collective-permute-start.10 = (bf16[180,1440]{1,0:T(8,128)(2,1)S(1)}, bf16[180,1440]{1,0:T(8,128)(2,1)S(1)}, u32[]{:S(2)}, u32[]{:S(2)}) collective-permute-start(bf16[180,1440]{1,0:T(8,128)(2,1)S(1)} %get-tuple-element.76), channel_id=1, source_target_pairs={{0,256},{128,384},{256,0},{384,128},{1,257},{129,385},{257,1},{385... | collective-permute-start | bytes 1555208 | tf_op jit(solution)/shard_map/ppermute | solution.py:25
  120.2 2.0 %shard_map.114 = (f32[180,1440]{1,0:T(8,128)S(1)}, f32[180,1440]{1,0:T(8,128)S(1)}, f32[180,1440]{1,0:T(8,128)S(1)}) custom-call(bf16[320,512]{1,0:T(8,128)(2,1)S(1)} %get-tuple-element.60.refs_0_, bf16[320,1024]{1,0:T(8,128)(2,1)S(1)} %get-tuple-element.61.refs_1_, bf16[320,1440]{1,0:T(8,128)(2,1)S(1)} %get-tuple-element.62.refs_2_, ...), custom_call_target="tpu_custom_call" | custom-call | flops 995328000 | bytes 7372800 | tf_op jit(solution)/shard_map/pallas_call | solution.py:275
  122.2 0.0 copy-done.6
  122.2 0.0 collective-permute-done.5
  122.3 15.9 %collective-permute-done.8 = bf16[1024,512]{1,0:T(8,128)(2,1)S(1)} collective-permute-done((bf16[1024,512]{1,0:T(8,128)(2,1)S(1)}, bf16[1024,512]{1,0:T(8,128)(2,1)S(1)}, u32[]{:S(2)}, u32[]{:S(2)}) %collective-permute-start.8) | collective-permute-done | bytes 1048608 | tf_op jit(solution)/shard_map/ppermute | solution.py:25
  138.1 1.4 add_convert_fusion
  139.5 0.0 collective-permute-done.9.refs_3_
  139.5 0.0 copy-start.2
  139.6 0.8 copy-done.2
  140.4 2.7 %collective-permute-done.10.refs_4_ = bf16[180,1440]{1,0:T(8,128)(2,1)S(1)} collective-permute-done((bf16[180,1440]{1,0:T(8,128)(2,1)S(1)}, bf16[180,1440]{1,0:T(8,128)(2,1)S(1)}, u32[]{:S(2)}, u32[]{:S(2)}) %collective-permute-start.10) | collective-permute-done | bytes 518432 | tf_op jit(solution)/shard_map/ppermute | solution.py:25
  143.0 0.0 copy-start.4
  143.0 0.8 copy-done.4
  143.8 0.0 copy-start.7
  143.8 0.0 copy-start.8
  143.8 13.4 %all-to-all-start.1 = ((bf16[128,8,512]{2,1,0:T(8,128)(2,1)}), bf16[128,8,512]{2,1,0:T(8,128)(2,1)}, u32[]{:S(2)}, u32[]{:S(2)}) async-start(bf16[128,8,512]{2,1,0:T(8,128)(2,1)} %bitcast.33), calls=%async_computation.1 | async-start | bytes 2097152 | tf_op jit(solution)/shard_map/all_to_all | solution.py:316
  157.2 4.2 %collective-permute-start.11 = (bf16[180,1440]{1,0:T(8,128)(2,1)}, bf16[180,1440]{1,0:T(8,128)(2,1)S(1)}, u32[]{:S(2)}, u32[]{:S(2)}) collective-permute-start(bf16[180,1440]{1,0:T(8,128)(2,1)} %copy-done.6), channel_id=1, source_target_pairs={{0,256},{128,384},{256,0},{384,128},{1,257},{129,385},{257,1},{385... | collective-permute-start | bytes 1555208 | tf_op jit(solution)/shard_map/ppermute | solution.py:25
  161.5 23.1 %collective-permute-done.11.refs_5_ = bf16[180,1440]{1,0:T(8,128)(2,1)S(1)} collective-permute-done((bf16[180,1440]{1,0:T(8,128)(2,1)}, bf16[180,1440]{1,0:T(8,128)(2,1)S(1)}, u32[]{:S(2)}, u32[]{:S(2)}) %collective-permute-start.11) | collective-permute-done | bytes 518432 | tf_op jit(solution)/shard_map/ppermute | solution.py:25
  184.6 0.0 copy-start.3
  184.6 1.1 copy-done.3
  185.6 0.0 copy-start.5
  185.6 1.1 copy-done.5
  186.7 1.4 shard_map.115
  188.1 0.0 all-to-all-done.1
  188.1 0.0 copy-done.7
  188.1 0.0 copy-done.8
  188.1 3.1 %shard_map.116 = (bf16[360,128]{1,0:T(8,128)(2,1)}, bf16[360,128]{1,0:T(8,128)(2,1)}) custom-call(s32[4,128]{1,0:T(4,128)S(1)} %bitcast.30, f32[4,128]{1,0:T(4,128)S(1)} %bitcast.32, bf16[1024,512]{1,0:T(8,128)(2,1)} %bitcast.17.raw_ref), custom_call_target="tpu_custom_call" | custom-call | flops 536870912 | bytes 1048576 | tf_op jit(solution)/shard_map/pallas_call | solution.py:132
  (1 shorter events, 0.0 us)
Async XLA Ops:
  0.6 23.9 %copy-start.9 = (bf16[1,180,1440]{2,1,0:T(8,128)(2,1)S(1)}, bf16[1,180,1440]{2,1,0:T(8,128)(2,1)}, u32[]{:S(2)}) copy-start(bf16[1,180,1440]{2,1,0:T(8,128)(2,1)} %param.11) | copy-start | bytes 1555204
  3.7 53.6 %all-to-all-start = ((bf16[128,8,512]{2,1,0:T(8,128)(2,1)}), bf16[128,8,512]{2,1,0:T(8,128)(2,1)S(1)}, u32[]{:S(2)}, u32[]{:S(2)}) async-start(bf16[128,8,512]{2,1,0:T(8,128)(2,1)} %bitcast.34), calls=%async_computation | async-start | bytes 2097152 | tf_op jit(solution)/shard_map/all_to_all | solution.py:316
  24.5 23.3 %collective-permute-start = (bf16[1,180,1440]{2,1,0:T(8,128)(2,1)S(1)}, bf16[1,180,1440]{2,1,0:T(8,128)(2,1)}, u32[]{:S(2)}, u32[]{:S(2)}) collective-permute-start(bf16[1,180,1440]{2,1,0:T(8,128)(2,1)S(1)} %copy-done.9), channel_id=1, source_target_pairs={{0,256},{128,384},{256,0},{384,128},{1,257},{129,385},{257,1},{385... | collective-permute-start | bytes 1555208 | tf_op jit(solution)/shard_map/ppermute | solution.py:25
  28.9 35.8 %collective-permute-start.3 = (bf16[1,180,1440]{2,1,0:T(8,128)(2,1)}, bf16[1,180,1440]{2,1,0:T(8,128)(2,1)}, u32[]{:S(2)}, u32[]{:S(2)}) collective-permute-start(bf16[1,180,1440]{2,1,0:T(8,128)(2,1)} %param.12), channel_id=1, source_target_pairs={{0,256},{128,384},{256,0},{384,128},{1,257},{129,385},{257,1},{385... | collective-permute-start | bytes 1555208 | tf_op jit(solution)/shard_map/ppermute | solution.py:25
  31.3 45.4 %collective-permute-start.4 = (bf16[1,180,1440]{2,1,0:T(8,128)(2,1)}, bf16[1,180,1440]{2,1,0:T(8,128)(2,1)}, u32[]{:S(2)}, u32[]{:S(2)}) collective-permute-start(bf16[1,180,1440]{2,1,0:T(8,128)(2,1)} %param.13), channel_id=1, source_target_pairs={{0,256},{128,384},{256,0},{384,128},{1,257},{129,385},{257,1},{385... | collective-permute-start | bytes 1555208 | tf_op jit(solution)/shard_map/ppermute | solution.py:25
  57.3 24.6 %collective-permute-start.2 = (bf16[1024,512]{1,0:T(8,128)(2,1)S(1)}, bf16[1024,512]{1,0:T(8,128)(2,1)S(1)}, u32[]{:S(2)}, u32[]{:S(2)}) collective-permute-start(bf16[1024,512]{1,0:T(8,128)(2,1)S(1)} %bitcast.26), channel_id=1, source_target_pairs={{0,1},{1,0},{2,3},{3,2},{4,5},{5,4},{6,7},{7,6},{8,9},{9,8},{10,11... | collective-permute-start | bytes 3145736 | tf_op jit(solution)/shard_map/ppermute | solution.py:25
  59.2 22.7 %collective-permute-start.1 = (bf16[1024,512]{1,0:T(8,128)(2,1)S(1)}, bf16[1024,512]{1,0:T(8,128)(2,1)S(1)}, u32[]{:S(2)}, u32[]{:S(2)}) collective-permute-start(bf16[1024,512]{1,0:T(8,128)(2,1)S(1)} %bitcast.27), channel_id=1, source_target_pairs={{0,128},{128,0},{256,384},{384,256},{1,129},{129,1},{257,385},{385... | collective-permute-start | bytes 3145736 | tf_op jit(solution)/shard_map/ppermute | solution.py:25
  81.9 14.5 %collective-permute-start.6 = (bf16[1024,512]{1,0:T(8,128)(2,1)S(1)}, bf16[1024,512]{1,0:T(8,128)(2,1)}, u32[]{:S(2)}, u32[]{:S(2)}) collective-permute-start(bf16[1024,512]{1,0:T(8,128)(2,1)S(1)} %collective-permute-done.2.mine_ref), channel_id=1, source_target_pairs={{0,128},{128,0},{256,384},{384,256},{1,129},{129,1},{257,385},{385... | collective-permute-start | bytes 3145736 | tf_op jit(solution)/shard_map/ppermute | solution.py:25
  86.7 2.3 %copy-start = (bf16[3,512,1440]{2,1,0:T(8,128)(2,1)S(1)}, bf16[3,512,1440]{2,1,0:T(8,128)(2,1)}, u32[]{:S(2)}) copy-start(bf16[3,512,1440]{2,1,0:T(8,128)(2,1)} %pad_maximum_fusion.w_ref) | copy-start | bytes 13271044
  89.0 7.4 %copy-start.1 = (bf16[3,512,1440]{2,1,0:T(8,128)(2,1)S(1)}, bf16[3,512,1440]{2,1,0:T(8,128)(2,1)}, u32[]{:S(2)}) copy-start(bf16[3,512,1440]{2,1,0:T(8,128)(2,1)} %pad_maximum_fusion.w_ref) | copy-start | bytes 13271044
  104.8 6.4 %collective-permute-start.7 = (bf16[1024,512]{1,0:T(8,128)(2,1)S(1)}, bf16[1024,512]{1,0:T(8,128)(2,1)S(1)}, u32[]{:S(2)}, u32[]{:S(2)}) collective-permute-start(bf16[1024,512]{1,0:T(8,128)(2,1)S(1)} %get-tuple-element.59), channel_id=1, source_target_pairs={{0,128},{128,0},{256,384},{384,256},{1,129},{129,1},{257,385},{385... | collective-permute-start | bytes 3145736 | tf_op jit(solution)/shard_map/ppermute | solution.py:25
  106.7 15.5 %collective-permute-start.5 = (bf16[1024,512]{1,0:T(8,128)(2,1)S(1)}, bf16[1024,512]{1,0:T(8,128)(2,1)S(1)}, u32[]{:S(2)}, u32[]{:S(2)}) collective-permute-start(bf16[1024,512]{1,0:T(8,128)(2,1)S(1)} %get-tuple-element.55), channel_id=1, source_target_pairs={{0,128},{128,0},{256,384},{384,256},{1,129},{129,1},{257,385},{385... | collective-permute-start | bytes 3145736 | tf_op jit(solution)/shard_map/ppermute | solution.py:25
  111.1 11.1 %copy-start.6 = (bf16[180,1440]{1,0:T(8,128)(2,1)}, bf16[180,1440]{1,0:T(8,128)(2,1)S(1)}, u32[]{:S(2)}) copy-start(bf16[180,1440]{1,0:T(8,128)(2,1)S(1)} %get-tuple-element.83) | copy-start | bytes 1555204
  111.5 26.7 %collective-permute-start.8 = (bf16[1024,512]{1,0:T(8,128)(2,1)S(1)}, bf16[1024,512]{1,0:T(8,128)(2,1)S(1)}, u32[]{:S(2)}, u32[]{:S(2)}) collective-permute-start(bf16[1024,512]{1,0:T(8,128)(2,1)S(1)} %add_convert_fusion.1), channel_id=1, source_target_pairs={{0,1},{1,0},{2,3},{3,2},{4,5},{5,4},{6,7},{7,6},{8,9},{9,8},{10,11... | collective-permute-start | bytes 3145736 | tf_op jit(solution)/shard_map/ppermute | solution.py:25
  113.4 26.1 %collective-permute-start.9 = (bf16[180,1440]{1,0:T(8,128)(2,1)S(1)}, bf16[180,1440]{1,0:T(8,128)(2,1)S(1)}, u32[]{:S(2)}, u32[]{:S(2)}) collective-permute-start(bf16[180,1440]{1,0:T(8,128)(2,1)S(1)} %get-tuple-element.75), channel_id=1, source_target_pairs={{0,256},{128,384},{256,0},{384,128},{1,257},{129,385},{257,1},{385... | collective-permute-start | bytes 1555208 | tf_op jit(solution)/shard_map/ppermute | solution.py:25
  115.8 27.2 %collective-permute-start.10 = (bf16[180,1440]{1,0:T(8,128)(2,1)S(1)}, bf16[180,1440]{1,0:T(8,128)(2,1)S(1)}, u32[]{:S(2)}, u32[]{:S(2)}) collective-permute-start(bf16[180,1440]{1,0:T(8,128)(2,1)S(1)} %get-tuple-element.76), channel_id=1, source_target_pairs={{0,256},{128,384},{256,0},{384,128},{1,257},{129,385},{257,1},{385... | collective-permute-start | bytes 1555208 | tf_op jit(solution)/shard_map/ppermute | solution.py:25
  139.5 0.8 copy-start.2
  143.0 0.8 copy-start.4
  143.8 44.3 %copy-start.7 = (s32[128,4]{0,1:T(4,128)S(1)}, s32[128,4]{0,1:T(4,128)}, u32[]{:S(2)}) copy-start(s32[128,4]{0,1:T(4,128)} %param.8) | copy-start | bytes 6148
  143.8 44.3 %copy-start.8 = (f32[128,4]{0,1:T(4,128)S(1)}, f32[128,4]{0,1:T(4,128)}, u32[]{:S(2)}) copy-start(f32[128,4]{0,1:T(4,128)} %param.9) | copy-start | bytes 6148
  143.8 44.3 %all-to-all-start.1 = ((bf16[128,8,512]{2,1,0:T(8,128)(2,1)}), bf16[128,8,512]{2,1,0:T(8,128)(2,1)}, u32[]{:S(2)}, u32[]{:S(2)}) async-start(bf16[128,8,512]{2,1,0:T(8,128)(2,1)} %bitcast.33), calls=%async_computation.1 | async-start | bytes 2097152 | tf_op jit(solution)/shard_map/all_to_all | solution.py:316
  157.2 27.4 %collective-permute-start.11 = (bf16[180,1440]{1,0:T(8,128)(2,1)}, bf16[180,1440]{1,0:T(8,128)(2,1)S(1)}, u32[]{:S(2)}, u32[]{:S(2)}) collective-permute-start(bf16[180,1440]{1,0:T(8,128)(2,1)} %copy-done.6), channel_id=1, source_target_pairs={{0,256},{128,384},{256,0},{384,128},{1,257},{129,385},{257,1},{385... | collective-permute-start | bytes 1555208 | tf_op jit(solution)/shard_map/ppermute | solution.py:25
  184.6 1.1 copy-start.3
  185.6 1.1 copy-start.5

commit v6 on v5

--- a/solution.py
+++ b/solution.py
@@ -112,33 +112,52 @@
     )(ids, gates, tok, grad)
 
 
-def combine_kernel(ids_ref, gates_ref, raw_ref, out_ref, in_ref):
-    experts = raw_ref.shape[0] // (2 * CHUNK)
+def mask_kernel(ids_ref, gates_ref, masks_ref):
+    experts = masks_ref.shape[1] // (2 * CHUNK)
     main, even, odd, gate = placed(ids_ref[...], gates_ref[...], experts)
     weight = jnp.where(main, gate, 0.0)
     high = weight.astype(low)
-    rest = (weight - high.astype(full)).astype(low)
-    main1, even1, odd1 = [ones_at(mask).astype(low) for mask in (main, even, odd)]
-    out = contract(raw_ref[:, :384], high, 0, 0) + contract(raw_ref[:, :384], rest, 0, 0)
+    masks_ref[0] = high
+    masks_ref[1] = (weight - high.astype(full)).astype(low)
+    for number, mask in enumerate((main, even, odd)):
+        masks_ref[2 + number] = ones_at(mask).astype(low)
+
+
+def masks_of(ids, gates, rows):
+    return pl.pallas_call(
+        mask_kernel,
+        grid=(1,),
+        out_shape=jax.ShapeDtypeStruct((5, rows, ids.shape[1]), low),
+        compiler_params=small_params(24),
+        cost_estimate=pl.CostEstimate(
+            flops=20 * rows * 128, bytes_accessed=20 * rows * 128, transcendentals=0
+        ),
+    )(ids, gates)
+
+
+def combine_kernel(masks_ref, raw_ref, out_ref, in_ref):
+    out = contract(raw_ref[:, :384], masks_ref[0], 0, 0)
+    out = out + contract(raw_ref[:, :384], masks_ref[1], 0, 0)
     out_ref[...] = out[:QUARTER].astype(low)
-    first = contract(raw_ref[:, 384:512], main1, 0, 0)
-    second = contract(raw_ref[:, 0:256], even1, 0, 0) + contract(raw_ref[:, 256:512], odd1, 0, 0)
+    first = contract(raw_ref[:, 384:512], masks_ref[2], 0, 0)
+    second = contract(raw_ref[:, 0:256], masks_ref[3], 0, 0)
+    second = second + contract(raw_ref[:, 256:512], masks_ref[4], 0, 0)
     in_ref[0:128, :] = first.astype(low)
     in_ref[128:QUARTER, :] = second[: QUARTER - 128].astype(low)
 
 
-def combine(ids, gates, raw):
+def combine(masks, raw):
     rows = raw.shape[0]
     return pl.pallas_call(
         combine_kernel,
-        in_specs=in_vmem(3),
+        in_specs=in_vmem(2),
         out_specs=in_vmem(2),
-        out_shape=[jax.ShapeDtypeStruct((QUARTER, ids.shape[1]), low)] * 2,
+        out_shape=[jax.ShapeDtypeStruct((QUARTER, masks.shape[2]), low)] * 2,
         compiler_params=small_params(),
         cost_estimate=pl.CostEstimate(
             flops=8 * rows * 128 * 512, bytes_accessed=2 * rows * 512, transcendentals=0
         ),
-    )(ids, gates, raw)
+    )(masks, raw)
 
 
 def selection():
@@ -150,6 +169,16 @@
     rest = same & (row == SLOTS + slot // 2)
     masks = (main, rest & (slot % 2 == 0), rest & (slot % 2 == 1))
     return jnp.concatenate([ones_at(mask).astype(low) for mask in masks], axis=0)
+
+
+def first_kernel(core_ref, mine_ref, other_ref, own_ref, gate_ref, up_ref, down_ref, *refs):
+    w_ref = refs[6]
+    hidden = own_ref.shape[1]
+    for number, peer in enumerate((gate_ref, up_ref, down_ref)):
+        w_ref[number] = jnp.zeros(w_ref.shape[1:], low)
+        w_ref[number, :hidden] = own_ref[number]
+        w_ref[number, PEER : PEER + hidden] = peer[0]
+    expert_kernel(core_ref, mine_ref, other_ref, w_ref, *refs[:6], *refs[7:])
 
 
 def expert_kernel(
@@ -224,27 +253,30 @@
         ).astype(low)
 
 
-def expert(core, mine, other, weights):
+def expert(core, mine, other, weights, scale):
     raw_rows = mine.shape[0]
     count = raw_rows // (2 * CHUNK) * SLOTS
-    hidden, width = weights.shape[1:]
+    hidden, width = 2 * PEER, weights[0].shape[2]
     shape = lambda cols: jax.ShapeDtypeStruct((count, cols), low)
-    return pl.pallas_call(
-        expert_kernel,
-        in_specs=[scalar()] + in_vmem(3),
-        out_specs=in_vmem(6),
-        out_shape=[jax.ShapeDtypeStruct((raw_rows, PIECE), low)] * 2
-        + [shape(width)] * 2
-        + [shape(hidden), shape(2 * hidden)],
+    outs = [jax.ShapeDtypeStruct((raw_rows, PIECE), low)] * 2 + [shape(width)] * 2
+    outs += [shape(hidden), shape(2 * hidden)]
+    first = len(weights) > 1
+    if first:
+        outs += [jax.ShapeDtypeStruct((3, hidden, width), low)]
+    return pl.pallas_call(
+        first_kernel if first else expert_kernel,
+        in_specs=[scalar()] + in_vmem(2 + len(weights)),
+        out_specs=in_vmem(len(outs)),
+        out_shape=outs,
         scratch_shapes=[pltpu.VMEM((2, 2, count, 2 * STRIDE), low)]
         + [pltpu.VMEM((count, width), low)] * 2,
         compiler_params=small_params(20),
         cost_estimate=pl.CostEstimate(
-            flops=12 * count * width * hidden,
-            bytes_accessed=16 * count * width,
+            flops=scale * count * width * hidden,
+            bytes_accessed=scale * count * width,
             transcendentals=count * hidden,
         ),
-    )(core, mine, other, weights)
+    )(core, mine, other, *weights)
 
 
 def weight_products(refs, lanes):
@@ -272,11 +304,13 @@
 
 
 def weight_grads(first, second, start, hidden, width, dtype):
+    shape = jax.ShapeDtypeStruct((hidden, width), dtype)
+    outs = [shape] * 3
     return pl.pallas_call(
         functools.partial(product_kernel, start),
         in_specs=in_vmem(8),
-        out_specs=in_vmem(3),
-        out_shape=[jax.ShapeDtypeStruct((hidden, width), dtype)] * 3,
+        out_specs=in_vmem(len(outs)),
+        out_shape=outs,
         compiler_params=small_params(18),
         cost_estimate=pl.CostEstimate(
             flops=12 * first[2].shape[0] * width * hidden,
@@ -287,21 +321,23 @@
 
 
 def total_kernel(*refs):
-    for number in range(3):
-        own, got, out = refs[number], refs[3 + number], refs[6 + number]
+    count = len(refs) // 3
+    for own, got, out in zip(refs[:count], refs[count : 2 * count], refs[2 * count :]):
         out[...] = (own[...] + got[...].astype(full)).astype(low)
 
 
-def weight_totals(owns, got):
+def weight_totals(owns, got, scale):
     hidden, width = owns[0].shape
     return pl.pallas_call(
         total_kernel,
-        in_specs=in_vmem(6),
-        out_specs=in_vmem(3),
-        out_shape=[jax.ShapeDtypeStruct((hidden, width), low)] * 3,
+        in_specs=in_vmem(2 * len(owns)),
+        out_specs=in_vmem(len(owns)),
+        out_shape=[jax.ShapeDtypeStruct((hidden, width), low)] * len(owns),
         compiler_params=small_params(16),
         cost_estimate=pl.CostEstimate(
-            flops=3 * hidden * width, bytes_accessed=24 * hidden * width, transcendentals=0
+            flops=scale * hidden * width,
+            bytes_accessed=scale * hidden * width,
+            transcendentals=0,
         ),
     )(*owns, *got)
 
@@ -329,28 +365,24 @@
     ]
     packed = pack(ids, gates, tokens.T, out_grad.T, exp_count * CHUNK)
     mine = by_parity(packed, exp_count)
-    mine, peer_gate = lax.optimization_barrier((mine, peer_gate))
+    masks = masks_of(ids, gates, exp_count * CHUNK)
+    own_weights = jnp.concatenate([gate_weight, up_weight, down_weight], axis=0)
+    mine, peer_gate, peer_up, masks, own_weights = lax.optimization_barrier(
+        (mine, peer_gate, peer_up, masks, own_weights)
+    )
     next_mine = exchanged(mine, "exp", 1)
     beside = exchanged(mine, "rep", 1)
-    gap = jnp.zeros((PEER - hidden, width), low)
-    weights = jnp.stack(
-        [
-            jnp.concatenate([own[0], gap, peer[0], gap], axis=0)
-            for own, peer in (
-                (gate_weight, peer_gate),
-                (up_weight, peer_up),
-                (down_weight, peer_down),
-            )
-        ]
-    )
-    mine, beside, next_mine, weights = lax.optimization_barrier(
-        (mine, beside, next_mine, weights)
-    )
+    weights = (own_weights, peer_gate, peer_up, peer_down)
     next_beside = exchanged(next_mine, "rep", 1)
-    keep_a, send_a, tok_a, grad_a, hid_a, both_a = expert(core, mine, beside, weights)
+    keep_a, send_a, tok_a, grad_a, hid_a, both_a, wide = expert(
+        core, mine, beside, weights, 100000
+    )
     got_a = exchanged(send_a, "rep", 1)
+    sum_a = (keep_a.astype(full) + got_a.astype(full)).astype(low)
     next_beside, send_a = lax.optimization_barrier((next_beside, send_a))
-    keep_b, send_b, tok_b, grad_b, hid_b, both_b = expert(core, next_mine, next_beside, weights)
+    keep_b, send_b, tok_b, grad_b, hid_b, both_b = expert(
+        core, next_mine, next_beside, (wide,), 12
+    )
     got_b = exchanged(send_b, "rep", 1)
     rows_a, rows_b = (hid_a, both_a, tok_a, grad_a), (hid_b, both_b, tok_b, grad_b)
     peers = weight_grads(rows_a, rows_b, PEER, hidden, width, low)
@@ -359,16 +391,14 @@
     got_sum = exchanged(sum_b, "exp", 1)
     got_peers = [exchanged(part, "rep", 2) for part in peers]
     owns = weight_grads(rows_a, rows_b, 0, hidden, width, full)
-    total = (
-        keep_a.astype(full) + got_a.astype(full) + got_sum.astype(full)
-    ).astype(low)
-    total, owns, *got_peers[:2] = lax.optimization_barrier((total, owns, *got_peers[:2]))
+    early = []
+    total = (sum_a.astype(full) + got_sum.astype(full)).astype(low)
+    total, owns = lax.optimization_barrier((total, owns))
     returned = by_parity(total, exp_count)
-    gate_grad, up_grad, down_grad = weight_totals(owns, got_peers)
-    returned, gate_grad, up_grad, down_grad = lax.optimization_barrier(
-        (returned, gate_grad, up_grad, down_grad)
-    )
-    layer_out, input_grad = combine(ids, gates, returned)
+    late = weight_totals(owns[0:], got_peers[0:], 1000000)
+    returned, *late = lax.optimization_barrier((returned, *late))
+    gate_grad, up_grad, down_grad = [*early, *late]
+    layer_out, input_grad = combine(masks, returned)
     return (layer_out.T, input_grad.T, gate_grad[None], up_grad[None], down_grad[None])
 
 

time: 193 us -> 201 us (1.041)
  waiting for transfers between devices: 77 us -> 84.5 us
  Pallas kernels: 27.3 us -> 32.5 us
  other arithmetic: 6.74 us -> 3.32 us
    all_to_all x2, waiting for transfers between devices: 9.49 us -> 24.2 us  [by_parity(): lax.all_to_all(chunks, ('rep', 'exp'), split_axis=0, concat_axis=0, axis_...]
    ppermute x12, waiting for transfers between devices: 67.5 us -> 60.3 us  [exchanged(): return lax.ppermute(block, axis, [(i, i ^ distance) for i in range(count)])]
    another operation x2 -> x0, other arithmetic: 5.04 us -> none  [local(): jnp.stack([jnp.concatenate([own[0], gap, peer[0], gap], axis=0) for own,...]
    pallas_call x4 -> x5, Pallas kernels: 20.2 us -> 24.6 us  [the longest x2 18.1 us: expert(): pl.pallas_call(first_kernel if first else expert_kernel, in_specs=[scalar...]
  transfers between devices with their start and end apart: 14 -> 14, of which waited for: 7 -> 6; matrix products, arithmetic and copies ran while one was open for 4% -> 2% of each run, Pallas kernels for 7% -> 9%
where the time goes in v6:
time: 201 us; the launch traced here: 200 us
  waiting for transfers between devices  84.5 us (42%)
  starting transfers between devices  72.5 us (36%)
  Pallas kernels  32.5 us (16%)
  local copies, waits for them, and re-layouts  6.24 us (3%)
  other arithmetic  3.32 us (2%)
    ppermute x12, waiting for transfers between devices, exchanged(): return lax.ppermute(block, axis, [(i, i ^ distance) for i in range(count)])  60.3 us
    ppermute x12, starting transfers between devices, exchanged(): return lax.ppermute(block, axis, [(i, i ^ distance) for i in range(count)])  37 us
    all_to_all x2, starting transfers between devices, by_parity(): lax.all_to_all(chunks, ('rep', 'exp'), split_axis=0, concat_axis=0, axis_...  35.5 us
    all_to_all x2, waiting for transfers between devices, by_parity(): lax.all_to_all(chunks, ('rep', 'exp'), split_axis=0, concat_axis=0, axis_...  24.2 us
    pallas_call x2, Pallas kernels, expert(): pl.pallas_call(first_kernel if first else expert_kernel, in_specs=[scalar...  18.1 us
    unnamed x20, local copies, waits for them, and re-layouts  6.24 us
    pallas_call x2, Pallas kernels, weight_grads(): pl.pallas_call(functools.partial(product_kernel, start), in_specs=in_vmem...  4.86 us
  transfers between devices with their start and end apart: 14, of which 6 were waited for; matrix products, arithmetic and copies ran while one was open for 2% of the time, Pallas kernels for 9%

profile of v6, /device:TPU:1, one launch (start us, length us, event | category | flops | bytes accessed | tf_op | source)
XLA Modules:
  0.0 199.9 jit_solution(12731437780059830324)
XLA Ops:
  0.6 0.0 copy-start
  0.6 0.0 copy-start.1
  0.7 3.0 %shard_map.110 = bf16[1024,512]{1,0:T(8,128)(2,1)} custom-call(s32[4,128]{1,0:T(4,128)} %bitcast.14, f32[4,128]{1,0:T(4,128)} %bitcast.16, bf16[360,128]{1,0:T(8,128)(2,1)} %bitcast.20, bf16[360,128]{1,0:T(8,128)(2,1)} %bitcast.21), custom_call_target="tpu_custom_call" | custom-call | flops 536870912 | bytes 1048576 | tf_op jit(solution)/shard_map/pallas_call | solution.py:103
  3.7 21.3 %all-to-all-start = ((bf16[128,8,512]{2,1,0:T(8,128)(2,1)}), bf16[128,8,512]{2,1,0:T(8,128)(2,1)}, u32[]{:S(2)}, u32[]{:S(2)}) async-start(bf16[128,8,512]{2,1,0:T(8,128)(2,1)} %bitcast.19), calls=%async_computation | async-start | bytes 2097152 | tf_op jit(solution)/shard_map/all_to_all | solution.py:352
  25.0 4.2 %collective-permute-start = (bf16[1,180,1440]{2,1,0:T(8,128)(2,1)}, bf16[1,180,1440]{2,1,0:T(8,128)(2,1)S(1)}, u32[]{:S(2)}, u32[]{:S(2)}) collective-permute-start(bf16[1,180,1440]{2,1,0:T(8,128)(2,1)} %param.11), channel_id=1, source_target_pairs={{0,256},{128,384},{256,0},{384,128},{1,257},{129,385},{257,1},{385... | collective-permute-start | bytes 1555208 | tf_op jit(solution)/shard_map/ppermute | solution.py:25
  29.3 2.6 %collective-permute-start.1 = (bf16[1,180,1440]{2,1,0:T(8,128)(2,1)}, bf16[1,180,1440]{2,1,0:T(8,128)(2,1)S(1)}, u32[]{:S(2)}, u32[]{:S(2)}) collective-permute-start(bf16[1,180,1440]{2,1,0:T(8,128)(2,1)} %param.12), channel_id=1, source_target_pairs={{0,256},{128,384},{256,0},{384,128},{1,257},{129,385},{257,1},{385... | collective-permute-start | bytes 1555208 | tf_op jit(solution)/shard_map/ppermute | solution.py:25
  31.8 0.0 copy-done
  31.8 0.0 copy-done.1
  31.9 1.0 shard_map.111.masks_ref
  32.9 1.6 pad_maximum_fusion.own_ref
  34.5 14.0 %collective-permute-done.gate_ref = bf16[1,180,1440]{2,1,0:T(8,128)(2,1)S(1)} collective-permute-done((bf16[1,180,1440]{2,1,0:T(8,128)(2,1)}, bf16[1,180,1440]{2,1,0:T(8,128)(2,1)S(1)}, u32[]{:S(2)}, u32[]{:S(2)}) %collective-permute-start) | collective-permute-done | bytes 518432 | tf_op jit(solution)/shard_map/ppermute | solution.py:25
  48.4 0.0 copy-start.6
  48.4 0.8 copy-done.6
  49.3 15.7 %collective-permute-done.1.up_ref = bf16[1,180,1440]{2,1,0:T(8,128)(2,1)S(1)} collective-permute-done((bf16[1,180,1440]{2,1,0:T(8,128)(2,1)}, bf16[1,180,1440]{2,1,0:T(8,128)(2,1)S(1)}, u32[]{:S(2)}, u32[]{:S(2)}) %collective-permute-start.1) | collective-permute-done | bytes 518432 | tf_op jit(solution)/shard_map/ppermute | solution.py:25
  64.9 0.0 copy-start.8
  64.9 0.8 copy-done.8
  65.7 0.0 all-to-all-done
  65.7 2.5 %collective-permute-start.5 = (bf16[1024,512]{1,0:T(8,128)(2,1)}, bf16[1024,512]{1,0:T(8,128)(2,1)}, u32[]{:S(2)}, u32[]{:S(2)}) collective-permute-start(bf16[1024,512]{1,0:T(8,128)(2,1)} %bitcast.5.mine_ref), channel_id=1, source_target_pairs={{0,1},{1,0},{2,3},{3,2},{4,5},{5,4},{6,7},{7,6},{8,9},{9,8},{10,11... | collective-permute-start | bytes 3145736 | tf_op jit(solution)/shard_map/ppermute | solution.py:25
  68.2 3.6 %collective-permute-start.2 = (bf16[1024,512]{1,0:T(8,128)(2,1)}, bf16[1024,512]{1,0:T(8,128)(2,1)}, u32[]{:S(2)}, u32[]{:S(2)}) collective-permute-start(bf16[1024,512]{1,0:T(8,128)(2,1)} %bitcast.5.mine_ref), channel_id=1, source_target_pairs={{0,128},{128,0},{256,384},{384,256},{1,129},{129,1},{257,385},{385... | collective-permute-start | bytes 3145736 | tf_op jit(solution)/shard_map/ppermute | solution.py:25
  71.8 3.2 %collective-permute-start.3 = (bf16[1,180,1440]{2,1,0:T(8,128)(2,1)}, bf16[1,180,1440]{2,1,0:T(8,128)(2,1)}, u32[]{:S(2)}, u32[]{:S(2)}) collective-permute-start(bf16[1,180,1440]{2,1,0:T(8,128)(2,1)} %param.13), channel_id=1, source_target_pairs={{0,256},{128,384},{256,0},{384,128},{1,257},{129,385},{257,1},{385... | collective-permute-start | bytes 1555208 | tf_op jit(solution)/shard_map/ppermute | solution.py:25
  75.0 16.1 %collective-permute-done.5.mine_ref = bf16[1024,512]{1,0:T(8,128)(2,1)} collective-permute-done((bf16[1024,512]{1,0:T(8,128)(2,1)}, bf16[1024,512]{1,0:T(8,128)(2,1)}, u32[]{:S(2)}, u32[]{:S(2)}) %collective-permute-start.5) | collective-permute-done | bytes 1048608 | tf_op jit(solution)/shard_map/ppermute | solution.py:25
  91.1 4.3 %collective-permute-start.6 = (bf16[1024,512]{1,0:T(8,128)(2,1)}, bf16[1024,512]{1,0:T(8,128)(2,1)}, u32[]{:S(2)}, u32[]{:S(2)}) collective-permute-start(bf16[1024,512]{1,0:T(8,128)(2,1)} %collective-permute-done.5.mine_ref), channel_id=1, source_target_pairs={{0,128},{128,0},{256,384},{384,256},{1,129},{129,1},{257,385},{385... | collective-permute-start | bytes 3145736 | tf_op jit(solution)/shard_map/ppermute | solution.py:25
  95.4 0.0 collective-permute-done.3.down_ref
  95.4 0.0 collective-permute-done.2.other_ref
  95.4 0.0 copy-start.7
  95.4 1.0 copy-done.7
  96.5 0.0 copy-start.9
  96.5 1.1 copy-done.9
  97.6 9.3 %shard_map.112 = (bf16[1024,512]{1,0:T(8,128)(2,1)S(1)}, bf16[1024,512]{1,0:T(8,128)(2,1)S(1)}, bf16[320,1440]{1,0:T(8,128)(2,1)S(1)}, bf16[320,1440]{1,0:T(8,12...) custom-call(s32[1]{0:T(128)} %bitcast.6.core_ref, ...), custom_call_target="tpu_custom_call" | custom-call | flops 23592960000000 | bytes 46080000000 | tf_op jit(solution)/shard_map/pallas_call | solution.py:266
  106.9 0.0 collective-permute-done.6.other_ref
  106.9 8.7 %shard_map.113 = (bf16[1024,512]{1,0:T(8,128)(2,1)S(1)}, bf16[1024,512]{1,0:T(8,128)(2,1)S(1)}, bf16[320,1440]{1,0:T(8,128)(2,1)S(1)}, bf16[320,1440]{1,0:T(8,12...) custom-call(s32[1]{0:T(128)} %bitcast.6.core_ref, ...), custom_call_target="tpu_custom_call" | custom-call | flops 2831155200 | bytes 5529600 | tf_op jit(solution)/shard_map/pallas_call | solution.py:266
  115.6 1.9 collective-permute-start.7
  117.6 2.4 %collective-permute-start.4 = (bf16[1024,512]{1,0:T(8,128)(2,1)S(1)}, bf16[1024,512]{1,0:T(8,128)(2,1)S(1)}, u32[]{:S(2)}, u32[]{:S(2)}) collective-permute-start(bf16[1024,512]{1,0:T(8,128)(2,1)S(1)} %get-tuple-element.53), channel_id=1, source_target_pairs={{0,128},{128,0},{256,384},{384,256},{1,129},{129,1},{257,385},{385... | collective-permute-start | bytes 3145736 | tf_op jit(solution)/shard_map/ppermute | solution.py:25
  120.0 2.8 %shard_map.114 = (bf16[180,1440]{1,0:T(8,128)(2,1)S(1)}, bf16[180,1440]{1,0:T(8,128)(2,1)}, bf16[180,1440]{1,0:T(8,128)(2,1)}) custom-call(bf16[320,512]{1,0:T(8,128)(2,1)S(1)} %get-tuple-element.58.refs_0_, bf16[320,1024]{1,0:T(8,128)(2,1)S(1)} %get-tuple-element.59.refs_1_, bf16[320,1440]{1,0:T(8,128)(2,1)S(1)} %get-tuple-element.60.refs_2_, ...), custom_call_target="tpu_custom_call" | custom-call | flops 995328000 | bytes 7372800 | tf_op jit(solution)/shard_map/pallas_call | solution.py:309
  122.8 0.0 collective-permute-done.7
  122.8 0.3 add_convert_fusion.1
  123.1 2.5 %collective-permute-start.8 = (bf16[1024,512]{1,0:T(8,128)(2,1)S(1)}, bf16[1024,512]{1,0:T(8,128)(2,1)S(1)}, u32[]{:S(2)}, u32[]{:S(2)}) collective-permute-start(bf16[1024,512]{1,0:T(8,128)(2,1)S(1)} %add_convert_fusion.1), channel_id=1, source_target_pairs={{0,1},{1,0},{2,3},{3,2},{4,5},{5,4},{6,7},{7,6},{8,9},{9,8},{10,11... | collective-permute-start | bytes 3145736 | tf_op jit(solution)/shard_map/ppermute | solution.py:25
  125.6 3.1 %collective-permute-start.10 = (bf16[180,1440]{1,0:T(8,128)(2,1)}, bf16[180,1440]{1,0:T(8,128)(2,1)}, u32[]{:S(2)}, u32[]{:S(2)}) collective-permute-start(bf16[180,1440]{1,0:T(8,128)(2,1)} %get-tuple-element.78), channel_id=1, source_target_pairs={{0,256},{128,384},{256,0},{384,128},{1,257},{129,385},{257,1},{385... | collective-permute-start | bytes 1555208 | tf_op jit(solution)/shard_map/ppermute | solution.py:25
  128.7 3.7 %collective-permute-start.11 = (bf16[180,1440]{1,0:T(8,128)(2,1)}, bf16[180,1440]{1,0:T(8,128)(2,1)}, u32[]{:S(2)}, u32[]{:S(2)}) collective-permute-start(bf16[180,1440]{1,0:T(8,128)(2,1)} %get-tuple-element.79), channel_id=1, source_target_pairs={{0,256},{128,384},{256,0},{384,128},{1,257},{129,385},{257,1},{385... | collective-permute-start | bytes 1555208 | tf_op jit(solution)/shard_map/ppermute | solution.py:25
  132.4 3.1 %collective-permute-start.9 = (bf16[180,1440]{1,0:T(8,128)(2,1)S(1)}, bf16[180,1440]{1,0:T(8,128)(2,1)}, u32[]{:S(2)}, u32[]{:S(2)}) collective-permute-start(bf16[180,1440]{1,0:T(8,128)(2,1)S(1)} %get-tuple-element.77), channel_id=1, source_target_pairs={{0,256},{128,384},{256,0},{384,128},{1,257},{129,385},{257,1},{385... | collective-permute-start | bytes 1555208 | tf_op jit(solution)/shard_map/ppermute | solution.py:25
  135.5 2.0 %shard_map.115 = (f32[180,1440]{1,0:T(8,128)S(1)}, f32[180,1440]{1,0:T(8,128)S(1)}, f32[180,1440]{1,0:T(8,128)S(1)}) custom-call(bf16[320,512]{1,0:T(8,128)(2,1)S(1)} %get-tuple-element.58.refs_0_, bf16[320,1024]{1,0:T(8,128)(2,1)S(1)} %get-tuple-element.59.refs_1_, bf16[320,1440]{1,0:T(8,128)(2,1)S(1)} %get-tuple-element.60.refs_2_, ...), custom_call_target="tpu_custom_call" | custom-call | flops 995328000 | bytes 7372800 | tf_op jit(solution)/shard_map/pallas_call | solution.py:309
  137.5 0.0 copy-start.2
  137.5 0.0 copy-start.4
  137.5 0.0 collective-permute-done.4
  137.5 12.4 %collective-permute-done.8 = bf16[1024,512]{1,0:T(8,128)(2,1)S(1)} collective-permute-done((bf16[1024,512]{1,0:T(8,128)(2,1)S(1)}, bf16[1024,512]{1,0:T(8,128)(2,1)S(1)}, u32[]{:S(2)}, u32[]{:S(2)}) %collective-permute-start.8) | collective-permute-done | bytes 1048608 | tf_op jit(solution)/shard_map/ppermute | solution.py:25
  149.9 1.4 add_convert_fusion
  151.3 0.0 copy-done.2
  151.3 0.0 copy-done.4
  151.3 14.1 %all-to-all-start.1 = ((bf16[128,8,512]{2,1,0:T(8,128)(2,1)}), bf16[128,8,512]{2,1,0:T(8,128)(2,1)}, u32[]{:S(2)}, u32[]{:S(2)}) async-start(bf16[128,8,512]{2,1,0:T(8,128)(2,1)} %bitcast.18), calls=%async_computation.1 | async-start | bytes 2097152 | tf_op jit(solution)/shard_map/all_to_all | solution.py:352
  165.5 0.0 collective-permute-done.10.refs_4_
  165.5 0.0 collective-permute-done.11.refs_5_
  165.5 2.2 %collective-permute-done.9.refs_3_ = bf16[180,1440]{1,0:T(8,128)(2,1)} collective-permute-done((bf16[180,1440]{1,0:T(8,128)(2,1)S(1)}, bf16[180,1440]{1,0:T(8,128)(2,1)}, u32[]{:S(2)}, u32[]{:S(2)}) %collective-permute-start.9) | collective-permute-done | bytes 518432 | tf_op jit(solution)/shard_map/ppermute | solution.py:25
  167.7 0.0 copy-start.3
  167.7 1.3 copy-done.3
  168.9 0.0 copy-start.5
  168.9 1.3 copy-done.5
  170.2 2.7 %shard_map.116 = (bf16[180,1440]{1,0:T(8,128)(2,1)}, bf16[180,1440]{1,0:T(8,128)(2,1)}, bf16[180,1440]{1,0:T(8,128)(2,1)}) custom-call(f32[180,1440]{1,0:T(8,128)S(1)} %get-tuple-element.74.refs_0_, f32[180,1440]{1,0:T(8,128)S(1)} %copy-done.3, f32[180,1440]{1,0:T(8,128)S(1)} %copy-done.5, bf16[180,1440]{1,0:T(8,128)(2,1)} %collective-permute-done.9.refs_3_, ...), custom_call_target="tpu_custom_call" | custom-call | flops 259199991808 | bytes 259199991808 | tf_op jit(solution)/shard_map/pallas_call | solution.py:331
  172.9 24.2 %all-to-all-done.1 = bf16[128,8,512]{2,1,0:T(8,128)(2,1)} async-done(((bf16[128,8,512]{2,1,0:T(8,128)(2,1)}), bf16[128,8,512]{2,1,0:T(8,128)(2,1)}, u32[]{:S(2)}, u32[]{:S(2)}) %all-to-all-start.1) | async-done | bytes 1048608 | tf_op jit(solution)/shard_map/all_to_all | solution.py:352
  197.1 2.9 %shard_map.117 = (bf16[360,128]{1,0:T(8,128)(2,1)}, bf16[360,128]{1,0:T(8,128)(2,1)}) custom-call(bf16[5,1024,128]{2,1,0:T(8,128)(2,1)S(1)} %shard_map.111.masks_ref, bf16[1024,512]{1,0:T(8,128)(2,1)} %bitcast.8.raw_ref), custom_call_target="tpu_custom_call" | custom-call | flops 536870912 | bytes 1048576 | tf_op jit(solution)/shard_map/pallas_call | solution.py:151
Async XLA Ops:
  0.6 31.2 %copy-start = (s32[128,4]{0,1:T(4,128)S(1)}, s32[128,4]{0,1:T(4,128)}, u32[]{:S(2)}) copy-start(s32[128,4]{0,1:T(4,128)} %param.8) | copy-start | bytes 6148
  0.6 31.2 %copy-start.1 = (f32[128,4]{0,1:T(4,128)S(1)}, f32[128,4]{0,1:T(4,128)}, u32[]{:S(2)}) copy-start(f32[128,4]{0,1:T(4,128)} %param.9) | copy-start | bytes 6148
  3.7 62.1 %all-to-all-start = ((bf16[128,8,512]{2,1,0:T(8,128)(2,1)}), bf16[128,8,512]{2,1,0:T(8,128)(2,1)}, u32[]{:S(2)}, u32[]{:S(2)}) async-start(bf16[128,8,512]{2,1,0:T(8,128)(2,1)} %bitcast.19), calls=%async_computation | async-start | bytes 2097152 | tf_op jit(solution)/shard_map/all_to_all | solution.py:352
  25.0 23.4 %collective-permute-start = (bf16[1,180,1440]{2,1,0:T(8,128)(2,1)}, bf16[1,180,1440]{2,1,0:T(8,128)(2,1)S(1)}, u32[]{:S(2)}, u32[]{:S(2)}) collective-permute-start(bf16[1,180,1440]{2,1,0:T(8,128)(2,1)} %param.11), channel_id=1, source_target_pairs={{0,256},{128,384},{256,0},{384,128},{1,257},{129,385},{257,1},{385... | collective-permute-start | bytes 1555208 | tf_op jit(solution)/shard_map/ppermute | solution.py:25
  29.3 35.7 %collective-permute-start.1 = (bf16[1,180,1440]{2,1,0:T(8,128)(2,1)}, bf16[1,180,1440]{2,1,0:T(8,128)(2,1)S(1)}, u32[]{:S(2)}, u32[]{:S(2)}) collective-permute-start(bf16[1,180,1440]{2,1,0:T(8,128)(2,1)} %param.12), channel_id=1, source_target_pairs={{0,256},{128,384},{256,0},{384,128},{1,257},{129,385},{257,1},{385... | collective-permute-start | bytes 1555208 | tf_op jit(solution)/shard_map/ppermute | solution.py:25
  48.4 0.8 copy-start.6
  64.9 0.8 copy-start.8
  65.7 25.4 %collective-permute-start.5 = (bf16[1024,512]{1,0:T(8,128)(2,1)}, bf16[1024,512]{1,0:T(8,128)(2,1)}, u32[]{:S(2)}, u32[]{:S(2)}) collective-permute-start(bf16[1024,512]{1,0:T(8,128)(2,1)} %bitcast.5.mine_ref), channel_id=1, source_target_pairs={{0,1},{1,0},{2,3},{3,2},{4,5},{5,4},{6,7},{7,6},{8,9},{9,8},{10,11... | collective-permute-start | bytes 3145736 | tf_op jit(solution)/shard_map/ppermute | solution.py:25
  68.2 27.2 %collective-permute-start.2 = (bf16[1024,512]{1,0:T(8,128)(2,1)}, bf16[1024,512]{1,0:T(8,128)(2,1)}, u32[]{:S(2)}, u32[]{:S(2)}) collective-permute-start(bf16[1024,512]{1,0:T(8,128)(2,1)} %bitcast.5.mine_ref), channel_id=1, source_target_pairs={{0,128},{128,0},{256,384},{384,256},{1,129},{129,1},{257,385},{385... | collective-permute-start | bytes 3145736 | tf_op jit(solution)/shard_map/ppermute | solution.py:25
  71.8 23.6 %collective-permute-start.3 = (bf16[1,180,1440]{2,1,0:T(8,128)(2,1)}, bf16[1,180,1440]{2,1,0:T(8,128)(2,1)}, u32[]{:S(2)}, u32[]{:S(2)}) collective-permute-start(bf16[1,180,1440]{2,1,0:T(8,128)(2,1)} %param.13), channel_id=1, source_target_pairs={{0,256},{128,384},{256,0},{384,128},{1,257},{129,385},{257,1},{385... | collective-permute-start | bytes 1555208 | tf_op jit(solution)/shard_map/ppermute | solution.py:25
  91.1 15.8 %collective-permute-start.6 = (bf16[1024,512]{1,0:T(8,128)(2,1)}, bf16[1024,512]{1,0:T(8,128)(2,1)}, u32[]{:S(2)}, u32[]{:S(2)}) collective-permute-start(bf16[1024,512]{1,0:T(8,128)(2,1)} %collective-permute-done.5.mine_ref), channel_id=1, source_target_pairs={{0,128},{128,0},{256,384},{384,256},{1,129},{129,1},{257,385},{385... | collective-permute-start | bytes 3145736 | tf_op jit(solution)/shard_map/ppermute | solution.py:25
  95.4 1.1 copy-start.7
  96.5 1.1 copy-start.9
  115.6 7.2 %collective-permute-start.7 = (bf16[1024,512]{1,0:T(8,128)(2,1)S(1)}, bf16[1024,512]{1,0:T(8,128)(2,1)S(1)}, u32[]{:S(2)}, u32[]{:S(2)}) collective-permute-start(bf16[1024,512]{1,0:T(8,128)(2,1)S(1)} %get-tuple-element.57), channel_id=1, source_target_pairs={{0,128},{128,0},{256,384},{384,256},{1,129},{129,1},{257,385},{385... | collective-permute-start | bytes 3145736 | tf_op jit(solution)/shard_map/ppermute | solution.py:25
  117.6 20.0 %collective-permute-start.4 = (bf16[1024,512]{1,0:T(8,128)(2,1)S(1)}, bf16[1024,512]{1,0:T(8,128)(2,1)S(1)}, u32[]{:S(2)}, u32[]{:S(2)}) collective-permute-start(bf16[1024,512]{1,0:T(8,128)(2,1)S(1)} %get-tuple-element.53), channel_id=1, source_target_pairs={{0,128},{128,0},{256,384},{384,256},{1,129},{129,1},{257,385},{385... | collective-permute-start | bytes 3145736 | tf_op jit(solution)/shard_map/ppermute | solution.py:25
  123.1 26.8 %collective-permute-start.8 = (bf16[1024,512]{1,0:T(8,128)(2,1)S(1)}, bf16[1024,512]{1,0:T(8,128)(2,1)S(1)}, u32[]{:S(2)}, u32[]{:S(2)}) collective-permute-start(bf16[1024,512]{1,0:T(8,128)(2,1)S(1)} %add_convert_fusion.1), channel_id=1, source_target_pairs={{0,1},{1,0},{2,3},{3,2},{4,5},{5,4},{6,7},{7,6},{8,9},{9,8},{10,11... | collective-permute-start | bytes 3145736 | tf_op jit(solution)/shard_map/ppermute | solution.py:25
  125.6 39.8 %collective-permute-start.10 = (bf16[180,1440]{1,0:T(8,128)(2,1)}, bf16[180,1440]{1,0:T(8,128)(2,1)}, u32[]{:S(2)}, u32[]{:S(2)}) collective-permute-start(bf16[180,1440]{1,0:T(8,128)(2,1)} %get-tuple-element.78), channel_id=1, source_target_pairs={{0,256},{128,384},{256,0},{384,128},{1,257},{129,385},{257,1},{385... | collective-permute-start | bytes 1555208 | tf_op jit(solution)/shard_map/ppermute | solution.py:25
  128.7 36.8 %collective-permute-start.11 = (bf16[180,1440]{1,0:T(8,128)(2,1)}, bf16[180,1440]{1,0:T(8,128)(2,1)}, u32[]{:S(2)}, u32[]{:S(2)}) collective-permute-start(bf16[180,1440]{1,0:T(8,128)(2,1)} %get-tuple-element.79), channel_id=1, source_target_pairs={{0,256},{128,384},{256,0},{384,128},{1,257},{129,385},{257,1},{385... | collective-permute-start | bytes 1555208 | tf_op jit(solution)/shard_map/ppermute | solution.py:25
  132.4 35.2 %collective-permute-start.9 = (bf16[180,1440]{1,0:T(8,128)(2,1)S(1)}, bf16[180,1440]{1,0:T(8,128)(2,1)}, u32[]{:S(2)}, u32[]{:S(2)}) collective-permute-start(bf16[180,1440]{1,0:T(8,128)(2,1)S(1)} %get-tuple-element.77), channel_id=1, source_target_pairs={{0,256},{128,384},{256,0},{384,128},{1,257},{129,385},{257,1},{385... | collective-permute-start | bytes 1555208 | tf_op jit(solution)/shard_map/ppermute | solution.py:25
  137.5 13.8 %copy-start.2 = (f32[180,1440]{1,0:T(8,128)}, f32[180,1440]{1,0:T(8,128)S(1)}, u32[]{:S(2)}) copy-start(f32[180,1440]{1,0:T(8,128)S(1)} %get-tuple-element.75.refs_1_) | copy-start | bytes 3110404
  137.5 13.8 %copy-start.4 = (f32[180,1440]{1,0:T(8,128)}, f32[180,1440]{1,0:T(8,128)S(1)}, u32[]{:S(2)}) copy-start(f32[180,1440]{1,0:T(8,128)S(1)} %get-tuple-element.76.refs_2_) | copy-start | bytes 3110404
  151.3 45.7 %all-to-all-start.1 = ((bf16[128,8,512]{2,1,0:T(8,128)(2,1)}), bf16[128,8,512]{2,1,0:T(8,128)(2,1)}, u32[]{:S(2)}, u32[]{:S(2)}) async-start(bf16[128,8,512]{2,1,0:T(8,128)(2,1)} %bitcast.18), calls=%async_computation.1 | async-start | bytes 2097152 | tf_op jit(solution)/shard_map/all_to_all | solution.py:352
  167.7 1.3 copy-start.3
  168.9 1.3 copy-start.5

commit v7 on v6

--- a/solution.py
+++ b/solution.py
@@ -171,32 +171,20 @@
     return jnp.concatenate([ones_at(mask).astype(low) for mask in masks], axis=0)
 
 
-def first_kernel(core_ref, mine_ref, other_ref, own_ref, gate_ref, up_ref, down_ref, *refs):
-    w_ref = refs[6]
-    hidden = own_ref.shape[1]
-    for number, peer in enumerate((gate_ref, up_ref, down_ref)):
-        w_ref[number] = jnp.zeros(w_ref.shape[1:], low)
-        w_ref[number, :hidden] = own_ref[number]
-        w_ref[number, PEER : PEER + hidden] = peer[0]
-    expert_kernel(core_ref, mine_ref, other_ref, w_ref, *refs[:6], *refs[7:])
-
-
-def expert_kernel(
-    core_ref, mine_ref, other_ref, w_ref,
-    keep_ref, send_ref, tok_ref, grad_ref, hid_ref, both_ref,
-    dense, out_rows, in_rows,
-):
+def raw_places(rows):
+    many, wide, half = GROUP * SLOTS, GROUP * CHUNK, rows // 2
+    for source in range(2):
+        for pair in range(2):
+            for g in range(half // wide):
+                start = pair * half + g * wide
+                yield source, pair, slice(g * many, (g + 1) * many), slice(start, start + wide)
+
+
+def unpack_kernel(core_ref, mine_ref, other_ref, tok_ref, grad_ref, dense):
     core = core_ref[0]
     chosen = selection()
-    many, wide = GROUP * SLOTS, GROUP * CHUNK
-    half = mine_ref.shape[0] // 2
-    places = [
-        (source, pair, slice(g * many, (g + 1) * many), slice(pair * half + g * wide, pair * half + (g + 1) * wide))
-        for source in range(2)
-        for pair in range(2)
-        for g in range(half // wide)
-    ]
-    for source, pair, at, raw_at in places:
+    many = GROUP * SLOTS
+    for source, pair, at, raw_at in raw_places(mine_ref.shape[0]):
         found = contract(chosen, (mine_ref, other_ref)[source][raw_at, :], 1, 0)
         dense[source, pair, at, 0:512] = found[:many].astype(low)
         dense[source, pair, at, 512:768] = (
@@ -214,6 +202,14 @@
                         source, pair, :, STRIDE : STRIDE + QUARTER
                     ]
 
+
+def rows_kernel(
+    core_ref, tok_ref, grad_ref, w_ref, keep_ref, send_ref, hid_ref, both_ref,
+    dense, out_rows, in_rows,
+):
+    core = core_ref[0]
+    chosen = selection()
+    many = GROUP * SLOTS
     tok = tok_ref[...]
     pre_gate = contract(tok, w_ref[0], 1, 1)
     pre_up = contract(tok, w_ref[1], 1, 1)
@@ -241,7 +237,7 @@
                         :, start : start + QUARTER
                     ]
 
-    for source, pair, at, raw_at in places:
+    for source, pair, at, raw_at in raw_places(keep_ref.shape[0]):
         head = contract(chosen[:many], dense[source, pair, at, 0:512], 0, 0)
         tail = dense[source, pair, at, 512:768]
         raw_ref = (keep_ref, send_ref)[source]
@@ -253,30 +249,45 @@
         ).astype(low)
 
 
-def expert(core, mine, other, weights, scale):
-    raw_rows = mine.shape[0]
+def second_kernel(
+    core_ref, mine_ref, other_ref, w_ref,
+    keep_ref, send_ref, hid_ref, both_ref, tok_ref, grad_ref,
+    dense, out_rows, in_rows,
+):
+    unpack_kernel(core_ref, mine_ref, other_ref, tok_ref, grad_ref, dense)
+    rows_kernel(
+        core_ref, tok_ref, grad_ref, w_ref, keep_ref, send_ref, hid_ref, both_ref,
+        dense, out_rows, in_rows,
+    )
+
+
+def expert_call(kernel, core, raw_rows, width, operands, extra, scale):
     count = raw_rows // (2 * CHUNK) * SLOTS
-    hidden, width = 2 * PEER, weights[0].shape[2]
-    shape = lambda cols: jax.ShapeDtypeStruct((count, cols), low)
-    outs = [jax.ShapeDtypeStruct((raw_rows, PIECE), low)] * 2 + [shape(width)] * 2
-    outs += [shape(hidden), shape(2 * hidden)]
-    first = len(weights) > 1
-    if first:
-        outs += [jax.ShapeDtypeStruct((3, hidden, width), low)]
-    return pl.pallas_call(
-        first_kernel if first else expert_kernel,
-        in_specs=[scalar()] + in_vmem(2 + len(weights)),
+    hidden = 2 * PEER
+    row = jax.ShapeDtypeStruct((count, width), low)
+    shapes = {
+        "raw": jax.ShapeDtypeStruct((raw_rows, PIECE), low),
+        "row": row,
+        "hid": jax.ShapeDtypeStruct((count, hidden), low),
+        "both": jax.ShapeDtypeStruct((count, 2 * hidden), low),
+    }
+    names = ["raw", "raw", "hid", "both"] if kernel is not unpack_kernel else []
+    outs = [shapes[name] for name in names + extra]
+    dense = [pltpu.VMEM((2, 2, count, 2 * STRIDE), low)]
+    rows = [pltpu.VMEM((count, width), low)] * 2
+    return pl.pallas_call(
+        kernel,
+        in_specs=[scalar()] + in_vmem(len(operands)),
         out_specs=in_vmem(len(outs)),
         out_shape=outs,
-        scratch_shapes=[pltpu.VMEM((2, 2, count, 2 * STRIDE), low)]
-        + [pltpu.VMEM((count, width), low)] * 2,
+        scratch_shapes=dense + (rows if kernel is not unpack_kernel else []),
         compiler_params=small_params(20),
         cost_estimate=pl.CostEstimate(
             flops=scale * count * width * hidden,
             bytes_accessed=scale * count * width,
             transcendentals=count * hidden,
         ),
-    )(core, mine, other, *weights)
+    )(core, *operands)
 
 
 def weight_products(refs, lanes):
@@ -366,29 +377,42 @@
     packed = pack(ids, gates, tokens.T, out_grad.T, exp_count * CHUNK)
     mine = by_parity(packed, exp_count)
     masks = masks_of(ids, gates, exp_count * CHUNK)
-    own_weights = jnp.concatenate([gate_weight, up_weight, down_weight], axis=0)
-    mine, peer_gate, peer_up, masks, own_weights = lax.optimization_barrier(
-        (mine, peer_gate, peer_up, masks, own_weights)
-    )
+    mine, peer_gate, masks = lax.optimization_barrier((mine, peer_gate, masks))
     next_mine = exchanged(mine, "exp", 1)
     beside = exchanged(mine, "rep", 1)
-    weights = (own_weights, peer_gate, peer_up, peer_down)
+    raw_rows = mine.shape[0]
+    tok_a, grad_a = expert_call(
+        unpack_kernel, core, raw_rows, width, (mine, beside), ["row", "row"], 1
+    )
+    gap = jnp.zeros((PEER - hidden, width), low)
+    wide = jnp.stack(
+        [
+            jnp.concatenate([own[0], gap, peer[0], gap], axis=0)
+            for own, peer in (
+                (gate_weight, peer_gate),
+                (up_weight, peer_up),
+                (down_weight, peer_down),
+            )
+        ]
+    )
+    next_mine, wide, tok_a = lax.optimization_barrier((next_mine, wide, tok_a))
+    keep_a, send_a, hid_a, both_a = expert_call(
+        rows_kernel, core, raw_rows, width, (tok_a, grad_a, wide), [], 12
+    )
     next_beside = exchanged(next_mine, "rep", 1)
-    keep_a, send_a, tok_a, grad_a, hid_a, both_a, wide = expert(
-        core, mine, beside, weights, 100000
-    )
-    got_a = exchanged(send_a, "rep", 1)
-    sum_a = (keep_a.astype(full) + got_a.astype(full)).astype(low)
     next_beside, send_a = lax.optimization_barrier((next_beside, send_a))
-    keep_b, send_b, tok_b, grad_b, hid_b, both_b = expert(
-        core, next_mine, next_beside, (wide,), 12
+    keep_b, send_b, hid_b, both_b, tok_b, grad_b = expert_call(
+        second_kernel, core, raw_rows, width, (next_mine, next_beside, wide), ["row", "row"], 12
     )
     got_b = exchanged(send_b, "rep", 1)
     rows_a, rows_b = (hid_a, both_a, tok_a, grad_a), (hid_b, both_b, tok_b, grad_b)
     peers = weight_grads(rows_a, rows_b, PEER, hidden, width, low)
     got_b, *peers = lax.optimization_barrier((got_b, *peers))
     sum_b = (keep_b.astype(full) + got_b.astype(full)).astype(low)
+    sum_b, send_a = lax.optimization_barrier((sum_b, send_a))
     got_sum = exchanged(sum_b, "exp", 1)
+    got_a = exchanged(send_a, "rep", 1)
+    sum_a = (keep_a.astype(full) + got_a.astype(full)).astype(low)
     got_peers = [exchanged(part, "rep", 2) for part in peers]
     owns = weight_grads(rows_a, rows_b, 0, hidden, width, full)
     early = []

time: 201 us -> 187 us (0.930)
  starting transfers between devices: 72.5 us -> 65.5 us
  local copies, waits for them, and re-layouts: 6.24 us -> 2.55 us
  Pallas kernels: 32.5 us -> 29.8 us
    ppermute x12, waiting for transfers between devices: 60.3 us -> 51.2 us  [exchanged(): return lax.ppermute(block, axis, [(i, i ^ distance) for i in range(count)])]
    all_to_all x2, waiting for transfers between devices: 24.2 us -> 31.7 us  [by_parity(): lax.all_to_all(chunks, ('rep', 'exp'), split_axis=0, concat_axis=0, axis_...]
    all_to_all x2, starting transfers between devices: 35.5 us -> 30.8 us  [by_parity(): lax.all_to_all(chunks, ('rep', 'exp'), split_axis=0, concat_axis=0, axis_...]
    unnamed x20 -> x14, local copies, waits for them, and re-layouts: 6.24 us -> 2.53 us
    another operation x0 -> x2, other arithmetic: none -> 3.14 us  [local(): jnp.stack([jnp.concatenate([own[0], gap, peer[0], gap], axis=0) for own,...]
    ppermute x12, starting transfers between devices: 37 us -> 34.7 us  [exchanged(): return lax.ppermute(block, axis, [(i, i ^ distance) for i in range(count)])]
    pallas_call x2 -> x3, Pallas kernels: 18.1 us -> 16 us  [expert_call(): pl.pallas_call(kernel, in_specs=[scalar()] + in_vmem(len(operands)), out_...]
  transfers between devices with their start and end apart: 14 -> 14, of which waited for: 6 -> 9; matrix products, arithmetic and copies ran while one was open for 2% -> 2% of each run, Pallas kernels for 9% -> 8%
where the time goes in v7:
time: 187 us
  waiting for transfers between devices  82.9 us (44%)
  starting transfers between devices  65.5 us (35%)
  Pallas kernels  29.8 us (16%)
  other arithmetic  4.87 us (3%)
  local copies, waits for them, and re-layouts  2.55 us (1%)
    ppermute x12, waiting for transfers between devices, exchanged(): return lax.ppermute(block, axis, [(i, i ^ distance) for i in range(count)])  51.2 us
    ppermute x12, starting transfers between devices, exchanged(): return lax.ppermute(block, axis, [(i, i ^ distance) for i in range(count)])  34.7 us
    all_to_all x2, waiting for transfers between devices, by_parity(): lax.all_to_all(chunks, ('rep', 'exp'), split_axis=0, concat_axis=0, axis_...  31.7 us
    all_to_all x2, starting transfers between devices, by_parity(): lax.all_to_all(chunks, ('rep', 'exp'), split_axis=0, concat_axis=0, axis_...  30.8 us
    pallas_call x3, Pallas kernels, expert_call(): pl.pallas_call(kernel, in_specs=[scalar()] + in_vmem(len(operands)), out_...  16 us
    pallas_call x2, Pallas kernels, weight_grads(): pl.pallas_call(functools.partial(product_kernel, start), in_specs=in_vmem...  4.27 us
  transfers between devices with their start and end apart: 14, of which 9 were waited for; matrix products, arithmetic and copies ran while one was open for 2% of the time, Pallas kernels for 8%

profile of v7, /device:TPU:1, one launch (start us, length us, event | category | flops | bytes accessed | tf_op | source)
XLA Modules:
  0.0 186.6 jit_solution(12666252312485124341)
XLA Ops:
  0.6 0.0 copy-start.1
  0.6 0.0 copy-start
  0.7 0.0 copy-start.6
  0.7 3.1 %shard_map.110 = bf16[1024,512]{1,0:T(8,128)(2,1)} custom-call(s32[4,128]{1,0:T(4,128)} %bitcast.29, f32[4,128]{1,0:T(4,128)} %bitcast.31, bf16[360,128]{1,0:T(8,128)(2,1)} %bitcast.36, bf16[360,128]{1,0:T(8,128)(2,1)} %bitcast.37), custom_call_target="tpu_custom_call" | custom-call | flops 536870912 | bytes 1048576 | tf_op jit(solution)/shard_map/pallas_call | solution.py:103
  3.7 20.8 %all-to-all-start = ((bf16[128,8,512]{2,1,0:T(8,128)(2,1)}), bf16[128,8,512]{2,1,0:T(8,128)(2,1)S(1)}, u32[]{:S(2)}, u32[]{:S(2)}) async-start(bf16[128,8,512]{2,1,0:T(8,128)(2,1)} %bitcast.34), calls=%async_computation | async-start | bytes 2097152 | tf_op jit(solution)/shard_map/all_to_all | solution.py:363
  24.6 0.0 copy-done.6
  24.6 4.3 %collective-permute-start = (bf16[1,180,1440]{2,1,0:T(8,128)(2,1)S(1)}, bf16[1,180,1440]{2,1,0:T(8,128)(2,1)}, u32[]{:S(2)}, u32[]{:S(2)}) collective-permute-start(bf16[1,180,1440]{2,1,0:T(8,128)(2,1)S(1)} %copy-done.6), channel_id=1, source_target_pairs={{0,256},{128,384},{256,0},{384,128},{1,257},{129,385},{257,1},{385... | collective-permute-start | bytes 1555208 | tf_op jit(solution)/shard_map/ppermute | solution.py:25
  28.9 2.5 %collective-permute-start.2 = (bf16[1,180,1440]{2,1,0:T(8,128)(2,1)}, bf16[1,180,1440]{2,1,0:T(8,128)(2,1)}, u32[]{:S(2)}, u32[]{:S(2)}) collective-permute-start(bf16[1,180,1440]{2,1,0:T(8,128)(2,1)} %param.12), channel_id=1, source_target_pairs={{0,256},{128,384},{256,0},{384,128},{1,257},{129,385},{257,1},{385... | collective-permute-start | bytes 1555208 | tf_op jit(solution)/shard_map/ppermute | solution.py:25
  31.4 4.3 %collective-permute-start.3 = (bf16[1,180,1440]{2,1,0:T(8,128)(2,1)}, bf16[1,180,1440]{2,1,0:T(8,128)(2,1)}, u32[]{:S(2)}, u32[]{:S(2)}) collective-permute-start(bf16[1,180,1440]{2,1,0:T(8,128)(2,1)} %param.13), channel_id=1, source_target_pairs={{0,256},{128,384},{256,0},{384,128},{1,257},{129,385},{257,1},{385... | collective-permute-start | bytes 1555208 | tf_op jit(solution)/shard_map/ppermute | solution.py:25
  35.7 0.0 copy-done.1
  35.7 0.0 copy-done
  35.7 1.0 shard_map.111.masks_ref
  36.7 11.1 %collective-permute-done = bf16[1,180,1440]{2,1,0:T(8,128)(2,1)} collective-permute-done((bf16[1,180,1440]{2,1,0:T(8,128)(2,1)S(1)}, bf16[1,180,1440]{2,1,0:T(8,128)(2,1)}, u32[]{:S(2)}, u32[]{:S(2)}) %collective-permute-start) | collective-permute-done | bytes 518432 | tf_op jit(solution)/shard_map/ppermute | solution.py:25
  47.8 9.5 %all-to-all-done = bf16[128,8,512]{2,1,0:T(8,128)(2,1)S(1)} async-done(((bf16[128,8,512]{2,1,0:T(8,128)(2,1)}), bf16[128,8,512]{2,1,0:T(8,128)(2,1)S(1)}, u32[]{:S(2)}, u32[]{:S(2)}) %all-to-all-start) | async-done | bytes 1048608 | tf_op jit(solution)/shard_map/all_to_all | solution.py:363
  57.3 3.9 %collective-permute-start.4 = (bf16[1024,512]{1,0:T(8,128)(2,1)S(1)}, bf16[1024,512]{1,0:T(8,128)(2,1)S(1)}, u32[]{:S(2)}, u32[]{:S(2)}) collective-permute-start(bf16[1024,512]{1,0:T(8,128)(2,1)S(1)} %bitcast.26), channel_id=1, source_target_pairs={{0,128},{128,0},{256,384},{384,256},{1,129},{129,1},{257,385},{385... | collective-permute-start | bytes 3145736 | tf_op jit(solution)/shard_map/ppermute | solution.py:25
  61.2 1.9 %collective-permute-start.1 = (bf16[1024,512]{1,0:T(8,128)(2,1)S(1)}, bf16[1024,512]{1,0:T(8,128)(2,1)}, u32[]{:S(2)}, u32[]{:S(2)}) collective-permute-start(bf16[1024,512]{1,0:T(8,128)(2,1)S(1)} %bitcast.27), channel_id=1, source_target_pairs={{0,1},{1,0},{2,3},{3,2},{4,5},{5,4},{6,7},{7,6},{8,9},{9,8},{10,11... | collective-permute-start | bytes 3145736 | tf_op jit(solution)/shard_map/ppermute | solution.py:25
  63.2 1.5 collective-permute-done.2
  64.7 12.1 %collective-permute-done.3 = bf16[1,180,1440]{2,1,0:T(8,128)(2,1)} collective-permute-done((bf16[1,180,1440]{2,1,0:T(8,128)(2,1)}, bf16[1,180,1440]{2,1,0:T(8,128)(2,1)}, u32[]{:S(2)}, u32[]{:S(2)}) %collective-permute-start.3) | collective-permute-done | bytes 518432 | tf_op jit(solution)/shard_map/ppermute | solution.py:25
  76.9 2.5 %fusion.3 = (bf16[1,512,1440]{2,1,0:T(8,128)(2,1)S(1)}, bf16[1,512,1440]{2,1,0:T(8,128)(2,1)S(1)}, bf16[1,512,1440]{2,1,0:T(8,128)(2,1)S(1)}) fusion(bf16[76,1440]{1,0:T(8,128)(2,1)S(1)} %broadcast_in_dim.12, bf16[180,1440]{1,0:T(8,128)(2,1)} %bitcast.8, bf16[180,1440]{1,0:T(8,128)(2,1)} %bitcast.35, bf16[180,1440]{1,0:T(8,128)(2,1)} %bitcast.14, ...), kind=kLoop, calls=%fused_computation.13 | loop fusion | flops 14745600 | bytes 7752960 | tf_op jit(solution)/shard_map/stack | solution.py:388
  79.4 0.6 pad_maximum_fusion.w_ref
  80.0 0.0 collective-permute-done.4.other_ref
  80.0 1.8 shard_map.112
  81.9 6.1 %collective-permute-done.1.mine_ref = bf16[1024,512]{1,0:T(8,128)(2,1)} collective-permute-done((bf16[1024,512]{1,0:T(8,128)(2,1)S(1)}, bf16[1024,512]{1,0:T(8,128)(2,1)}, u32[]{:S(2)}, u32[]{:S(2)}) %collective-permute-start.1) | collective-permute-done | bytes 1048608 | tf_op jit(solution)/shard_map/ppermute | solution.py:25
  88.0 2.7 %collective-permute-start.5 = (bf16[1024,512]{1,0:T(8,128)(2,1)}, bf16[1024,512]{1,0:T(8,128)(2,1)S(1)}, u32[]{:S(2)}, u32[]{:S(2)}) collective-permute-start(bf16[1024,512]{1,0:T(8,128)(2,1)} %collective-permute-done.1.mine_ref), channel_id=1, source_target_pairs={{0,128},{128,0},{256,384},{384,256},{1,129},{129,1},{257,385},{385... | collective-permute-start | bytes 3145736 | tf_op jit(solution)/shard_map/ppermute | solution.py:25
  90.7 5.6 %shard_map.113 = (bf16[1024,512]{1,0:T(8,128)(2,1)S(1)}, bf16[1024,512]{1,0:T(8,128)(2,1)S(1)}, bf16[320,512]{1,0:T(8,128)(2,1)S(1)}, bf16[320,1024]{1,0:T(8,128)(2,1)S(1)}) custom-call(s32[1]{0:T(128)} %bitcast.6.core_ref, bf16[320,1440]{1,0:T(8,128)(2,1)S(1)} %get-tuple-element.54.tok_ref.refs_2_, ...), custom_call_target="tpu_custom_call" | custom-call | flops 2831155200 | bytes 5529600 | tf_op jit(solution)/shard_map/pallas_call | solution.py:278
  96.4 0.0 collective-permute-done.5.other_ref
  96.4 8.5 %shard_map.114 = (bf16[1024,512]{1,0:T(8,128)(2,1)S(1)}, bf16[1024,512]{1,0:T(8,128)(2,1)S(1)}, bf16[320,512]{1,0:T(8,128)(2,1)S(1)}, bf16[320,1024]{1,0:T(8,128...) custom-call(s32[1]{0:T(128)} %bitcast.6.core_ref, ...), custom_call_target="tpu_custom_call" | custom-call | flops 2831155200 | bytes 5529600 | tf_op jit(solution)/shard_map/pallas_call | solution.py:278
  104.9 1.9 %collective-permute-start.6 = (bf16[1024,512]{1,0:T(8,128)(2,1)S(1)}, bf16[1024,512]{1,0:T(8,128)(2,1)S(1)}, u32[]{:S(2)}, u32[]{:S(2)}) collective-permute-start(bf16[1024,512]{1,0:T(8,128)(2,1)S(1)} %get-tuple-element.62), channel_id=1, source_target_pairs={{0,128},{128,0},{256,384},{384,256},{1,129},{129,1},{257,385},{385... | collective-permute-start | bytes 3145736 | tf_op jit(solution)/shard_map/ppermute | solution.py:25
  106.8 2.2 %shard_map.115 = (bf16[180,1440]{1,0:T(8,128)(2,1)}, bf16[180,1440]{1,0:T(8,128)(2,1)}, bf16[180,1440]{1,0:T(8,128)(2,1)S(1)}) custom-call(bf16[320,512]{1,0:T(8,128)(2,1)S(1)} %get-tuple-element.63.refs_0_, bf16[320,1024]{1,0:T(8,128)(2,1)S(1)} %get-tuple-element.64.refs_1_, bf16[320,1440]{1,0:T(8,128)(2,1)S(1)} %get-tuple-element.54.tok_ref.refs_2_, ...), custom_call_target="tpu_custom_call" | custom-call | flops 995328000 | bytes 7372800 | tf_op jit(solution)/shard_map/pallas_call | solution.py:320
  109.0 0.4 collective-permute-done.6
  109.4 0.3 add_convert_fusion.2
  109.7 2.0 %collective-permute-start.7 = (bf16[1024,512]{1,0:T(8,128)(2,1)S(1)}, bf16[1024,512]{1,0:T(8,128)(2,1)S(1)}, u32[]{:S(2)}, u32[]{:S(2)}) collective-permute-start(bf16[1024,512]{1,0:T(8,128)(2,1)S(1)} %get-tuple-element.74), channel_id=1, source_target_pairs={{0,128},{128,0},{256,384},{384,256},{1,129},{129,1},{257,385},{385... | collective-permute-start | bytes 3145736 | tf_op jit(solution)/shard_map/ppermute | solution.py:25
  111.8 1.9 %collective-permute-start.8 = (bf16[1024,512]{1,0:T(8,128)(2,1)S(1)}, bf16[1024,512]{1,0:T(8,128)(2,1)S(1)}, u32[]{:S(2)}, u32[]{:S(2)}) collective-permute-start(bf16[1024,512]{1,0:T(8,128)(2,1)S(1)} %add_convert_fusion.2), channel_id=1, source_target_pairs={{0,1},{1,0},{2,3},{3,2},{4,5},{5,4},{6,7},{7,6},{8,9},{9,8},{10,11... | collective-permute-start | bytes 3145736 | tf_op jit(solution)/shard_map/ppermute | solution.py:25
  113.7 2.4 %collective-permute-start.9 = (bf16[180,1440]{1,0:T(8,128)(2,1)}, bf16[180,1440]{1,0:T(8,128)(2,1)}, u32[]{:S(2)}, u32[]{:S(2)}) collective-permute-start(bf16[180,1440]{1,0:T(8,128)(2,1)} %get-tuple-element.83), channel_id=1, source_target_pairs={{0,256},{128,384},{256,0},{384,128},{1,257},{129,385},{257,1},{385... | collective-permute-start | bytes 1555208 | tf_op jit(solution)/shard_map/ppermute | solution.py:25
  116.1 4.4 %collective-permute-start.10 = (bf16[180,1440]{1,0:T(8,128)(2,1)}, bf16[180,1440]{1,0:T(8,128)(2,1)}, u32[]{:S(2)}, u32[]{:S(2)}) collective-permute-start(bf16[180,1440]{1,0:T(8,128)(2,1)} %get-tuple-element.84), channel_id=1, source_target_pairs={{0,256},{128,384},{256,0},{384,128},{1,257},{129,385},{257,1},{385... | collective-permute-start | bytes 1555208 | tf_op jit(solution)/shard_map/ppermute | solution.py:25
  120.5 2.4 %collective-permute-start.11 = (bf16[180,1440]{1,0:T(8,128)(2,1)S(1)}, bf16[180,1440]{1,0:T(8,128)(2,1)}, u32[]{:S(2)}, u32[]{:S(2)}) collective-permute-start(bf16[180,1440]{1,0:T(8,128)(2,1)S(1)} %get-tuple-element.85), channel_id=1, source_target_pairs={{0,256},{128,384},{256,0},{384,128},{1,257},{129,385},{257,1},{385... | collective-permute-start | bytes 1555208 | tf_op jit(solution)/shard_map/ppermute | solution.py:25
  122.9 2.0 %shard_map.116 = (f32[180,1440]{1,0:T(8,128)S(1)}, f32[180,1440]{1,0:T(8,128)S(1)}, f32[180,1440]{1,0:T(8,128)S(1)}) custom-call(bf16[320,512]{1,0:T(8,128)(2,1)S(1)} %get-tuple-element.63.refs_0_, bf16[320,1024]{1,0:T(8,128)(2,1)S(1)} %get-tuple-element.64.refs_1_, bf16[320,1440]{1,0:T(8,128)(2,1)S(1)} %get-tuple-element.54.tok_ref.refs_2_, ...), custom_call_target="tpu_custom_call" | custom-call | flops 995328000 | bytes 7372800 | tf_op jit(solution)/shard_map/pallas_call | solution.py:320
  125.0 0.0 copy-start.2
  125.0 0.0 copy-start.4
  125.0 0.0 collective-permute-done.7
  125.0 13.2 %collective-permute-done.8 = bf16[1024,512]{1,0:T(8,128)(2,1)S(1)} collective-permute-done((bf16[1024,512]{1,0:T(8,128)(2,1)S(1)}, bf16[1024,512]{1,0:T(8,128)(2,1)S(1)}, u32[]{:S(2)}, u32[]{:S(2)}) %collective-permute-start.8) | collective-permute-done | bytes 1048608 | tf_op jit(solution)/shard_map/ppermute | solution.py:25
  138.1 1.4 add_convert_fusion
  139.6 0.0 copy-done.2
  139.6 0.0 copy-done.4
  139.6 10.0 %all-to-all-start.1 = ((bf16[128,8,512]{2,1,0:T(8,128)(2,1)}), bf16[128,8,512]{2,1,0:T(8,128)(2,1)}, u32[]{:S(2)}, u32[]{:S(2)}) async-start(bf16[128,8,512]{2,1,0:T(8,128)(2,1)} %bitcast.33), calls=%async_computation.1 | async-start | bytes 2097152 | tf_op jit(solution)/shard_map/all_to_all | solution.py:363
  149.6 0.0 collective-permute-done.9.refs_3_
  149.6 0.0 collective-permute-done.10.refs_4_
  149.6 6.8 %collective-permute-done.11.refs_5_ = bf16[180,1440]{1,0:T(8,128)(2,1)} collective-permute-done((bf16[180,1440]{1,0:T(8,128)(2,1)S(1)}, bf16[180,1440]{1,0:T(8,128)(2,1)}, u32[]{:S(2)}, u32[]{:S(2)}) %collective-permute-start.11) | collective-permute-done | bytes 518432 | tf_op jit(solution)/shard_map/ppermute | solution.py:25
  156.3 0.0 copy-start.3
  156.3 1.3 copy-done.3
  157.6 0.0 copy-start.5
  157.6 1.3 copy-done.5
  158.9 2.7 %shard_map.117 = (bf16[180,1440]{1,0:T(8,128)(2,1)}, bf16[180,1440]{1,0:T(8,128)(2,1)}, bf16[180,1440]{1,0:T(8,128)(2,1)}) custom-call(f32[180,1440]{1,0:T(8,128)S(1)} %get-tuple-element.80.refs_0_, f32[180,1440]{1,0:T(8,128)S(1)} %copy-done.3, f32[180,1440]{1,0:T(8,128)S(1)} %copy-done.5, bf16[180,1440]{1,0:T(8,128)(2,1)} %collective-permute-done.9.refs_3_, ...), custom_call_target="tpu_custom_call" | custom-call | flops 259199991808 | bytes 259199991808 | tf_op jit(solution)/shard_map/pallas_call | solution.py:342
  161.5 22.2 %all-to-all-done.1 = bf16[128,8,512]{2,1,0:T(8,128)(2,1)} async-done(((bf16[128,8,512]{2,1,0:T(8,128)(2,1)}), bf16[128,8,512]{2,1,0:T(8,128)(2,1)}, u32[]{:S(2)}, u32[]{:S(2)}) %all-to-all-start.1) | async-done | bytes 1048608 | tf_op jit(solution)/shard_map/all_to_all | solution.py:363
  183.7 2.9 %shard_map.118 = (bf16[360,128]{1,0:T(8,128)(2,1)}, bf16[360,128]{1,0:T(8,128)(2,1)}) custom-call(bf16[5,1024,128]{2,1,0:T(8,128)(2,1)S(1)} %shard_map.111.masks_ref, bf16[1024,512]{1,0:T(8,128)(2,1)} %bitcast.17.raw_ref), custom_call_target="tpu_custom_call" | custom-call | flops 536870912 | bytes 1048576 | tf_op jit(solution)/shard_map/pallas_call | solution.py:151
  (1 shorter events, 0.0 us)
Async XLA Ops:
  0.6 35.1 %copy-start.1 = (f32[128,4]{0,1:T(4,128)S(1)}, f32[128,4]{0,1:T(4,128)}, u32[]{:S(2)}) copy-start(f32[128,4]{0,1:T(4,128)} %param.9) | copy-start | bytes 6148
  0.6 35.1 %copy-start = (s32[128,4]{0,1:T(4,128)S(1)}, s32[128,4]{0,1:T(4,128)}, u32[]{:S(2)}) copy-start(s32[128,4]{0,1:T(4,128)} %param.8) | copy-start | bytes 6148
  0.7 23.9 %copy-start.6 = (bf16[1,180,1440]{2,1,0:T(8,128)(2,1)S(1)}, bf16[1,180,1440]{2,1,0:T(8,128)(2,1)}, u32[]{:S(2)}) copy-start(bf16[1,180,1440]{2,1,0:T(8,128)(2,1)} %param.11) | copy-start | bytes 1555204
  3.7 53.6 %all-to-all-start = ((bf16[128,8,512]{2,1,0:T(8,128)(2,1)}), bf16[128,8,512]{2,1,0:T(8,128)(2,1)S(1)}, u32[]{:S(2)}, u32[]{:S(2)}) async-start(bf16[128,8,512]{2,1,0:T(8,128)(2,1)} %bitcast.34), calls=%async_computation | async-start | bytes 2097152 | tf_op jit(solution)/shard_map/all_to_all | solution.py:363
  24.6 23.3 %collective-permute-start = (bf16[1,180,1440]{2,1,0:T(8,128)(2,1)S(1)}, bf16[1,180,1440]{2,1,0:T(8,128)(2,1)}, u32[]{:S(2)}, u32[]{:S(2)}) collective-permute-start(bf16[1,180,1440]{2,1,0:T(8,128)(2,1)S(1)} %copy-done.6), channel_id=1, source_target_pairs={{0,256},{128,384},{256,0},{384,128},{1,257},{129,385},{257,1},{385... | collective-permute-start | bytes 1555208 | tf_op jit(solution)/shard_map/ppermute | solution.py:25
  28.9 35.8 %collective-permute-start.2 = (bf16[1,180,1440]{2,1,0:T(8,128)(2,1)}, bf16[1,180,1440]{2,1,0:T(8,128)(2,1)}, u32[]{:S(2)}, u32[]{:S(2)}) collective-permute-start(bf16[1,180,1440]{2,1,0:T(8,128)(2,1)} %param.12), channel_id=1, source_target_pairs={{0,256},{128,384},{256,0},{384,128},{1,257},{129,385},{257,1},{385... | collective-permute-start | bytes 1555208 | tf_op jit(solution)/shard_map/ppermute | solution.py:25
  31.4 45.4 %collective-permute-start.3 = (bf16[1,180,1440]{2,1,0:T(8,128)(2,1)}, bf16[1,180,1440]{2,1,0:T(8,128)(2,1)}, u32[]{:S(2)}, u32[]{:S(2)}) collective-permute-start(bf16[1,180,1440]{2,1,0:T(8,128)(2,1)} %param.13), channel_id=1, source_target_pairs={{0,256},{128,384},{256,0},{384,128},{1,257},{129,385},{257,1},{385... | collective-permute-start | bytes 1555208 | tf_op jit(solution)/shard_map/ppermute | solution.py:25
  57.3 22.7 %collective-permute-start.4 = (bf16[1024,512]{1,0:T(8,128)(2,1)S(1)}, bf16[1024,512]{1,0:T(8,128)(2,1)S(1)}, u32[]{:S(2)}, u32[]{:S(2)}) collective-permute-start(bf16[1024,512]{1,0:T(8,128)(2,1)S(1)} %bitcast.26), channel_id=1, source_target_pairs={{0,128},{128,0},{256,384},{384,256},{1,129},{129,1},{257,385},{385... | collective-permute-start | bytes 3145736 | tf_op jit(solution)/shard_map/ppermute | solution.py:25
  61.2 26.8 %collective-permute-start.1 = (bf16[1024,512]{1,0:T(8,128)(2,1)S(1)}, bf16[1024,512]{1,0:T(8,128)(2,1)}, u32[]{:S(2)}, u32[]{:S(2)}) collective-permute-start(bf16[1024,512]{1,0:T(8,128)(2,1)S(1)} %bitcast.27), channel_id=1, source_target_pairs={{0,1},{1,0},{2,3},{3,2},{4,5},{5,4},{6,7},{7,6},{8,9},{9,8},{10,11... | collective-permute-start | bytes 3145736 | tf_op jit(solution)/shard_map/ppermute | solution.py:25
  88.0 8.3 %collective-permute-start.5 = (bf16[1024,512]{1,0:T(8,128)(2,1)}, bf16[1024,512]{1,0:T(8,128)(2,1)S(1)}, u32[]{:S(2)}, u32[]{:S(2)}) collective-permute-start(bf16[1024,512]{1,0:T(8,128)(2,1)} %collective-permute-done.1.mine_ref), channel_id=1, source_target_pairs={{0,128},{128,0},{256,384},{384,256},{1,129},{129,1},{257,385},{385... | collective-permute-start | bytes 3145736 | tf_op jit(solution)/shard_map/ppermute | solution.py:25
  104.9 4.6 %collective-permute-start.6 = (bf16[1024,512]{1,0:T(8,128)(2,1)S(1)}, bf16[1024,512]{1,0:T(8,128)(2,1)S(1)}, u32[]{:S(2)}, u32[]{:S(2)}) collective-permute-start(bf16[1024,512]{1,0:T(8,128)(2,1)S(1)} %get-tuple-element.62), channel_id=1, source_target_pairs={{0,128},{128,0},{256,384},{384,256},{1,129},{129,1},{257,385},{385... | collective-permute-start | bytes 3145736 | tf_op jit(solution)/shard_map/ppermute | solution.py:25
  109.7 15.3 %collective-permute-start.7 = (bf16[1024,512]{1,0:T(8,128)(2,1)S(1)}, bf16[1024,512]{1,0:T(8,128)(2,1)S(1)}, u32[]{:S(2)}, u32[]{:S(2)}) collective-permute-start(bf16[1024,512]{1,0:T(8,128)(2,1)S(1)} %get-tuple-element.74), channel_id=1, source_target_pairs={{0,128},{128,0},{256,384},{384,256},{1,129},{129,1},{257,385},{385... | collective-permute-start | bytes 3145736 | tf_op jit(solution)/shard_map/ppermute | solution.py:25
  111.8 26.4 %collective-permute-start.8 = (bf16[1024,512]{1,0:T(8,128)(2,1)S(1)}, bf16[1024,512]{1,0:T(8,128)(2,1)S(1)}, u32[]{:S(2)}, u32[]{:S(2)}) collective-permute-start(bf16[1024,512]{1,0:T(8,128)(2,1)S(1)} %add_convert_fusion.2), channel_id=1, source_target_pairs={{0,1},{1,0},{2,3},{3,2},{4,5},{5,4},{6,7},{7,6},{8,9},{9,8},{10,11... | collective-permute-start | bytes 3145736 | tf_op jit(solution)/shard_map/ppermute | solution.py:25
  113.7 35.9 %collective-permute-start.9 = (bf16[180,1440]{1,0:T(8,128)(2,1)}, bf16[180,1440]{1,0:T(8,128)(2,1)}, u32[]{:S(2)}, u32[]{:S(2)}) collective-permute-start(bf16[180,1440]{1,0:T(8,128)(2,1)} %get-tuple-element.83), channel_id=1, source_target_pairs={{0,256},{128,384},{256,0},{384,128},{1,257},{129,385},{257,1},{385... | collective-permute-start | bytes 1555208 | tf_op jit(solution)/shard_map/ppermute | solution.py:25
  116.1 33.4 %collective-permute-start.10 = (bf16[180,1440]{1,0:T(8,128)(2,1)}, bf16[180,1440]{1,0:T(8,128)(2,1)}, u32[]{:S(2)}, u32[]{:S(2)}) collective-permute-start(bf16[180,1440]{1,0:T(8,128)(2,1)} %get-tuple-element.84), channel_id=1, source_target_pairs={{0,256},{128,384},{256,0},{384,128},{1,257},{129,385},{257,1},{385... | collective-permute-start | bytes 1555208 | tf_op jit(solution)/shard_map/ppermute | solution.py:25
  120.5 35.8 %collective-permute-start.11 = (bf16[180,1440]{1,0:T(8,128)(2,1)S(1)}, bf16[180,1440]{1,0:T(8,128)(2,1)}, u32[]{:S(2)}, u32[]{:S(2)}) collective-permute-start(bf16[180,1440]{1,0:T(8,128)(2,1)S(1)} %get-tuple-element.85), channel_id=1, source_target_pairs={{0,256},{128,384},{256,0},{384,128},{1,257},{129,385},{257,1},{385... | collective-permute-start | bytes 1555208 | tf_op jit(solution)/shard_map/ppermute | solution.py:25
  125.0 14.6 %copy-start.2 = (f32[180,1440]{1,0:T(8,128)}, f32[180,1440]{1,0:T(8,128)S(1)}, u32[]{:S(2)}) copy-start(f32[180,1440]{1,0:T(8,128)S(1)} %get-tuple-element.81.refs_1_) | copy-start | bytes 3110404
  125.0 14.6 %copy-start.4 = (f32[180,1440]{1,0:T(8,128)}, f32[180,1440]{1,0:T(8,128)S(1)}, u32[]{:S(2)}) copy-start(f32[180,1440]{1,0:T(8,128)S(1)} %get-tuple-element.82.refs_2_) | copy-start | bytes 3110404
  139.6 44.1 %all-to-all-start.1 = ((bf16[128,8,512]{2,1,0:T(8,128)(2,1)}), bf16[128,8,512]{2,1,0:T(8,128)(2,1)}, u32[]{:S(2)}, u32[]{:S(2)}) async-start(bf16[128,8,512]{2,1,0:T(8,128)(2,1)} %bitcast.33), calls=%async_computation.1 | async-start | bytes 2097152 | tf_op jit(solution)/shard_map/all_to_all | solution.py:363
  156.3 1.3 copy-start.3
  157.6 1.3 copy-start.5

commit v8 on v7

--- a/solution.py
+++ b/solution.py
@@ -395,12 +395,14 @@
             )
         ]
     )
-    next_mine, wide, tok_a = lax.optimization_barrier((next_mine, wide, tok_a))
     keep_a, send_a, hid_a, both_a = expert_call(
         rows_kernel, core, raw_rows, width, (tok_a, grad_a, wide), [], 12
     )
+    next_mine, wide, send_a = lax.optimization_barrier((next_mine, wide, send_a))
     next_beside = exchanged(next_mine, "rep", 1)
-    next_beside, send_a = lax.optimization_barrier((next_beside, send_a))
+    got_a = exchanged(send_a, "rep", 1)
+    sum_a = (keep_a.astype(full) + got_a.astype(full)).astype(low)
+    next_beside, sum_a = lax.optimization_barrier((next_beside, sum_a))
     keep_b, send_b, hid_b, both_b, tok_b, grad_b = expert_call(
         second_kernel, core, raw_rows, width, (next_mine, next_beside, wide), ["row", "row"], 12
     )
@@ -409,10 +411,7 @@
     peers = weight_grads(rows_a, rows_b, PEER, hidden, width, low)
     got_b, *peers = lax.optimization_barrier((got_b, *peers))
     sum_b = (keep_b.astype(full) + got_b.astype(full)).astype(low)
-    sum_b, send_a = lax.optimization_barrier((sum_b, send_a))
     got_sum = exchanged(sum_b, "exp", 1)
-    got_a = exchanged(send_a, "rep", 1)
-    sum_a = (keep_a.astype(full) + got_a.astype(full)).astype(low)
     got_peers = [exchanged(part, "rep", 2) for part in peers]
     owns = weight_grads(rows_a, rows_b, 0, hidden, width, full)
     early = []

time: 187 us -> 185 us (0.989)
  waiting for transfers between devices: 82.9 us -> 73.2 us
  starting transfers between devices: 65.5 us -> 71.4 us
  local copies, waits for them, and re-layouts: 2.55 us -> 4.56 us
    ppermute x12, waiting for transfers between devices: 51.2 us -> 39.8 us  [exchanged(): return lax.ppermute(block, axis, [(i, i ^ distance) for i in range(count)])]
    all_to_all x2, starting transfers between devices: 30.8 us -> 35.2 us  [by_parity(): lax.all_to_all(chunks, ('rep', 'exp'), split_axis=0, concat_axis=0, axis_...]
    unnamed x14, local copies, waits for them, and re-layouts: 2.53 us -> 4.54 us
  transfers between devices with their start and end apart: 14 -> 14, of which waited for: 9 -> 11; matrix products, arithmetic and copies ran while one was open for 2% -> 3% of each run, Pallas kernels for 8% -> 8%
where the time goes in v8:
time: 185 us; the launch traced here: 184 us
  waiting for transfers between devices  73.2 us (40%)
  starting transfers between devices  71.4 us (39%)
  Pallas kernels  28.6 us (15%)
  other arithmetic  5.05 us (3%)
  local copies, waits for them, and re-layouts  4.56 us (2%)
    ppermute x12, waiting for transfers between devices, exchanged(): return lax.ppermute(block, axis, [(i, i ^ distance) for i in range(count)])  39.8 us
    ppermute x12, starting transfers between devices, exchanged(): return lax.ppermute(block, axis, [(i, i ^ distance) for i in range(count)])  36.2 us
    all_to_all x2, starting transfers between devices, by_parity(): lax.all_to_all(chunks, ('rep', 'exp'), split_axis=0, concat_axis=0, axis_...  35.2 us
    all_to_all x2, waiting for transfers between devices, by_parity(): lax.all_to_all(chunks, ('rep', 'exp'), split_axis=0, concat_axis=0, axis_...  33.4 us
    pallas_call x3, Pallas kernels, expert_call(): pl.pallas_call(kernel, in_specs=[scalar()] + in_vmem(len(operands)), out_...  14.7 us
    unnamed x14, local copies, waits for them, and re-layouts  4.54 us
    pallas_call x2, Pallas kernels, weight_grads(): pl.pallas_call(functools.partial(product_kernel, start), in_specs=in_vmem...  4.27 us
  transfers between devices with their start and end apart: 14, of which 11 were waited for; matrix products, arithmetic and copies ran while one was open for 3% of the time, Pallas kernels for 8%

profile of v8, /device:TPU:1, one launch (start us, length us, event | category | flops | bytes accessed | tf_op | source)
XLA Modules:
  0.0 183.7 jit_solution(14306933712660059011)
XLA Ops:
  0.6 0.0 copy-start.1
  0.6 0.0 copy-start
  0.7 0.0 copy-start.6
  0.7 3.1 %shard_map.110 = bf16[1024,512]{1,0:T(8,128)(2,1)} custom-call(s32[4,128]{1,0:T(4,128)} %bitcast.29, f32[4,128]{1,0:T(4,128)} %bitcast.31, bf16[360,128]{1,0:T(8,128)(2,1)} %bitcast.36, bf16[360,128]{1,0:T(8,128)(2,1)} %bitcast.37), custom_call_target="tpu_custom_call" | custom-call | flops 536870912 | bytes 1048576 | tf_op jit(solution)/shard_map/pallas_call | solution.py:103
  3.7 20.8 %all-to-all-start = ((bf16[128,8,512]{2,1,0:T(8,128)(2,1)}), bf16[128,8,512]{2,1,0:T(8,128)(2,1)S(1)}, u32[]{:S(2)}, u32[]{:S(2)}) async-start(bf16[128,8,512]{2,1,0:T(8,128)(2,1)} %bitcast.34), calls=%async_computation | async-start | bytes 2097152 | tf_op jit(solution)/shard_map/all_to_all | solution.py:363
  24.6 0.0 copy-done.6
  24.6 4.3 %collective-permute-start = (bf16[1,180,1440]{2,1,0:T(8,128)(2,1)S(1)}, bf16[1,180,1440]{2,1,0:T(8,128)(2,1)}, u32[]{:S(2)}, u32[]{:S(2)}) collective-permute-start(bf16[1,180,1440]{2,1,0:T(8,128)(2,1)S(1)} %copy-done.6), channel_id=1, source_target_pairs={{0,256},{128,384},{256,0},{384,128},{1,257},{129,385},{257,1},{385... | collective-permute-start | bytes 1555208 | tf_op jit(solution)/shard_map/ppermute | solution.py:25
  28.9 2.5 %collective-permute-start.2 = (bf16[1,180,1440]{2,1,0:T(8,128)(2,1)}, bf16[1,180,1440]{2,1,0:T(8,128)(2,1)}, u32[]{:S(2)}, u32[]{:S(2)}) collective-permute-start(bf16[1,180,1440]{2,1,0:T(8,128)(2,1)} %param.12), channel_id=1, source_target_pairs={{0,256},{128,384},{256,0},{384,128},{1,257},{129,385},{257,1},{385... | collective-permute-start | bytes 1555208 | tf_op jit(solution)/shard_map/ppermute | solution.py:25
  31.4 4.3 %collective-permute-start.3 = (bf16[1,180,1440]{2,1,0:T(8,128)(2,1)}, bf16[1,180,1440]{2,1,0:T(8,128)(2,1)}, u32[]{:S(2)}, u32[]{:S(2)}) collective-permute-start(bf16[1,180,1440]{2,1,0:T(8,128)(2,1)} %param.13), channel_id=1, source_target_pairs={{0,256},{128,384},{256,0},{384,128},{1,257},{129,385},{257,1},{385... | collective-permute-start | bytes 1555208 | tf_op jit(solution)/shard_map/ppermute | solution.py:25
  35.7 0.0 copy-done.1
  35.7 0.0 copy-done
  35.7 1.0 shard_map.111.masks_ref
  36.7 11.1 %collective-permute-done = bf16[1,180,1440]{2,1,0:T(8,128)(2,1)} collective-permute-done((bf16[1,180,1440]{2,1,0:T(8,128)(2,1)S(1)}, bf16[1,180,1440]{2,1,0:T(8,128)(2,1)}, u32[]{:S(2)}, u32[]{:S(2)}) %collective-permute-start) | collective-permute-done | bytes 518432 | tf_op jit(solution)/shard_map/ppermute | solution.py:25
  47.8 9.5 %all-to-all-done = bf16[128,8,512]{2,1,0:T(8,128)(2,1)S(1)} async-done(((bf16[128,8,512]{2,1,0:T(8,128)(2,1)}), bf16[128,8,512]{2,1,0:T(8,128)(2,1)S(1)}, u32[]{:S(2)}, u32[]{:S(2)}) %all-to-all-start) | async-done | bytes 1048608 | tf_op jit(solution)/shard_map/all_to_all | solution.py:363
  57.3 3.9 %collective-permute-start.4 = (bf16[1024,512]{1,0:T(8,128)(2,1)S(1)}, bf16[1024,512]{1,0:T(8,128)(2,1)S(1)}, u32[]{:S(2)}, u32[]{:S(2)}) collective-permute-start(bf16[1024,512]{1,0:T(8,128)(2,1)S(1)} %bitcast.26), channel_id=1, source_target_pairs={{0,128},{128,0},{256,384},{384,256},{1,129},{129,1},{257,385},{385... | collective-permute-start | bytes 3145736 | tf_op jit(solution)/shard_map/ppermute | solution.py:25
  61.2 1.9 %collective-permute-start.1 = (bf16[1024,512]{1,0:T(8,128)(2,1)S(1)}, bf16[1024,512]{1,0:T(8,128)(2,1)S(1)}, u32[]{:S(2)}, u32[]{:S(2)}) collective-permute-start(bf16[1024,512]{1,0:T(8,128)(2,1)S(1)} %bitcast.27), channel_id=1, source_target_pairs={{0,1},{1,0},{2,3},{3,2},{4,5},{5,4},{6,7},{7,6},{8,9},{9,8},{10,11... | collective-permute-start | bytes 3145736 | tf_op jit(solution)/shard_map/ppermute | solution.py:25
  63.2 1.5 collective-permute-done.2
  64.7 12.1 %collective-permute-done.3 = bf16[1,180,1440]{2,1,0:T(8,128)(2,1)} collective-permute-done((bf16[1,180,1440]{2,1,0:T(8,128)(2,1)}, bf16[1,180,1440]{2,1,0:T(8,128)(2,1)}, u32[]{:S(2)}, u32[]{:S(2)}) %collective-permute-start.3) | collective-permute-done | bytes 518432 | tf_op jit(solution)/shard_map/ppermute | solution.py:25
  76.9 2.5 %fusion.3 = (bf16[1,512,1440]{2,1,0:T(8,128)(2,1)S(1)}, bf16[1,512,1440]{2,1,0:T(8,128)(2,1)S(1)}, bf16[1,512,1440]{2,1,0:T(8,128)(2,1)S(1)}) fusion(bf16[76,1440]{1,0:T(8,128)(2,1)S(1)} %broadcast_in_dim.12, bf16[180,1440]{1,0:T(8,128)(2,1)} %bitcast.7, bf16[180,1440]{1,0:T(8,128)(2,1)} %bitcast.35, bf16[180,1440]{1,0:T(8,128)(2,1)} %bitcast.13, ...), kind=kLoop, calls=%fused_computation.13 | loop fusion | flops 14745600 | bytes 7752960 | tf_op jit(solution)/shard_map/stack | solution.py:388
  79.4 0.6 pad_maximum_fusion.w_ref
  80.0 0.0 collective-permute-done.4.other_ref
  80.0 1.8 %shard_map.112 = (bf16[320,1440]{1,0:T(8,128)(2,1)S(1)}, bf16[320,1440]{1,0:T(8,128)(2,1)S(1)}) custom-call(s32[1]{0:T(128)} %bitcast.15.core_ref, bf16[1024,512]{1,0:T(8,128)(2,1)S(1)} %bitcast.28, bf16[1024,512]{1,0:T(8,128)(2,1)S(1)} %collective-permute-done.4.other_ref), custom_call_target="tpu_custom_call" | custom-call | flops 235929600 | bytes 460800 | tf_op jit(solution)/shard_map/pallas_call | solution.py:278
  81.9 5.6 %shard_map.113 = (bf16[1024,512]{1,0:T(8,128)(2,1)S(1)}, bf16[1024,512]{1,0:T(8,128)(2,1)S(1)}, bf16[320,512]{1,0:T(8,128)(2,1)S(1)}, bf16[320,1024]{1,0:T(8,128)(2,1)S(1)}) custom-call(s32[1]{0:T(128)} %bitcast.15.core_ref, bf16[320,1440]{1,0:T(8,128)(2,1)S(1)} %get-tuple-element.51.tok_ref.refs_2_, ...), custom_call_target="tpu_custom_call" | custom-call | flops 2831155200 | bytes 5529600 | tf_op jit(solution)/shard_map/pallas_call | solution.py:278
  87.5 0.4 collective-permute-done.1.mine_ref
  87.9 2.9 %collective-permute-start.6 = (bf16[1024,512]{1,0:T(8,128)(2,1)S(1)}, bf16[1024,512]{1,0:T(8,128)(2,1)S(1)}, u32[]{:S(2)}, u32[]{:S(2)}) collective-permute-start(bf16[1024,512]{1,0:T(8,128)(2,1)S(1)} %get-tuple-element.56), channel_id=1, source_target_pairs={{0,128},{128,0},{256,384},{384,256},{1,129},{129,1},{257,385},{385... | collective-permute-start | bytes 3145736 | tf_op jit(solution)/shard_map/ppermute | solution.py:25
  90.9 1.9 %collective-permute-start.5 = (bf16[1024,512]{1,0:T(8,128)(2,1)S(1)}, bf16[1024,512]{1,0:T(8,128)(2,1)S(1)}, u32[]{:S(2)}, u32[]{:S(2)}) collective-permute-start(bf16[1024,512]{1,0:T(8,128)(2,1)S(1)} %collective-permute-done.1.mine_ref), channel_id=1, source_target_pairs={{0,128},{128,0},{256,384},{384,256},{1,129},{129,1},{257,385},{385... | collective-permute-start | bytes 3145736 | tf_op jit(solution)/shard_map/ppermute | solution.py:25
  92.8 0.3 collective-permute-done.6
  93.1 0.3 add_convert_fusion.2
  93.4 2.0 %collective-permute-done.5.other_ref = bf16[1024,512]{1,0:T(8,128)(2,1)S(1)} collective-permute-done((bf16[1024,512]{1,0:T(8,128)(2,1)S(1)}, bf16[1024,512]{1,0:T(8,128)(2,1)S(1)}, u32[]{:S(2)}, u32[]{:S(2)}) %collective-permute-start.5) | collective-permute-done | bytes 1048608 | tf_op jit(solution)/shard_map/ppermute | solution.py:25
  95.4 7.2 %shard_map.114 = (bf16[1024,512]{1,0:T(8,128)(2,1)S(1)}, bf16[1024,512]{1,0:T(8,128)(2,1)S(1)}, bf16[320,512]{1,0:T(8,128)(2,1)S(1)}, bf16[320,1024]{1,0:T(8,128...) custom-call(s32[1]{0:T(128)} %bitcast.15.core_ref, ...), custom_call_target="tpu_custom_call" | custom-call | flops 2831155200 | bytes 5529600 | tf_op jit(solution)/shard_map/pallas_call | solution.py:278
  102.7 2.0 %collective-permute-start.7 = (bf16[1024,512]{1,0:T(8,128)(2,1)S(1)}, bf16[1024,512]{1,0:T(8,128)(2,1)S(1)}, u32[]{:S(2)}, u32[]{:S(2)}) collective-permute-start(bf16[1024,512]{1,0:T(8,128)(2,1)S(1)} %get-tuple-element.61), channel_id=1, source_target_pairs={{0,128},{128,0},{256,384},{384,256},{1,129},{129,1},{257,385},{385... | collective-permute-start | bytes 3145736 | tf_op jit(solution)/shard_map/ppermute | solution.py:25
  104.7 2.2 %shard_map.115 = (bf16[180,1440]{1,0:T(8,128)(2,1)}, bf16[180,1440]{1,0:T(8,128)(2,1)}, bf16[180,1440]{1,0:T(8,128)(2,1)S(1)}) custom-call(bf16[320,512]{1,0:T(8,128)(2,1)S(1)} %get-tuple-element.62.refs_0_, bf16[320,1024]{1,0:T(8,128)(2,1)S(1)} %get-tuple-element.63.refs_1_, bf16[320,1440]{1,0:T(8,128)(2,1)S(1)} %get-tuple-element.51.tok_ref.refs_2_, ...), custom_call_target="tpu_custom_call" | custom-call | flops 995328000 | bytes 7372800 | tf_op jit(solution)/shard_map/pallas_call | solution.py:320
  106.9 0.3 collective-permute-done.7
  107.2 0.3 add_convert_fusion.1
  107.5 2.4 %collective-permute-start.8 = (bf16[1024,512]{1,0:T(8,128)(2,1)S(1)}, bf16[1024,512]{1,0:T(8,128)(2,1)S(1)}, u32[]{:S(2)}, u32[]{:S(2)}) collective-permute-start(bf16[1024,512]{1,0:T(8,128)(2,1)S(1)} %add_convert_fusion.1), channel_id=1, source_target_pairs={{0,1},{1,0},{2,3},{3,2},{4,5},{5,4},{6,7},{7,6},{8,9},{9,8},{10,11... | collective-permute-start | bytes 3145736 | tf_op jit(solution)/shard_map/ppermute | solution.py:25
  109.9 3.3 %collective-permute-start.9 = (bf16[180,1440]{1,0:T(8,128)(2,1)}, bf16[180,1440]{1,0:T(8,128)(2,1)}, u32[]{:S(2)}, u32[]{:S(2)}) collective-permute-start(bf16[180,1440]{1,0:T(8,128)(2,1)} %get-tuple-element.79), channel_id=1, source_target_pairs={{0,256},{128,384},{256,0},{384,128},{1,257},{129,385},{257,1},{385... | collective-permute-start | bytes 1555208 | tf_op jit(solution)/shard_map/ppermute | solution.py:25
  113.2 3.5 %collective-permute-start.10 = (bf16[180,1440]{1,0:T(8,128)(2,1)}, bf16[180,1440]{1,0:T(8,128)(2,1)}, u32[]{:S(2)}, u32[]{:S(2)}) collective-permute-start(bf16[180,1440]{1,0:T(8,128)(2,1)} %get-tuple-element.80), channel_id=1, source_target_pairs={{0,256},{128,384},{256,0},{384,128},{1,257},{129,385},{257,1},{385... | collective-permute-start | bytes 1555208 | tf_op jit(solution)/shard_map/ppermute | solution.py:25
  116.7 3.3 %collective-permute-start.11 = (bf16[180,1440]{1,0:T(8,128)(2,1)S(1)}, bf16[180,1440]{1,0:T(8,128)(2,1)}, u32[]{:S(2)}, u32[]{:S(2)}) collective-permute-start(bf16[180,1440]{1,0:T(8,128)(2,1)S(1)} %get-tuple-element.81), channel_id=1, source_target_pairs={{0,256},{128,384},{256,0},{384,128},{1,257},{129,385},{257,1},{385... | collective-permute-start | bytes 1555208 | tf_op jit(solution)/shard_map/ppermute | solution.py:25
  120.0 2.0 %shard_map.116 = (f32[180,1440]{1,0:T(8,128)S(1)}, f32[180,1440]{1,0:T(8,128)S(1)}, f32[180,1440]{1,0:T(8,128)S(1)}) custom-call(bf16[320,512]{1,0:T(8,128)(2,1)S(1)} %get-tuple-element.62.refs_0_, bf16[320,1024]{1,0:T(8,128)(2,1)S(1)} %get-tuple-element.63.refs_1_, bf16[320,1440]{1,0:T(8,128)(2,1)S(1)} %get-tuple-element.51.tok_ref.refs_2_, ...), custom_call_target="tpu_custom_call" | custom-call | flops 995328000 | bytes 7372800 | tf_op jit(solution)/shard_map/pallas_call | solution.py:320
  122.0 0.0 copy-start.2
  122.1 1.0 copy-done.2
  123.1 0.0 copy-start.4
  123.1 1.0 copy-done.4
  124.1 10.0 %collective-permute-done.8 = bf16[1024,512]{1,0:T(8,128)(2,1)S(1)} collective-permute-done((bf16[1024,512]{1,0:T(8,128)(2,1)S(1)}, bf16[1024,512]{1,0:T(8,128)(2,1)S(1)}, u32[]{:S(2)}, u32[]{:S(2)}) %collective-permute-start.8) | collective-permute-done | bytes 1048608 | tf_op jit(solution)/shard_map/ppermute | solution.py:25
  134.1 1.3 add_convert_fusion
  135.5 14.3 %all-to-all-start.1 = ((bf16[128,8,512]{2,1,0:T(8,128)(2,1)}), bf16[128,8,512]{2,1,0:T(8,128)(2,1)}, u32[]{:S(2)}, u32[]{:S(2)}) async-start(bf16[128,8,512]{2,1,0:T(8,128)(2,1)} %bitcast.33), calls=%async_computation.1 | async-start | bytes 2097152 | tf_op jit(solution)/shard_map/all_to_all | solution.py:363
  149.8 0.0 collective-permute-done.9.refs_3_
  149.8 0.0 collective-permute-done.10.refs_4_
  149.8 1.9 %collective-permute-done.11.refs_5_ = bf16[180,1440]{1,0:T(8,128)(2,1)} collective-permute-done((bf16[180,1440]{1,0:T(8,128)(2,1)S(1)}, bf16[180,1440]{1,0:T(8,128)(2,1)}, u32[]{:S(2)}, u32[]{:S(2)}) %collective-permute-start.11) | collective-permute-done | bytes 518432 | tf_op jit(solution)/shard_map/ppermute | solution.py:25
  151.8 0.0 copy-start.3
  151.8 1.3 copy-done.3
  153.0 0.0 copy-start.5
  153.0 1.3 copy-done.5
  154.3 2.7 %shard_map.117 = (bf16[180,1440]{1,0:T(8,128)(2,1)}, bf16[180,1440]{1,0:T(8,128)(2,1)}, bf16[180,1440]{1,0:T(8,128)(2,1)}) custom-call(f32[180,1440]{1,0:T(8,128)S(1)} %get-tuple-element.76.refs_0_, f32[180,1440]{1,0:T(8,128)S(1)} %copy-done.3, f32[180,1440]{1,0:T(8,128)S(1)} %copy-done.5, bf16[180,1440]{1,0:T(8,128)(2,1)} %collective-permute-done.9.refs_3_, ...), custom_call_target="tpu_custom_call" | custom-call | flops 259199991808 | bytes 259199991808 | tf_op jit(solution)/shard_map/pallas_call | solution.py:342
  156.9 23.9 %all-to-all-done.1 = bf16[128,8,512]{2,1,0:T(8,128)(2,1)} async-done(((bf16[128,8,512]{2,1,0:T(8,128)(2,1)}), bf16[128,8,512]{2,1,0:T(8,128)(2,1)}, u32[]{:S(2)}, u32[]{:S(2)}) %all-to-all-start.1) | async-done | bytes 1048608 | tf_op jit(solution)/shard_map/all_to_all | solution.py:363
  180.9 2.9 %shard_map.118 = (bf16[360,128]{1,0:T(8,128)(2,1)}, bf16[360,128]{1,0:T(8,128)(2,1)}) custom-call(bf16[5,1024,128]{2,1,0:T(8,128)(2,1)S(1)} %shard_map.111.masks_ref, bf16[1024,512]{1,0:T(8,128)(2,1)} %bitcast.17.raw_ref), custom_call_target="tpu_custom_call" | custom-call | flops 536870912 | bytes 1048576 | tf_op jit(solution)/shard_map/pallas_call | solution.py:151
  (1 shorter events, 0.0 us)
Async XLA Ops:
  0.6 35.1 %copy-start.1 = (f32[128,4]{0,1:T(4,128)S(1)}, f32[128,4]{0,1:T(4,128)}, u32[]{:S(2)}) copy-start(f32[128,4]{0,1:T(4,128)} %param.9) | copy-start | bytes 6148
  0.6 35.1 %copy-start = (s32[128,4]{0,1:T(4,128)S(1)}, s32[128,4]{0,1:T(4,128)}, u32[]{:S(2)}) copy-start(s32[128,4]{0,1:T(4,128)} %param.8) | copy-start | bytes 6148
  0.7 23.9 %copy-start.6 = (bf16[1,180,1440]{2,1,0:T(8,128)(2,1)S(1)}, bf16[1,180,1440]{2,1,0:T(8,128)(2,1)}, u32[]{:S(2)}) copy-start(bf16[1,180,1440]{2,1,0:T(8,128)(2,1)} %param.11) | copy-start | bytes 1555204
  3.7 53.6 %all-to-all-start = ((bf16[128,8,512]{2,1,0:T(8,128)(2,1)}), bf16[128,8,512]{2,1,0:T(8,128)(2,1)S(1)}, u32[]{:S(2)}, u32[]{:S(2)}) async-start(bf16[128,8,512]{2,1,0:T(8,128)(2,1)} %bitcast.34), calls=%async_computation | async-start | bytes 2097152 | tf_op jit(solution)/shard_map/all_to_all | solution.py:363
  24.6 23.3 %collective-permute-start = (bf16[1,180,1440]{2,1,0:T(8,128)(2,1)S(1)}, bf16[1,180,1440]{2,1,0:T(8,128)(2,1)}, u32[]{:S(2)}, u32[]{:S(2)}) collective-permute-start(bf16[1,180,1440]{2,1,0:T(8,128)(2,1)S(1)} %copy-done.6), channel_id=1, source_target_pairs={{0,256},{128,384},{256,0},{384,128},{1,257},{129,385},{257,1},{385... | collective-permute-start | bytes 1555208 | tf_op jit(solution)/shard_map/ppermute | solution.py:25
  28.9 35.8 %collective-permute-start.2 = (bf16[1,180,1440]{2,1,0:T(8,128)(2,1)}, bf16[1,180,1440]{2,1,0:T(8,128)(2,1)}, u32[]{:S(2)}, u32[]{:S(2)}) collective-permute-start(bf16[1,180,1440]{2,1,0:T(8,128)(2,1)} %param.12), channel_id=1, source_target_pairs={{0,256},{128,384},{256,0},{384,128},{1,257},{129,385},{257,1},{385... | collective-permute-start | bytes 1555208 | tf_op jit(solution)/shard_map/ppermute | solution.py:25
  31.4 45.4 %collective-permute-start.3 = (bf16[1,180,1440]{2,1,0:T(8,128)(2,1)}, bf16[1,180,1440]{2,1,0:T(8,128)(2,1)}, u32[]{:S(2)}, u32[]{:S(2)}) collective-permute-start(bf16[1,180,1440]{2,1,0:T(8,128)(2,1)} %param.13), channel_id=1, source_target_pairs={{0,256},{128,384},{256,0},{384,128},{1,257},{129,385},{257,1},{385... | collective-permute-start | bytes 1555208 | tf_op jit(solution)/shard_map/ppermute | solution.py:25
  57.3 22.7 %collective-permute-start.4 = (bf16[1024,512]{1,0:T(8,128)(2,1)S(1)}, bf16[1024,512]{1,0:T(8,128)(2,1)S(1)}, u32[]{:S(2)}, u32[]{:S(2)}) collective-permute-start(bf16[1024,512]{1,0:T(8,128)(2,1)S(1)} %bitcast.26), channel_id=1, source_target_pairs={{0,128},{128,0},{256,384},{384,256},{1,129},{129,1},{257,385},{385... | collective-permute-start | bytes 3145736 | tf_op jit(solution)/shard_map/ppermute | solution.py:25
  61.2 26.7 %collective-permute-start.1 = (bf16[1024,512]{1,0:T(8,128)(2,1)S(1)}, bf16[1024,512]{1,0:T(8,128)(2,1)S(1)}, u32[]{:S(2)}, u32[]{:S(2)}) collective-permute-start(bf16[1024,512]{1,0:T(8,128)(2,1)S(1)} %bitcast.27), channel_id=1, source_target_pairs={{0,1},{1,0},{2,3},{3,2},{4,5},{5,4},{6,7},{7,6},{8,9},{9,8},{10,11... | collective-permute-start | bytes 3145736 | tf_op jit(solution)/shard_map/ppermute | solution.py:25
  87.9 5.2 %collective-permute-start.6 = (bf16[1024,512]{1,0:T(8,128)(2,1)S(1)}, bf16[1024,512]{1,0:T(8,128)(2,1)S(1)}, u32[]{:S(2)}, u32[]{:S(2)}) collective-permute-start(bf16[1024,512]{1,0:T(8,128)(2,1)S(1)} %get-tuple-element.56), channel_id=1, source_target_pairs={{0,128},{128,0},{256,384},{384,256},{1,129},{129,1},{257,385},{385... | collective-permute-start | bytes 3145736 | tf_op jit(solution)/shard_map/ppermute | solution.py:25
  90.9 4.6 %collective-permute-start.5 = (bf16[1024,512]{1,0:T(8,128)(2,1)S(1)}, bf16[1024,512]{1,0:T(8,128)(2,1)S(1)}, u32[]{:S(2)}, u32[]{:S(2)}) collective-permute-start(bf16[1024,512]{1,0:T(8,128)(2,1)S(1)} %collective-permute-done.1.mine_ref), channel_id=1, source_target_pairs={{0,128},{128,0},{256,384},{384,256},{1,129},{129,1},{257,385},{385... | collective-permute-start | bytes 3145736 | tf_op jit(solution)/shard_map/ppermute | solution.py:25
  102.7 4.6 %collective-permute-start.7 = (bf16[1024,512]{1,0:T(8,128)(2,1)S(1)}, bf16[1024,512]{1,0:T(8,128)(2,1)S(1)}, u32[]{:S(2)}, u32[]{:S(2)}) collective-permute-start(bf16[1024,512]{1,0:T(8,128)(2,1)S(1)} %get-tuple-element.61), channel_id=1, source_target_pairs={{0,128},{128,0},{256,384},{384,256},{1,129},{129,1},{257,385},{385... | collective-permute-start | bytes 3145736 | tf_op jit(solution)/shard_map/ppermute | solution.py:25
  107.5 26.6 %collective-permute-start.8 = (bf16[1024,512]{1,0:T(8,128)(2,1)S(1)}, bf16[1024,512]{1,0:T(8,128)(2,1)S(1)}, u32[]{:S(2)}, u32[]{:S(2)}) collective-permute-start(bf16[1024,512]{1,0:T(8,128)(2,1)S(1)} %add_convert_fusion.1), channel_id=1, source_target_pairs={{0,1},{1,0},{2,3},{3,2},{4,5},{5,4},{6,7},{7,6},{8,9},{9,8},{10,11... | collective-permute-start | bytes 3145736 | tf_op jit(solution)/shard_map/ppermute | solution.py:25
  109.9 39.9 %collective-permute-start.9 = (bf16[180,1440]{1,0:T(8,128)(2,1)}, bf16[180,1440]{1,0:T(8,128)(2,1)}, u32[]{:S(2)}, u32[]{:S(2)}) collective-permute-start(bf16[180,1440]{1,0:T(8,128)(2,1)} %get-tuple-element.79), channel_id=1, source_target_pairs={{0,256},{128,384},{256,0},{384,128},{1,257},{129,385},{257,1},{385... | collective-permute-start | bytes 1555208 | tf_op jit(solution)/shard_map/ppermute | solution.py:25
  113.2 36.6 %collective-permute-start.10 = (bf16[180,1440]{1,0:T(8,128)(2,1)}, bf16[180,1440]{1,0:T(8,128)(2,1)}, u32[]{:S(2)}, u32[]{:S(2)}) collective-permute-start(bf16[180,1440]{1,0:T(8,128)(2,1)} %get-tuple-element.80), channel_id=1, source_target_pairs={{0,256},{128,384},{256,0},{384,128},{1,257},{129,385},{257,1},{385... | collective-permute-start | bytes 1555208 | tf_op jit(solution)/shard_map/ppermute | solution.py:25
  116.7 35.1 %collective-permute-start.11 = (bf16[180,1440]{1,0:T(8,128)(2,1)S(1)}, bf16[180,1440]{1,0:T(8,128)(2,1)}, u32[]{:S(2)}, u32[]{:S(2)}) collective-permute-start(bf16[180,1440]{1,0:T(8,128)(2,1)S(1)} %get-tuple-element.81), channel_id=1, source_target_pairs={{0,256},{128,384},{256,0},{384,128},{1,257},{129,385},{257,1},{385... | collective-permute-start | bytes 1555208 | tf_op jit(solution)/shard_map/ppermute | solution.py:25
  122.0 1.0 copy-start.2
  123.1 1.0 copy-start.4
  135.5 45.4 %all-to-all-start.1 = ((bf16[128,8,512]{2,1,0:T(8,128)(2,1)}), bf16[128,8,512]{2,1,0:T(8,128)(2,1)}, u32[]{:S(2)}, u32[]{:S(2)}) async-start(bf16[128,8,512]{2,1,0:T(8,128)(2,1)} %bitcast.33), calls=%async_computation.1 | async-start | bytes 2097152 | tf_op jit(solution)/shard_map/all_to_all | solution.py:363
  151.8 1.3 copy-start.3
  153.0 1.3 copy-start.5

commit v9 on v8

--- a/solution.py
+++ b/solution.py
@@ -113,37 +113,37 @@
 
 
 def mask_kernel(ids_ref, gates_ref, masks_ref):
-    experts = masks_ref.shape[1] // (2 * CHUNK)
+    experts = masks_ref.shape[0] // (2 * CHUNK)
     main, even, odd, gate = placed(ids_ref[...], gates_ref[...], experts)
     weight = jnp.where(main, gate, 0.0)
     high = weight.astype(low)
-    masks_ref[0] = high
-    masks_ref[1] = (weight - high.astype(full)).astype(low)
-    for number, mask in enumerate((main, even, odd)):
-        masks_ref[2 + number] = ones_at(mask).astype(low)
+    rest = (weight - high.astype(full)).astype(low)
+    parts = [high, rest] + [ones_at(mask).astype(low) for mask in (main, even, odd)]
+    for number, part in enumerate(parts):
+        masks_ref[:, number * 2 * HALF : (number + 1) * 2 * HALF] = part
 
 
 def masks_of(ids, gates, rows):
     return pl.pallas_call(
         mask_kernel,
         grid=(1,),
-        out_shape=jax.ShapeDtypeStruct((5, rows, ids.shape[1]), low),
+        out_shape=jax.ShapeDtypeStruct((rows, 5 * ids.shape[1]), low),
         compiler_params=small_params(24),
         cost_estimate=pl.CostEstimate(
-            flops=20 * rows * 128, bytes_accessed=20 * rows * 128, transcendentals=0
+            flops=20 * rows * 128, bytes_accessed=10 * rows * 128, transcendentals=0
         ),
     )(ids, gates)
 
 
 def combine_kernel(masks_ref, raw_ref, out_ref, in_ref):
-    out = contract(raw_ref[:, :384], masks_ref[0], 0, 0)
-    out = out + contract(raw_ref[:, :384], masks_ref[1], 0, 0)
-    out_ref[...] = out[:QUARTER].astype(low)
-    first = contract(raw_ref[:, 384:512], masks_ref[2], 0, 0)
-    second = contract(raw_ref[:, 0:256], masks_ref[3], 0, 0)
-    second = second + contract(raw_ref[:, 256:512], masks_ref[4], 0, 0)
-    in_ref[0:128, :] = first.astype(low)
-    in_ref[128:QUARTER, :] = second[: QUARTER - 128].astype(low)
+    tokens = out_ref.shape[1]
+    found = contract(raw_ref[...], masks_ref[...], 0, 0)
+    high, rest, main, even, odd = [
+        found[:, number * tokens : (number + 1) * tokens] for number in range(5)
+    ]
+    out_ref[...] = (high[:QUARTER] + rest[:QUARTER]).astype(low)
+    in_ref[0:128, :] = main[384:512].astype(low)
+    in_ref[128:QUARTER, :] = (even[: QUARTER - 128] + odd[256 : QUARTER + 128]).astype(low)
 
 
 def combine(masks, raw):
@@ -152,7 +152,7 @@
         combine_kernel,
         in_specs=in_vmem(2),
         out_specs=in_vmem(2),
-        out_shape=[jax.ShapeDtypeStruct((QUARTER, masks.shape[2]), low)] * 2,
+        out_shape=[jax.ShapeDtypeStruct((QUARTER, masks.shape[1] // 5), low)] * 2,
         compiler_params=small_params(),
         cost_estimate=pl.CostEstimate(
             flops=8 * rows * 128 * 512, bytes_accessed=2 * rows * 512, transcendentals=0

time: 185 us -> 185 us (level)
  no operation moved by 1% of the time
where the time goes in v9:
time: 185 us; the launch traced here: 184 us
  waiting for transfers between devices  73.2 us (40%)
  starting transfers between devices  71.4 us (39%)
  Pallas kernels  28.7 us (16%)
  other arithmetic  5.05 us (3%)
  local copies, waits for them, and re-layouts  4.56 us (2%)
    ppermute x12, waiting for transfers between devices, exchanged(): return lax.ppermute(block, axis, [(i, i ^ distance) for i in range(count)])  39.8 us
    ppermute x12, starting transfers between devices, exchanged(): return lax.ppermute(block, axis, [(i, i ^ distance) for i in range(count)])  36.2 us
    all_to_all x2, starting transfers between devices, by_parity(): lax.all_to_all(chunks, ('rep', 'exp'), split_axis=0, concat_axis=0, axis_...  35.2 us
    all_to_all x2, waiting for transfers between devices, by_parity(): lax.all_to_all(chunks, ('rep', 'exp'), split_axis=0, concat_axis=0, axis_...  33.4 us
    pallas_call x3, Pallas kernels, expert_call(): pl.pallas_call(kernel, in_specs=[scalar()] + in_vmem(len(operands)), out_...  14.7 us
    unnamed x14, local copies, waits for them, and re-layouts  4.54 us
    pallas_call x2, Pallas kernels, weight_grads(): pl.pallas_call(functools.partial(product_kernel, start), in_specs=in_vmem...  4.27 us
  transfers between devices with their start and end apart: 14, of which 11 were waited for; matrix products, arithmetic and copies ran while one was open for 3% of the time, Pallas kernels for 8%

profile of v9, /device:TPU:1, one launch (start us, length us, event | category | flops | bytes accessed | tf_op | source)
XLA Modules:
  0.0 183.7 jit_solution(8270061323869929847)
XLA Ops:
  0.6 0.0 copy-start.1
  0.6 0.0 copy-start
  0.7 0.0 copy-start.6
  0.7 3.1 %shard_map.110 = bf16[1024,512]{1,0:T(8,128)(2,1)} custom-call(s32[4,128]{1,0:T(4,128)} %bitcast.29, f32[4,128]{1,0:T(4,128)} %bitcast.31, bf16[360,128]{1,0:T(8,128)(2,1)} %bitcast.36, bf16[360,128]{1,0:T(8,128)(2,1)} %bitcast.37), custom_call_target="tpu_custom_call" | custom-call | flops 536870912 | bytes 1048576 | tf_op jit(solution)/shard_map/pallas_call | solution.py:103
  3.7 20.8 %all-to-all-start = ((bf16[128,8,512]{2,1,0:T(8,128)(2,1)}), bf16[128,8,512]{2,1,0:T(8,128)(2,1)S(1)}, u32[]{:S(2)}, u32[]{:S(2)}) async-start(bf16[128,8,512]{2,1,0:T(8,128)(2,1)} %bitcast.34), calls=%async_computation | async-start | bytes 2097152 | tf_op jit(solution)/shard_map/all_to_all | solution.py:363
  24.6 0.0 copy-done.6
  24.6 4.3 %collective-permute-start = (bf16[1,180,1440]{2,1,0:T(8,128)(2,1)S(1)}, bf16[1,180,1440]{2,1,0:T(8,128)(2,1)}, u32[]{:S(2)}, u32[]{:S(2)}) collective-permute-start(bf16[1,180,1440]{2,1,0:T(8,128)(2,1)S(1)} %copy-done.6), channel_id=1, source_target_pairs={{0,256},{128,384},{256,0},{384,128},{1,257},{129,385},{257,1},{385... | collective-permute-start | bytes 1555208 | tf_op jit(solution)/shard_map/ppermute | solution.py:25
  28.9 2.5 %collective-permute-start.2 = (bf16[1,180,1440]{2,1,0:T(8,128)(2,1)}, bf16[1,180,1440]{2,1,0:T(8,128)(2,1)}, u32[]{:S(2)}, u32[]{:S(2)}) collective-permute-start(bf16[1,180,1440]{2,1,0:T(8,128)(2,1)} %param.12), channel_id=1, source_target_pairs={{0,256},{128,384},{256,0},{384,128},{1,257},{129,385},{257,1},{385... | collective-permute-start | bytes 1555208 | tf_op jit(solution)/shard_map/ppermute | solution.py:25
  31.4 4.3 %collective-permute-start.3 = (bf16[1,180,1440]{2,1,0:T(8,128)(2,1)}, bf16[1,180,1440]{2,1,0:T(8,128)(2,1)}, u32[]{:S(2)}, u32[]{:S(2)}) collective-permute-start(bf16[1,180,1440]{2,1,0:T(8,128)(2,1)} %param.13), channel_id=1, source_target_pairs={{0,256},{128,384},{256,0},{384,128},{1,257},{129,385},{257,1},{385... | collective-permute-start | bytes 1555208 | tf_op jit(solution)/shard_map/ppermute | solution.py:25
  35.7 0.0 copy-done.1
  35.7 0.0 copy-done
  35.7 1.1 shard_map.111.masks_ref
  36.8 11.0 %collective-permute-done = bf16[1,180,1440]{2,1,0:T(8,128)(2,1)} collective-permute-done((bf16[1,180,1440]{2,1,0:T(8,128)(2,1)S(1)}, bf16[1,180,1440]{2,1,0:T(8,128)(2,1)}, u32[]{:S(2)}, u32[]{:S(2)}) %collective-permute-start) | collective-permute-done | bytes 518432 | tf_op jit(solution)/shard_map/ppermute | solution.py:25
  47.8 9.5 %all-to-all-done = bf16[128,8,512]{2,1,0:T(8,128)(2,1)S(1)} async-done(((bf16[128,8,512]{2,1,0:T(8,128)(2,1)}), bf16[128,8,512]{2,1,0:T(8,128)(2,1)S(1)}, u32[]{:S(2)}, u32[]{:S(2)}) %all-to-all-start) | async-done | bytes 1048608 | tf_op jit(solution)/shard_map/all_to_all | solution.py:363
  57.3 3.9 %collective-permute-start.4 = (bf16[1024,512]{1,0:T(8,128)(2,1)S(1)}, bf16[1024,512]{1,0:T(8,128)(2,1)S(1)}, u32[]{:S(2)}, u32[]{:S(2)}) collective-permute-start(bf16[1024,512]{1,0:T(8,128)(2,1)S(1)} %bitcast.26), channel_id=1, source_target_pairs={{0,128},{128,0},{256,384},{384,256},{1,129},{129,1},{257,385},{385... | collective-permute-start | bytes 3145736 | tf_op jit(solution)/shard_map/ppermute | solution.py:25
  61.2 1.9 %collective-permute-start.1 = (bf16[1024,512]{1,0:T(8,128)(2,1)S(1)}, bf16[1024,512]{1,0:T(8,128)(2,1)S(1)}, u32[]{:S(2)}, u32[]{:S(2)}) collective-permute-start(bf16[1024,512]{1,0:T(8,128)(2,1)S(1)} %bitcast.27), channel_id=1, source_target_pairs={{0,1},{1,0},{2,3},{3,2},{4,5},{5,4},{6,7},{7,6},{8,9},{9,8},{10,11... | collective-permute-start | bytes 3145736 | tf_op jit(solution)/shard_map/ppermute | solution.py:25
  63.2 1.5 collective-permute-done.2
  64.7 12.1 %collective-permute-done.3 = bf16[1,180,1440]{2,1,0:T(8,128)(2,1)} collective-permute-done((bf16[1,180,1440]{2,1,0:T(8,128)(2,1)}, bf16[1,180,1440]{2,1,0:T(8,128)(2,1)}, u32[]{:S(2)}, u32[]{:S(2)}) %collective-permute-start.3) | collective-permute-done | bytes 518432 | tf_op jit(solution)/shard_map/ppermute | solution.py:25
  76.9 2.5 %fusion.3 = (bf16[1,512,1440]{2,1,0:T(8,128)(2,1)S(1)}, bf16[1,512,1440]{2,1,0:T(8,128)(2,1)S(1)}, bf16[1,512,1440]{2,1,0:T(8,128)(2,1)S(1)}) fusion(bf16[76,1440]{1,0:T(8,128)(2,1)S(1)} %broadcast_in_dim.12, bf16[180,1440]{1,0:T(8,128)(2,1)} %bitcast.7, bf16[180,1440]{1,0:T(8,128)(2,1)} %bitcast.35, bf16[180,1440]{1,0:T(8,128)(2,1)} %bitcast.13, ...), kind=kLoop, calls=%fused_computation.13 | loop fusion | flops 14745600 | bytes 7752960 | tf_op jit(solution)/shard_map/stack | solution.py:388
  79.4 0.6 pad_maximum_fusion.w_ref
  80.0 0.0 collective-permute-done.4.other_ref
  80.0 1.8 %shard_map.112 = (bf16[320,1440]{1,0:T(8,128)(2,1)S(1)}, bf16[320,1440]{1,0:T(8,128)(2,1)S(1)}) custom-call(s32[1]{0:T(128)} %bitcast.15.core_ref, bf16[1024,512]{1,0:T(8,128)(2,1)S(1)} %bitcast.28, bf16[1024,512]{1,0:T(8,128)(2,1)S(1)} %collective-permute-done.4.other_ref), custom_call_target="tpu_custom_call" | custom-call | flops 235929600 | bytes 460800 | tf_op jit(solution)/shard_map/pallas_call | solution.py:278
  81.9 5.6 %shard_map.113 = (bf16[1024,512]{1,0:T(8,128)(2,1)S(1)}, bf16[1024,512]{1,0:T(8,128)(2,1)S(1)}, bf16[320,512]{1,0:T(8,128)(2,1)S(1)}, bf16[320,1024]{1,0:T(8,128)(2,1)S(1)}) custom-call(s32[1]{0:T(128)} %bitcast.15.core_ref, bf16[320,1440]{1,0:T(8,128)(2,1)S(1)} %get-tuple-element.51.tok_ref.refs_2_, ...), custom_call_target="tpu_custom_call" | custom-call | flops 2831155200 | bytes 5529600 | tf_op jit(solution)/shard_map/pallas_call | solution.py:278
  87.5 0.4 collective-permute-done.1.mine_ref
  87.9 2.9 %collective-permute-start.6 = (bf16[1024,512]{1,0:T(8,128)(2,1)S(1)}, bf16[1024,512]{1,0:T(8,128)(2,1)S(1)}, u32[]{:S(2)}, u32[]{:S(2)}) collective-permute-start(bf16[1024,512]{1,0:T(8,128)(2,1)S(1)} %get-tuple-element.56), channel_id=1, source_target_pairs={{0,128},{128,0},{256,384},{384,256},{1,129},{129,1},{257,385},{385... | collective-permute-start | bytes 3145736 | tf_op jit(solution)/shard_map/ppermute | solution.py:25
  90.9 1.9 %collective-permute-start.5 = (bf16[1024,512]{1,0:T(8,128)(2,1)S(1)}, bf16[1024,512]{1,0:T(8,128)(2,1)S(1)}, u32[]{:S(2)}, u32[]{:S(2)}) collective-permute-start(bf16[1024,512]{1,0:T(8,128)(2,1)S(1)} %collective-permute-done.1.mine_ref), channel_id=1, source_target_pairs={{0,128},{128,0},{256,384},{384,256},{1,129},{129,1},{257,385},{385... | collective-permute-start | bytes 3145736 | tf_op jit(solution)/shard_map/ppermute | solution.py:25
  92.8 0.3 collective-permute-done.6
  93.1 0.3 add_convert_fusion.2
  93.4 2.0 %collective-permute-done.5.other_ref = bf16[1024,512]{1,0:T(8,128)(2,1)S(1)} collective-permute-done((bf16[1024,512]{1,0:T(8,128)(2,1)S(1)}, bf16[1024,512]{1,0:T(8,128)(2,1)S(1)}, u32[]{:S(2)}, u32[]{:S(2)}) %collective-permute-start.5) | collective-permute-done | bytes 1048608 | tf_op jit(solution)/shard_map/ppermute | solution.py:25
  95.4 7.2 %shard_map.114 = (bf16[1024,512]{1,0:T(8,128)(2,1)S(1)}, bf16[1024,512]{1,0:T(8,128)(2,1)S(1)}, bf16[320,512]{1,0:T(8,128)(2,1)S(1)}, bf16[320,1024]{1,0:T(8,128...) custom-call(s32[1]{0:T(128)} %bitcast.15.core_ref, ...), custom_call_target="tpu_custom_call" | custom-call | flops 2831155200 | bytes 5529600 | tf_op jit(solution)/shard_map/pallas_call | solution.py:278
  102.7 2.0 %collective-permute-start.7 = (bf16[1024,512]{1,0:T(8,128)(2,1)S(1)}, bf16[1024,512]{1,0:T(8,128)(2,1)S(1)}, u32[]{:S(2)}, u32[]{:S(2)}) collective-permute-start(bf16[1024,512]{1,0:T(8,128)(2,1)S(1)} %get-tuple-element.61), channel_id=1, source_target_pairs={{0,128},{128,0},{256,384},{384,256},{1,129},{129,1},{257,385},{385... | collective-permute-start | bytes 3145736 | tf_op jit(solution)/shard_map/ppermute | solution.py:25
  104.7 2.2 %shard_map.115 = (bf16[180,1440]{1,0:T(8,128)(2,1)}, bf16[180,1440]{1,0:T(8,128)(2,1)}, bf16[180,1440]{1,0:T(8,128)(2,1)S(1)}) custom-call(bf16[320,512]{1,0:T(8,128)(2,1)S(1)} %get-tuple-element.62.refs_0_, bf16[320,1024]{1,0:T(8,128)(2,1)S(1)} %get-tuple-element.63.refs_1_, bf16[320,1440]{1,0:T(8,128)(2,1)S(1)} %get-tuple-element.51.tok_ref.refs_2_, ...), custom_call_target="tpu_custom_call" | custom-call | flops 995328000 | bytes 7372800 | tf_op jit(solution)/shard_map/pallas_call | solution.py:320
  106.9 0.3 collective-permute-done.7
  107.2 0.3 add_convert_fusion.1
  107.5 2.4 %collective-permute-start.8 = (bf16[1024,512]{1,0:T(8,128)(2,1)S(1)}, bf16[1024,512]{1,0:T(8,128)(2,1)S(1)}, u32[]{:S(2)}, u32[]{:S(2)}) collective-permute-start(bf16[1024,512]{1,0:T(8,128)(2,1)S(1)} %add_convert_fusion.1), channel_id=1, source_target_pairs={{0,1},{1,0},{2,3},{3,2},{4,5},{5,4},{6,7},{7,6},{8,9},{9,8},{10,11... | collective-permute-start | bytes 3145736 | tf_op jit(solution)/shard_map/ppermute | solution.py:25
  109.9 3.3 %collective-permute-start.9 = (bf16[180,1440]{1,0:T(8,128)(2,1)}, bf16[180,1440]{1,0:T(8,128)(2,1)}, u32[]{:S(2)}, u32[]{:S(2)}) collective-permute-start(bf16[180,1440]{1,0:T(8,128)(2,1)} %get-tuple-element.79), channel_id=1, source_target_pairs={{0,256},{128,384},{256,0},{384,128},{1,257},{129,385},{257,1},{385... | collective-permute-start | bytes 1555208 | tf_op jit(solution)/shard_map/ppermute | solution.py:25
  113.2 3.5 %collective-permute-start.10 = (bf16[180,1440]{1,0:T(8,128)(2,1)}, bf16[180,1440]{1,0:T(8,128)(2,1)}, u32[]{:S(2)}, u32[]{:S(2)}) collective-permute-start(bf16[180,1440]{1,0:T(8,128)(2,1)} %get-tuple-element.80), channel_id=1, source_target_pairs={{0,256},{128,384},{256,0},{384,128},{1,257},{129,385},{257,1},{385... | collective-permute-start | bytes 1555208 | tf_op jit(solution)/shard_map/ppermute | solution.py:25
  116.7 3.3 %collective-permute-start.11 = (bf16[180,1440]{1,0:T(8,128)(2,1)S(1)}, bf16[180,1440]{1,0:T(8,128)(2,1)}, u32[]{:S(2)}, u32[]{:S(2)}) collective-permute-start(bf16[180,1440]{1,0:T(8,128)(2,1)S(1)} %get-tuple-element.81), channel_id=1, source_target_pairs={{0,256},{128,384},{256,0},{384,128},{1,257},{129,385},{257,1},{385... | collective-permute-start | bytes 1555208 | tf_op jit(solution)/shard_map/ppermute | solution.py:25
  120.0 2.0 %shard_map.116 = (f32[180,1440]{1,0:T(8,128)S(1)}, f32[180,1440]{1,0:T(8,128)S(1)}, f32[180,1440]{1,0:T(8,128)S(1)}) custom-call(bf16[320,512]{1,0:T(8,128)(2,1)S(1)} %get-tuple-element.62.refs_0_, bf16[320,1024]{1,0:T(8,128)(2,1)S(1)} %get-tuple-element.63.refs_1_, bf16[320,1440]{1,0:T(8,128)(2,1)S(1)} %get-tuple-element.51.tok_ref.refs_2_, ...), custom_call_target="tpu_custom_call" | custom-call | flops 995328000 | bytes 7372800 | tf_op jit(solution)/shard_map/pallas_call | solution.py:320
  122.0 0.0 copy-start.2
  122.1 1.0 copy-done.2
  123.1 0.0 copy-start.4
  123.1 1.0 copy-done.4
  124.1 10.0 %collective-permute-done.8 = bf16[1024,512]{1,0:T(8,128)(2,1)S(1)} collective-permute-done((bf16[1024,512]{1,0:T(8,128)(2,1)S(1)}, bf16[1024,512]{1,0:T(8,128)(2,1)S(1)}, u32[]{:S(2)}, u32[]{:S(2)}) %collective-permute-start.8) | collective-permute-done | bytes 1048608 | tf_op jit(solution)/shard_map/ppermute | solution.py:25
  134.1 1.3 add_convert_fusion
  135.5 14.3 %all-to-all-start.1 = ((bf16[128,8,512]{2,1,0:T(8,128)(2,1)}), bf16[128,8,512]{2,1,0:T(8,128)(2,1)}, u32[]{:S(2)}, u32[]{:S(2)}) async-start(bf16[128,8,512]{2,1,0:T(8,128)(2,1)} %bitcast.33), calls=%async_computation.1 | async-start | bytes 2097152 | tf_op jit(solution)/shard_map/all_to_all | solution.py:363
  149.8 0.0 collective-permute-done.9.refs_3_
  149.8 0.0 collective-permute-done.10.refs_4_
  149.8 1.9 %collective-permute-done.11.refs_5_ = bf16[180,1440]{1,0:T(8,128)(2,1)} collective-permute-done((bf16[180,1440]{1,0:T(8,128)(2,1)S(1)}, bf16[180,1440]{1,0:T(8,128)(2,1)}, u32[]{:S(2)}, u32[]{:S(2)}) %collective-permute-start.11) | collective-permute-done | bytes 518432 | tf_op jit(solution)/shard_map/ppermute | solution.py:25
  151.8 0.0 copy-start.3
  151.8 1.3 copy-done.3
  153.0 0.0 copy-start.5
  153.0 1.3 copy-done.5
  154.3 2.7 %shard_map.117 = (bf16[180,1440]{1,0:T(8,128)(2,1)}, bf16[180,1440]{1,0:T(8,128)(2,1)}, bf16[180,1440]{1,0:T(8,128)(2,1)}) custom-call(f32[180,1440]{1,0:T(8,128)S(1)} %get-tuple-element.76.refs_0_, f32[180,1440]{1,0:T(8,128)S(1)} %copy-done.3, f32[180,1440]{1,0:T(8,128)S(1)} %copy-done.5, bf16[180,1440]{1,0:T(8,128)(2,1)} %collective-permute-done.9.refs_3_, ...), custom_call_target="tpu_custom_call" | custom-call | flops 259199991808 | bytes 259199991808 | tf_op jit(solution)/shard_map/pallas_call | solution.py:342
  156.9 23.9 %all-to-all-done.1 = bf16[128,8,512]{2,1,0:T(8,128)(2,1)} async-done(((bf16[128,8,512]{2,1,0:T(8,128)(2,1)}), bf16[128,8,512]{2,1,0:T(8,128)(2,1)}, u32[]{:S(2)}, u32[]{:S(2)}) %all-to-all-start.1) | async-done | bytes 1048608 | tf_op jit(solution)/shard_map/all_to_all | solution.py:363
  180.9 2.9 %shard_map.118 = (bf16[360,128]{1,0:T(8,128)(2,1)}, bf16[360,128]{1,0:T(8,128)(2,1)}) custom-call(bf16[1024,640]{1,0:T(8,128)(2,1)S(1)} %shard_map.111.masks_ref, bf16[1024,512]{1,0:T(8,128)(2,1)} %bitcast.17.raw_ref), custom_call_target="tpu_custom_call" | custom-call | flops 536870912 | bytes 1048576 | tf_op jit(solution)/shard_map/pallas_call | solution.py:151
  (1 shorter events, 0.0 us)
Async XLA Ops:
  0.6 35.1 %copy-start.1 = (f32[128,4]{0,1:T(4,128)S(1)}, f32[128,4]{0,1:T(4,128)}, u32[]{:S(2)}) copy-start(f32[128,4]{0,1:T(4,128)} %param.9) | copy-start | bytes 6148
  0.6 35.1 %copy-start = (s32[128,4]{0,1:T(4,128)S(1)}, s32[128,4]{0,1:T(4,128)}, u32[]{:S(2)}) copy-start(s32[128,4]{0,1:T(4,128)} %param.8) | copy-start | bytes 6148
  0.7 23.9 %copy-start.6 = (bf16[1,180,1440]{2,1,0:T(8,128)(2,1)S(1)}, bf16[1,180,1440]{2,1,0:T(8,128)(2,1)}, u32[]{:S(2)}) copy-start(bf16[1,180,1440]{2,1,0:T(8,128)(2,1)} %param.11) | copy-start | bytes 1555204
  3.7 53.6 %all-to-all-start = ((bf16[128,8,512]{2,1,0:T(8,128)(2,1)}), bf16[128,8,512]{2,1,0:T(8,128)(2,1)S(1)}, u32[]{:S(2)}, u32[]{:S(2)}) async-start(bf16[128,8,512]{2,1,0:T(8,128)(2,1)} %bitcast.34), calls=%async_computation | async-start | bytes 2097152 | tf_op jit(solution)/shard_map/all_to_all | solution.py:363
  24.6 23.3 %collective-permute-start = (bf16[1,180,1440]{2,1,0:T(8,128)(2,1)S(1)}, bf16[1,180,1440]{2,1,0:T(8,128)(2,1)}, u32[]{:S(2)}, u32[]{:S(2)}) collective-permute-start(bf16[1,180,1440]{2,1,0:T(8,128)(2,1)S(1)} %copy-done.6), channel_id=1, source_target_pairs={{0,256},{128,384},{256,0},{384,128},{1,257},{129,385},{257,1},{385... | collective-permute-start | bytes 1555208 | tf_op jit(solution)/shard_map/ppermute | solution.py:25
  28.9 35.8 %collective-permute-start.2 = (bf16[1,180,1440]{2,1,0:T(8,128)(2,1)}, bf16[1,180,1440]{2,1,0:T(8,128)(2,1)}, u32[]{:S(2)}, u32[]{:S(2)}) collective-permute-start(bf16[1,180,1440]{2,1,0:T(8,128)(2,1)} %param.12), channel_id=1, source_target_pairs={{0,256},{128,384},{256,0},{384,128},{1,257},{129,385},{257,1},{385... | collective-permute-start | bytes 1555208 | tf_op jit(solution)/shard_map/ppermute | solution.py:25
  31.4 45.4 %collective-permute-start.3 = (bf16[1,180,1440]{2,1,0:T(8,128)(2,1)}, bf16[1,180,1440]{2,1,0:T(8,128)(2,1)}, u32[]{:S(2)}, u32[]{:S(2)}) collective-permute-start(bf16[1,180,1440]{2,1,0:T(8,128)(2,1)} %param.13), channel_id=1, source_target_pairs={{0,256},{128,384},{256,0},{384,128},{1,257},{129,385},{257,1},{385... | collective-permute-start | bytes 1555208 | tf_op jit(solution)/shard_map/ppermute | solution.py:25
  57.3 22.7 %collective-permute-start.4 = (bf16[1024,512]{1,0:T(8,128)(2,1)S(1)}, bf16[1024,512]{1,0:T(8,128)(2,1)S(1)}, u32[]{:S(2)}, u32[]{:S(2)}) collective-permute-start(bf16[1024,512]{1,0:T(8,128)(2,1)S(1)} %bitcast.26), channel_id=1, source_target_pairs={{0,128},{128,0},{256,384},{384,256},{1,129},{129,1},{257,385},{385... | collective-permute-start | bytes 3145736 | tf_op jit(solution)/shard_map/ppermute | solution.py:25
  61.2 26.7 %collective-permute-start.1 = (bf16[1024,512]{1,0:T(8,128)(2,1)S(1)}, bf16[1024,512]{1,0:T(8,128)(2,1)S(1)}, u32[]{:S(2)}, u32[]{:S(2)}) collective-permute-start(bf16[1024,512]{1,0:T(8,128)(2,1)S(1)} %bitcast.27), channel_id=1, source_target_pairs={{0,1},{1,0},{2,3},{3,2},{4,5},{5,4},{6,7},{7,6},{8,9},{9,8},{10,11... | collective-permute-start | bytes 3145736 | tf_op jit(solution)/shard_map/ppermute | solution.py:25
  87.9 5.2 %collective-permute-start.6 = (bf16[1024,512]{1,0:T(8,128)(2,1)S(1)}, bf16[1024,512]{1,0:T(8,128)(2,1)S(1)}, u32[]{:S(2)}, u32[]{:S(2)}) collective-permute-start(bf16[1024,512]{1,0:T(8,128)(2,1)S(1)} %get-tuple-element.56), channel_id=1, source_target_pairs={{0,128},{128,0},{256,384},{384,256},{1,129},{129,1},{257,385},{385... | collective-permute-start | bytes 3145736 | tf_op jit(solution)/shard_map/ppermute | solution.py:25
  90.9 4.6 %collective-permute-start.5 = (bf16[1024,512]{1,0:T(8,128)(2,1)S(1)}, bf16[1024,512]{1,0:T(8,128)(2,1)S(1)}, u32[]{:S(2)}, u32[]{:S(2)}) collective-permute-start(bf16[1024,512]{1,0:T(8,128)(2,1)S(1)} %collective-permute-done.1.mine_ref), channel_id=1, source_target_pairs={{0,128},{128,0},{256,384},{384,256},{1,129},{129,1},{257,385},{385... | collective-permute-start | bytes 3145736 | tf_op jit(solution)/shard_map/ppermute | solution.py:25
  102.7 4.6 %collective-permute-start.7 = (bf16[1024,512]{1,0:T(8,128)(2,1)S(1)}, bf16[1024,512]{1,0:T(8,128)(2,1)S(1)}, u32[]{:S(2)}, u32[]{:S(2)}) collective-permute-start(bf16[1024,512]{1,0:T(8,128)(2,1)S(1)} %get-tuple-element.61), channel_id=1, source_target_pairs={{0,128},{128,0},{256,384},{384,256},{1,129},{129,1},{257,385},{385... | collective-permute-start | bytes 3145736 | tf_op jit(solution)/shard_map/ppermute | solution.py:25
  107.5 26.6 %collective-permute-start.8 = (bf16[1024,512]{1,0:T(8,128)(2,1)S(1)}, bf16[1024,512]{1,0:T(8,128)(2,1)S(1)}, u32[]{:S(2)}, u32[]{:S(2)}) collective-permute-start(bf16[1024,512]{1,0:T(8,128)(2,1)S(1)} %add_convert_fusion.1), channel_id=1, source_target_pairs={{0,1},{1,0},{2,3},{3,2},{4,5},{5,4},{6,7},{7,6},{8,9},{9,8},{10,11... | collective-permute-start | bytes 3145736 | tf_op jit(solution)/shard_map/ppermute | solution.py:25
  109.9 39.9 %collective-permute-start.9 = (bf16[180,1440]{1,0:T(8,128)(2,1)}, bf16[180,1440]{1,0:T(8,128)(2,1)}, u32[]{:S(2)}, u32[]{:S(2)}) collective-permute-start(bf16[180,1440]{1,0:T(8,128)(2,1)} %get-tuple-element.79), channel_id=1, source_target_pairs={{0,256},{128,384},{256,0},{384,128},{1,257},{129,385},{257,1},{385... | collective-permute-start | bytes 1555208 | tf_op jit(solution)/shard_map/ppermute | solution.py:25
  113.2 36.6 %collective-permute-start.10 = (bf16[180,1440]{1,0:T(8,128)(2,1)}, bf16[180,1440]{1,0:T(8,128)(2,1)}, u32[]{:S(2)}, u32[]{:S(2)}) collective-permute-start(bf16[180,1440]{1,0:T(8,128)(2,1)} %get-tuple-element.80), channel_id=1, source_target_pairs={{0,256},{128,384},{256,0},{384,128},{1,257},{129,385},{257,1},{385... | collective-permute-start | bytes 1555208 | tf_op jit(solution)/shard_map/ppermute | solution.py:25
  116.7 35.1 %collective-permute-start.11 = (bf16[180,1440]{1,0:T(8,128)(2,1)S(1)}, bf16[180,1440]{1,0:T(8,128)(2,1)}, u32[]{:S(2)}, u32[]{:S(2)}) collective-permute-start(bf16[180,1440]{1,0:T(8,128)(2,1)S(1)} %get-tuple-element.81), channel_id=1, source_target_pairs={{0,256},{128,384},{256,0},{384,128},{1,257},{129,385},{257,1},{385... | collective-permute-start | bytes 1555208 | tf_op jit(solution)/shard_map/ppermute | solution.py:25
  122.0 1.0 copy-start.2
  123.1 1.0 copy-start.4
  135.5 45.4 %all-to-all-start.1 = ((bf16[128,8,512]{2,1,0:T(8,128)(2,1)}), bf16[128,8,512]{2,1,0:T(8,128)(2,1)}, u32[]{:S(2)}, u32[]{:S(2)}) async-start(bf16[128,8,512]{2,1,0:T(8,128)(2,1)} %bitcast.33), calls=%async_computation.1 | async-start | bytes 2097152 | tf_op jit(solution)/shard_map/all_to_all | solution.py:363
  151.8 1.3 copy-start.3
  153.0 1.3 copy-start.5
